TPU v7x, 32 devices: a whole 2x2x4 slice. The times are simulated.
32 devices in a mesh: expert: 4 (over z), row: 4 (over y, x), col: 2 (over core).
Axes of the slice: x: 2, y: 2, z: 4, core: 2. Of those that a mesh axis runs over, the one named last changes fastest.
Arguments:
- layer_input: bfloat16 [4096, 2048], P(('expert', 'row', 'col')), may hold values from -6 to 6
- norm_attn: float32 [2048], replicated, may hold values from 0.25 to 1.75
- w_query: bfloat16 [2048, 4096], P(None, ('row', 'col')), may hold values from -0.125 to 0.125
- w_key: bfloat16 [2048, 512], P(None, 'row'), may hold values from -0.125 to 0.125
- w_value: bfloat16 [2048, 512], P(None, 'row'), may hold values from -0.125 to 0.125
- q_gain: float32 [128], replicated, may hold values from 0.25 to 1.75
- k_gain: float32 [128], replicated, may hold values from 0.25 to 1.75
- w_out: bfloat16 [4096, 2048], P(('row', 'col')), may hold values from -0.375 to 0.375
- norm_moe: float32 [2048], replicated, may hold values from 0.25 to 1.75
- w_router: bfloat16 [2048, 32], replicated, may hold values from -0.0625 to 0.0625
- w_gate: bfloat16 [32, 2048, 768], P(('expert', 'row', 'col')), may hold values from -0.125 to 0.125
- w_up: bfloat16 [32, 2048, 768], P(('expert', 'row', 'col')), may hold values from -0.125 to 0.125
- w_down: bfloat16 [32, 768, 2048], P(('expert', 'row', 'col')), may hold values from -0.875 to 0.875
- seq_lengths: int32 [4, 4], P('expert'), may hold values from 64 to 512, as said below
- routes: int32 [4096, 8], P(('expert', 'row', 'col')), may hold values from 0 to 31, all different within a row; in each aligned block of 128 rows (0 to 127, 128 to 255, ...) at most 34 rows name the same one
- out_grad: bfloat16 [4096, 2048], P(('expert', 'row', 'col')), may hold values from -6 to 6
Outputs:
- out: bfloat16 [4096, 2048], P(('expert', 'row', 'col'))
- grad_x: bfloat16 [4096, 2048], P(('expert', 'row', 'col'))
- grad_norm_attn: float32 [2048], replicated
- grad_query: float32 [2048, 4096], P(None, ('row', 'col'))
- grad_key: float32 [2048, 512], P(None, 'row')
- grad_value: float32 [2048, 512], P(None, 'row')
- grad_q_gain: float32 [128], replicated
- grad_k_gain: float32 [128], replicated
- grad_out_proj: float32 [4096, 2048], P(('row', 'col'))
- grad_norm_moe: float32 [2048], replicated
- grad_router: float32 [2048, 32], replicated
- grad_gate: float32 [32, 2048, 768], P(('expert', 'row', 'col'))
- grad_up: float32 [32, 2048, 768], P(('expert', 'row', 'col'))
- grad_down: float32 [32, 768, 2048], P(('expert', 'row', 'col'))
Inputs may be any that keep to these rules, and one draw needn't show every extreme that they name: `seq_lengths`: in every group one sequence has exactly 512 slots and the others 1024 // 16 to 170; the slots after them are padding. `routes`: the 8 experts of a slot differ; among the slots of one device no expert is named more than 34 times.
All inputs are finite; a program needn't handle non-finite values.
Results may differ from a plain program's by a relative error of at most 0.024.
Values may be sent and summed in bfloat16 or wider, within the bound.
No kernel may reach another device: no remote copies, remote signals or barrier semaphores. Data moves between devices by JAX's collectives and lax.ppermute only.
A program may use at most 192 MiB of HBM per device.

v0:
```python
import jax
import jax.numpy as jnp
from jax import lax
from jax.sharding import PartitionSpec as P

eps_norm = 1e-06
rope_base = 1000000.0
highest = lax.Precision.HIGHEST


def rms_scale(values, norm_gain):
    return (
        values * lax.rsqrt(jnp.mean(values * values, axis=-1, keepdims=True) + eps_norm) * norm_gain
    )


def head_prep(values, norm_gain, cosine_table, sine_table):
    normed = rms_scale(values, norm_gain)
    half_dim = values.shape[-1] // 2
    turned = jnp.concatenate([-normed[..., half_dim:], normed[..., :half_dim]], axis=-1)
    return normed * cosine_table[:, None, :] + turned * sine_table[:, None, :]


def rope_tables(positions, head_dim):
    half_dim = head_dim // 2
    inverse = rope_base ** (-(jnp.arange(half_dim, dtype=jnp.float32) * 2.0 / head_dim))
    angles = positions.astype(jnp.float32)[:, None] * inverse[None, :]
    angles = jnp.concatenate([angles, angles], axis=1)
    return (jnp.cos(angles), jnp.sin(angles))


def group_layout(lengths, slot_count):
    seq_count = lengths.shape[0]
    seq_ends = jnp.cumsum(lengths, dtype=jnp.int32)
    starts = seq_ends - lengths
    slot_ids = jnp.arange(slot_count, dtype=jnp.int32)
    segment = jnp.sum(
        (slot_ids[:, None] >= seq_ends[None, :]).astype(jnp.int32), axis=1, dtype=jnp.int32
    )
    inside = segment < seq_count
    seq_ids = jnp.arange(seq_count, dtype=jnp.int32)
    own_start = jnp.sum(
        jnp.where(seq_ids[None, :] == segment[:, None], starts[None, :], 0), axis=1, dtype=jnp.int32
    )
    positions = jnp.where(inside, slot_ids - own_start, 0)
    segment = jnp.where(inside, segment, seq_count + slot_ids)
    return (segment, positions)


def times_transposed(left, right):
    return lax.dot_general(
        left, right, (((1,), (1,)), ((), ())), preferred_element_type=jnp.float32
    )


def transposed_times(left, right):
    return lax.dot_general(
        left, right, (((0,), (0,)), ((), ())), preferred_element_type=jnp.float32
    )


def move_slots(slot_block):
    return lax.all_to_all(
        slot_block, ("expert", "row", "col"), split_axis=0, concat_axis=0, tiled=True
    )


def local(
    layer_input,
    norm_attn,
    w_query,
    w_key,
    w_value,
    q_gain,
    k_gain,
    w_out,
    norm_moe,
    w_router,
    w_gate,
    w_up,
    w_down,
    seq_lengths,
    routes,
    out_grad,
):
    tok_dev = layer_input.shape[0]
    model_width = layer_input.shape[1]
    group_tok = tok_dev * lax.axis_size(("row", "col"))
    head_dim = q_gain.shape[0]
    local_heads = w_query.shape[1] // head_dim
    softmax_scale = head_dim ** (-0.5)
    experts = w_router.shape[1]
    top_count = routes.shape[1]
    capacity = tok_dev * top_count * 17 // (16 * experts)
    input_rows = layer_input.astype(jnp.float32)
    normed_one, norm_one_back = jax.vjp(rms_scale, input_rows, norm_attn)
    normed_low = normed_one.astype(jnp.bfloat16)
    group_rows = lax.all_gather(normed_low, ("row", "col"), axis=0, tiled=True)
    segment, positions = group_layout(seq_lengths[0], group_tok)
    cosine_table, sine_table = rope_tables(positions, head_dim)
    query_pre = jnp.dot(group_rows, w_query, preferred_element_type=jnp.float32).reshape(
        group_tok, local_heads, head_dim
    )
    key_pre = jnp.dot(group_rows, w_key, preferred_element_type=jnp.float32)
    value_low = jnp.dot(group_rows, w_value, preferred_element_type=jnp.float32).astype(
        jnp.bfloat16
    )

    def query_prep(values, norm_gain):
        return head_prep(values, norm_gain, cosine_table, sine_table)

    def key_prep(values, norm_gain):
        return head_prep(values[:, None, :], norm_gain, cosine_table, sine_table)[:, 0, :]

    query_full, query_back = jax.vjp(query_prep, query_pre, q_gain)
    key_full, key_back = jax.vjp(key_prep, key_pre, k_gain)
    query_low = query_full.astype(jnp.bfloat16)
    key_low = key_full.astype(jnp.bfloat16)
    block_rows = min(512, group_tok)
    block_count = group_tok // block_rows
    query_blocks = query_low.reshape(block_count, block_rows, local_heads, head_dim)
    segment_blocks = segment.reshape(block_count, block_rows)
    position_blocks = positions.reshape(block_count, block_rows)

    def scores(query_block, segment_block, position_block):
        logits_block = (
            jnp.einsum("qhd,kd->hqk", query_block, key_low, preferred_element_type=jnp.float32)
            * softmax_scale
        )
        allowed = (segment_block[:, None] == segment[None, :]) & (
            positions[None, :] <= position_block[:, None]
        )
        return (logits_block, allowed[None, :, :])

    def attend(inputs):
        query_block, segment_block, position_block = inputs
        logits_block, allowed = scores(query_block, segment_block, position_block)
        weights = jnp.where(allowed, jnp.exp(logits_block), 0.0)
        totals = jnp.sum(weights, axis=-1)
        probabilities = (weights / totals[..., None]).astype(jnp.bfloat16)
        heads_out = jnp.einsum(
            "hqk,kd->qhd", probabilities, value_low, preferred_element_type=jnp.float32
        )
        return (heads_out.astype(jnp.bfloat16), jnp.log(totals))

    head_blocks, log_totals = lax.map(attend, (query_blocks, segment_blocks, position_blocks))
    heads_low = head_blocks.reshape(group_tok, local_heads * head_dim)
    attn_rows = lax.psum_scatter(
        jnp.dot(heads_low, w_out, preferred_element_type=jnp.float32).astype(jnp.bfloat16),
        ("row", "col"),
        scatter_dimension=0,
        tiled=True,
    ).astype(jnp.float32)
    mixed_rows = input_rows + attn_rows
    normed_two, norm_two_back = jax.vjp(rms_scale, mixed_rows, norm_moe)
    moe_input = normed_two.astype(jnp.bfloat16)
    router_logits = jnp.dot(moe_input, w_router, preferred_element_type=jnp.float32)

    def route_gates(all_logits):
        chosen = jnp.take_along_axis(all_logits, routes, axis=1)
        chosen = chosen - jnp.max(chosen, axis=1, keepdims=True)
        raised = jnp.exp(chosen)
        return raised / jnp.sum(raised, axis=1, keepdims=True)

    gate_values, gates_back = jax.vjp(route_gates, router_logits)
    picked = routes.reshape(-1)
    assign_count = picked.shape[0]
    onehot = (picked[:, None] == jnp.arange(experts, dtype=jnp.int32)[None, :]).astype(jnp.int32)
    slot_rank = (
        jnp.sum(jnp.cumsum(onehot, axis=0, dtype=jnp.int32) * onehot, axis=1, dtype=jnp.int32) - 1
    )
    slot_index = picked * capacity + slot_rank
    slot_owner = (
        jnp.full((experts * capacity,), assign_count, jnp.int32)
        .at[slot_index]
        .set(jnp.arange(assign_count, dtype=jnp.int32))
    )
    owner_row = slot_owner // top_count
    padded_input = jnp.concatenate([moe_input, jnp.zeros((1, model_width), jnp.bfloat16)], axis=0)
    send_rows = padded_input[owner_row].reshape(experts, capacity, model_width)
    slot_rows = move_slots(send_rows).reshape(experts * capacity, model_width)
    gate_matrix = w_gate[0]
    up_matrix = w_up[0]
    down_matrix = w_down[0]
    gate_pre = jnp.dot(slot_rows, gate_matrix, preferred_element_type=jnp.float32)
    up_pre = jnp.dot(slot_rows, up_matrix, preferred_element_type=jnp.float32)
    hidden_low = (jax.nn.silu(gate_pre) * up_pre).astype(jnp.bfloat16)
    expert_out = jnp.dot(hidden_low, down_matrix, preferred_element_type=jnp.float32).astype(
        jnp.bfloat16
    )
    returned = move_slots(expert_out.reshape(experts, capacity, model_width)).reshape(
        experts * capacity, model_width
    )
    assigned = returned[slot_index].reshape(tok_dev, top_count, model_width)
    moe_rows = jnp.sum(gate_values[:, :, None] * assigned, axis=1)
    out_rows = (mixed_rows + moe_rows).astype(jnp.bfloat16)
    grad_rows = out_grad.astype(jnp.float32)
    grad_gates = jnp.sum(assigned * grad_rows[:, None, :], axis=2)
    grad_assigned = (
        (gate_values[:, :, None] * grad_rows[:, None, :])
        .astype(jnp.bfloat16)
        .reshape(assign_count, model_width)
    )
    padded_grad = jnp.concatenate(
        [grad_assigned, jnp.zeros((1, model_width), jnp.bfloat16)], axis=0
    )
    grad_send = padded_grad[slot_owner].reshape(experts, capacity, model_width)
    grad_out_slots = move_slots(grad_send).reshape(experts * capacity, model_width)
    grad_hidden = times_transposed(grad_out_slots, down_matrix)
    grad_down = transposed_times(hidden_low, grad_out_slots)
    sigmoid_gate = jax.nn.sigmoid(gate_pre)
    grad_gate_pre = (
        grad_hidden * up_pre * sigmoid_gate * (1.0 + gate_pre * (1.0 - sigmoid_gate))
    ).astype(jnp.bfloat16)
    grad_up_pre = (grad_hidden * jax.nn.silu(gate_pre)).astype(jnp.bfloat16)
    grad_gate = transposed_times(slot_rows, grad_gate_pre)
    grad_up = transposed_times(slot_rows, grad_up_pre)
    grad_slot_rows = (
        times_transposed(grad_gate_pre, gate_matrix) + times_transposed(grad_up_pre, up_matrix)
    ).astype(jnp.bfloat16)
    grad_back = move_slots(grad_slot_rows.reshape(experts, capacity, model_width)).reshape(
        experts * capacity, model_width
    )
    grad_moe_input = jnp.sum(
        grad_back[slot_index].reshape(tok_dev, top_count, model_width), axis=1, dtype=jnp.float32
    )
    grad_logits = gates_back(grad_gates)[0]
    grad_router = jnp.einsum(
        "td,te->de", moe_input, grad_logits, precision=highest, preferred_element_type=jnp.float32
    )
    grad_moe_input = grad_moe_input + jnp.einsum(
        "te,de->td", grad_logits, w_router, precision=highest, preferred_element_type=jnp.float32
    )
    grad_mixed_norm, grad_norm_moe = norm_two_back(grad_moe_input)
    grad_mixed = grad_rows + grad_mixed_norm
    grad_attn_low = grad_mixed.astype(jnp.bfloat16)
    grad_group = lax.all_gather(grad_attn_low, ("row", "col"), axis=0, tiled=True)
    grad_out_proj = transposed_times(heads_low, grad_group)
    grad_heads = (
        times_transposed(grad_group, w_out)
        .astype(jnp.bfloat16)
        .reshape(block_count, block_rows, local_heads, head_dim)
    )

    def attend_back(totals, inputs):
        grad_key_acc, grad_value_acc = totals
        query_block, segment_block, position_block, log_block, grad_block = inputs
        logits_block, allowed = scores(query_block, segment_block, position_block)
        probabilities = jnp.where(allowed, jnp.exp(logits_block - log_block[..., None]), 0.0)
        probs_low = probabilities.astype(jnp.bfloat16)
        grad_probs = jnp.einsum(
            "qhd,kd->hqk", grad_block, value_low, preferred_element_type=jnp.float32
        )
        centre = jnp.sum(probabilities * grad_probs, axis=-1, keepdims=True)
        grad_scores = (probabilities * (grad_probs - centre)).astype(jnp.bfloat16)
        grad_query_block = (
            jnp.einsum("hqk,kd->qhd", grad_scores, key_low, preferred_element_type=jnp.float32)
            * softmax_scale
        )
        grad_key_acc = (
            grad_key_acc
            + jnp.einsum(
                "hqk,qhd->kd", grad_scores, query_block, preferred_element_type=jnp.float32
            )
            * softmax_scale
        )
        grad_value_acc = grad_value_acc + jnp.einsum(
            "hqk,qhd->kd", probs_low, grad_block, preferred_element_type=jnp.float32
        )
        return ((grad_key_acc, grad_value_acc), grad_query_block)

    zero_rows = jnp.zeros((group_tok, head_dim), jnp.float32)
    (grad_key_post, grad_value_pre), grad_query_blocks = lax.scan(
        attend_back,
        (zero_rows, zero_rows),
        (query_blocks, segment_blocks, position_blocks, log_totals, grad_heads),
    )
    grad_query_post = grad_query_blocks.reshape(group_tok, local_heads, head_dim)
    grad_query_pre, grad_q_gain = query_back(grad_query_post)
    grad_key_pre, grad_k_gain = key_back(grad_key_post)
    grad_query_low = grad_query_pre.reshape(group_tok, local_heads * head_dim).astype(jnp.bfloat16)
    grad_query = transposed_times(group_rows, grad_query_low)
    grad_kv = jnp.concatenate([grad_key_pre, grad_value_pre], axis=1)
    grad_key_value = jnp.einsum(
        "td,te->de", group_rows, grad_kv, precision=highest, preferred_element_type=jnp.float32
    )
    key_value_w = jnp.concatenate([w_key, w_value], axis=1)
    grad_normed = lax.psum_scatter(
        (
            times_transposed(grad_query_low, w_query)
            + jnp.einsum(
                "te,de->td",
                grad_kv,
                key_value_w,
                precision=highest,
                preferred_element_type=jnp.float32,
            )
        ).astype(jnp.bfloat16),
        ("row", "col"),
        scatter_dimension=0,
        tiled=True,
    ).astype(jnp.float32)
    grad_input_norm, grad_norm_attn = norm_one_back(grad_normed)
    grad_x = (grad_mixed + grad_input_norm).astype(jnp.bfloat16)
    grad_query, grad_out_proj = (
        lax.psum(grad_query.astype(jnp.bfloat16), "expert").astype(jnp.float32),
        lax.psum(grad_out_proj.astype(jnp.bfloat16), "expert").astype(jnp.float32),
    )
    grad_key, grad_value = (
        lax.psum(grad_key_value[:, :head_dim].astype(jnp.bfloat16), ("expert", "col")).astype(
            jnp.float32
        ),
        lax.psum(grad_key_value[:, head_dim:].astype(jnp.bfloat16), ("expert", "col")).astype(
            jnp.float32
        ),
    )
    grad_norm_attn, grad_q_gain, grad_k_gain, grad_norm_moe, grad_router = lax.psum(
        (grad_norm_attn, grad_q_gain, grad_k_gain, grad_norm_moe, grad_router),
        ("expert", "row", "col"),
    )
    return (
        out_rows,
        grad_x,
        grad_norm_attn,
        grad_query,
        grad_key,
        grad_value,
        grad_q_gain,
        grad_k_gain,
        grad_out_proj,
        grad_norm_moe,
        grad_router,
        grad_gate[None],
        grad_up[None],
        grad_down[None],
    )


def solution(mesh):
    placed = (
        P(("expert", "row", "col"), None),
        P(),
        P(None, ("row", "col")),
        P(None, "row"),
        P(None, "row"),
        P(),
        P(),
        P(("row", "col"), None),
        P(),
        P(),
        P(("expert", "row", "col"), None, None),
        P(("expert", "row", "col"), None, None),
        P(("expert", "row", "col"), None, None),
        P("expert", None),
        P(("expert", "row", "col"), None),
        P(("expert", "row", "col"), None),
    )
    return jax.shard_map(
        local,
        mesh=mesh,
        in_specs=placed,
        out_specs=(
            P(("expert", "row", "col"), None),
            P(("expert", "row", "col"), None),
            P(),
            P(None, ("row", "col")),
            P(None, "row"),
            P(None, "row"),
            P(),
            P(),
            P(("row", "col"), None),
            P(),
            P(),
            P(("expert", "row", "col"), None, None),
            P(("expert", "row", "col"), None, None),
            P(("expert", "row", "col"), None, None),
        ),
        check_vma=False,
    )
```

profile of v0, /device:TPU:1, one launch (start us, length us, event | category | flops | bytes accessed | tf_op | source)
XLA Modules:
  0.0 1269.3 jit_solution(868017892263990001)
XLA Ops:
  13.7 9.1 fusion.92
  22.8 28.3 %all-gather.3.cloned.1.call-done = bf16[1024,2048]{1,0:T(8,128)(2,1)} async-done(((bf16[128,2048]{1,0:T(8,128)(2,1)}), bf16[1024,2048]{1,0:T(8,128)(2,1)}) %all-gather.3.cloned.1.call-update) | async-done | bytes 4194320 | tf_op jit(solution)/shard_map/all_gather | solution.py:98
  93.0 16.1 %while.27 = (s32[]{:T(128)}, bf16[2,512,4,128]{3,2,1,0:T(4,128)(2,1)}, f32[2,4,512]{2,1,0:T(4,128)S(1)}, s32[2,512]{1,0:T(2,128)S(1)}, s32[1024]{0:T(1024)S(1)},...) while((s32[]{:T(128)}, ...), condition=%wide.region_8.9_spmd, body=%wide.region_6.8_spmd.sunk | while | flops 1090254848 | bytes 30462668 | solution.py:146
  116.6 9.0 reduce-window.11
  130.7 36.0 %reduce-scatter.3.cloned.1.call-done = bf16[128,2048]{1,0:T(8,128)(2,1)} async-done(((bf16[1024,2048]{1,0:T(8,128)(2,1)}), bf16[128,2048]{1,0:T(8,128)(2,1)}) %reduce-scatter.3.cloned.1.call-update) | async-done | bytes 524304 | tf_op jit(solution)/shard_map/reduce_scatter | solution.py:148
  171.3 11.7 gather_fusion
  210.8 13.3 %gather_fusion.2 = bf16[1088,2048]{1,0:T(8,128)(2,1)} fusion(bf16[1025,2048]{1,0:T(8,128)(2,1)} %concatenate.52, s32[2048]{0:T(1024)S(1)} %pad_clamp_fusion), kind=kCustom, calls=%fused_computation.2 | custom fusion | bytes 8917248 | tf_op jit(solution)/shard_map/gather | solution.py:207
  231.3 80.2 %all-to-all-done = bf16[32,34,2048]{2,1,0:T(8,128)(2,1)} async-done(((bf16[32,34,2048]{2,1,0:T(8,128)(2,1)}), bf16[32,34,2048]{2,1,0:T(8,128)(2,1)}, u32[]{:S(2)}, u32[]{:S(2)}) %all-to-all-start) | async-done | bytes 4456480 | tf_op jit(solution)/shard_map/all_to_all | solution.py:63
  311.5 12.8 %all-to-all-start.2 = ((bf16[32,34,2048]{2,1,0:T(8,128)(2,1)}), bf16[32,34,2048]{2,1,0:T(8,128)(2,1)}, u32[]{:S(2)}, u32[]{:S(2)}) async-start(bf16[32,34,2048]{2,1,0:T(8,128)(2,1)} %reshape.559), calls=%async_computation.3 | async-start | bytes 10485760 | tf_op jit(solution)/shard_map/all_to_all | solution.py:63
  331.7 8.7 fusion.58
  345.8 94.6 %all-to-all-done.2 = bf16[32,34,2048]{2,1,0:T(8,128)(2,1)} async-done(((bf16[32,34,2048]{2,1,0:T(8,128)(2,1)}), bf16[32,34,2048]{2,1,0:T(8,128)(2,1)}, u32[]{:S(2)}, u32[]{:S(2)}) %all-to-all-start.2) | async-done | bytes 4456480 | tf_op jit(solution)/shard_map/all_to_all | solution.py:63
  447.8 10.6 multiply_convert_fusion
  494.8 98.3 %all-to-all-done.1 = bf16[32,34,2048]{2,1,0:T(8,128)(2,1)} async-done(((bf16[32,34,2048]{2,1,0:T(8,128)(2,1)}), bf16[32,34,2048]{2,1,0:T(8,128)(2,1)}, u32[]{:S(2)}, u32[]{:S(2)}) %all-to-all-start.1) | async-done | bytes 4456480 | tf_op jit(solution)/shard_map/all_to_all | solution.py:63
  605.0 11.7 gather_fusion.1
  623.0 90.5 %all-to-all-done.3 = bf16[32,34,2048]{2,1,0:T(8,128)(2,1)} async-done(((bf16[32,34,2048]{2,1,0:T(8,128)(2,1)}), bf16[32,34,2048]{2,1,0:T(8,128)(2,1)}, u32[]{:S(2)}, u32[]{:S(2)}) %all-to-all-start.3) | async-done | bytes 4456480 | tf_op jit(solution)/shard_map/all_to_all | solution.py:63
  720.8 11.6 gather_fusion.3
  749.0 36.1 %all-gather.5.cloned.1.call-done = bf16[1024,2048]{1,0:T(8,128)(2,1)} async-done(((bf16[128,2048]{1,0:T(8,128)(2,1)}), bf16[1024,2048]{1,0:T(8,128)(2,1)}) %all-gather.5.cloned.1.call-update) | async-done | bytes 4194320 | tf_op jit(solution)/shard_map/all_gather | solution.py:237
  791.5 44.8 %while.28 = (s32[]{:T(128)}, f32[1024,128]{1,0:T(8,128)S(1)}, f32[1024,128]{1,0:T(8,128)}, f32[2,512,4,128]{3,1,0,2:T(8,128)}, s32[2,512]{1,0:T(2,128)S(1)}, /*i...) while((s32[]{:T(128)}, f32[1024,128]{1,0:T(8,128)S(1)}, ...), condition=%wide.region_27.28_spmd.clone, body=%wide.region_25.27_spmd.clone.sunk | while | flops 2718300160 | bytes 126694152 | solution.py:273
  885.5 8.6 convolution_bitcast_fusion.1
  894.1 8.6 convolution_bitcast_fusion.2
  920.2 155.6 %all-reduce.17.cloned.1.call-done = (bf16[2048,512]{1,0:T(8,128)(2,1)}, bf16[512,2048]{1,0:T(8,128)(2,1)}) async-done(((bf16[2048,512]{1,0:T(8,128)(2,1)}, bf16[512,2048]{1,0:T(8,128)(2,1)}), (bf16[2048,512]{1,0:T(8,128)(2,1)}, bf16[512,2048]{1,0:T(8,128)(2,1)})) %all-reduce.17.cloned.1.call-update) | async-done | bytes 4194320 | tf_op jit(solution)/shard_map/psum | solution.py:306
  1082.7 46.6 %reduce-scatter.5.cloned.1.call-done = bf16[128,2048]{1,0:T(8,128)(2,1)} async-done(((bf16[1024,2048]{1,0:T(8,128)(2,1)}), bf16[128,2048]{1,0:T(8,128)(2,1)}) %reduce-scatter.5.cloned.1.call-update) | async-done | bytes 524304 | tf_op jit(solution)/shard_map/reduce_scatter | solution.py:288
  1135.1 39.6 %all-reduce.6 = (f32[2048]{0:T(1024)}, f32[128]{0:T(128)}, f32[128]{0:T(128)}, f32[2048]{0:T(1024)}) all-reduce(f32[2048]{0:T(1024)S(1)} %get-tuple-element.375, f32[128]{0:T(128)S(1)} %get-tuple-element.371, f32[128]{0:T(128)S(1)} %get-tuple-element.373, ...), channel_id=1, replica_groups=mesh['expert'=4,'row'=4,'col'=2] {'expert','row','col'}, use_global_device_ids=true, to_apply=%region_33.34 | all-reduce | flops 4352 | bytes 34816 | tf_op jit(solution)/shard_map/psum | solution.py:317
  1174.7 85.9 %all-reduce.13.cloned.1.call-done = f32[2048,32]{0,1:T(8,128)} async-done(((f32[2048,32]{0,1:T(8,128)}), f32[2048,32]{0,1:T(8,128)}) %all-reduce.13.cloned.1.call-update) | async-done | bytes 262160 | tf_op jit(solution)/shard_map/psum | solution.py:317
  (385 shorter events, 345.7 us)
Async XLA Ops:
  7.2 440.6 %copy-start = (bf16[1,768,2048]{2,1,0:T(8,128)(2,1)S(1)}, bf16[1,768,2048]{2,1,0:T(8,128)(2,1)}, u32[]{:S(2)}) copy-start(bf16[1,768,2048]{2,1,0:T(8,128)(2,1)} %param.32) | copy-start | bytes 9437188
  7.2 43.9 %all-gather.3.cloned.1.call-start = ((), (), s32[]{:S(2)}) async-start(), calls=%async_computation.6 | async-start | bytes 4718592 | tf_op jit(solution)/shard_map/all_gather | solution.py:98
  11.7 155.0 %reduce-scatter.3.cloned.1.call-start = ((), (), s32[]{:S(2)}) async-start(), calls=%async_computation.7 | async-start | bytes 4718592 | tf_op jit(solution)/shard_map/reduce_scatter | solution.py:148
  22.8 61.4 %copy-start.22 = (f32[1024,64]{0,1:T(8,128)}, f32[1024,64]{0,1:T(8,128)S(1)}, u32[]{:S(2)}) copy-start(f32[1024,64]{0,1:T(8,128)S(1)} %broadcast_multiply_fusion.1) | copy-start | bytes 786436
  115.6 52.6 %copy-start.46 = (f32[2048]{0:T(1024)S(1)}, f32[2048]{0:T(1024)}, u32[]{:S(2)}) copy-start(f32[2048]{0:T(1024)} %param.28) | copy-start | bytes 24580
  190.3 121.3 %all-to-all-start = ((bf16[32,34,2048]{2,1,0:T(8,128)(2,1)}), bf16[32,34,2048]{2,1,0:T(8,128)(2,1)}, u32[]{:S(2)}, u32[]{:S(2)}) async-start(bf16[32,34,2048]{2,1,0:T(8,128)(2,1)} %reshape.555), calls=%async_computation.1 | async-start | bytes 10485760 | tf_op jit(solution)/shard_map/all_to_all | solution.py:63
  311.5 128.9 %all-to-all-start.2 = ((bf16[32,34,2048]{2,1,0:T(8,128)(2,1)}), bf16[32,34,2048]{2,1,0:T(8,128)(2,1)}, u32[]{:S(2)}, u32[]{:S(2)}) async-start(bf16[32,34,2048]{2,1,0:T(8,128)(2,1)} %reshape.559), calls=%async_computation.3 | async-start | bytes 10485760 | tf_op jit(solution)/shard_map/all_to_all | solution.py:63
  472.0 121.1 %all-to-all-start.1 = ((bf16[32,34,2048]{2,1,0:T(8,128)(2,1)}), bf16[32,34,2048]{2,1,0:T(8,128)(2,1)}, u32[]{:S(2)}, u32[]{:S(2)}) async-start(bf16[32,34,2048]{2,1,0:T(8,128)(2,1)} %reshape.557), calls=%async_computation.2 | async-start | bytes 10485760 | tf_op jit(solution)/shard_map/all_to_all | solution.py:63
  494.8 102.5 %copy-start.76 = (s32[2]{0:T(128)S(1)}, s32[2]{0:T(128)}, u32[]{:S(2)}) copy-start(s32[2]{0:T(128)} %constant.159) | copy-start | bytes 28
  494.8 102.6 %copy-start.75 = (s32[2]{0:T(128)S(1)}, s32[2]{0:T(128)}, u32[]{:S(2)}) copy-start(s32[2]{0:T(128)} %constant.162) | copy-start | bytes 28
  593.1 120.3 %all-to-all-start.3 = ((bf16[32,34,2048]{2,1,0:T(8,128)(2,1)}), bf16[32,34,2048]{2,1,0:T(8,128)(2,1)}, u32[]{:S(2)}, u32[]{:S(2)}) async-start(bf16[32,34,2048]{2,1,0:T(8,128)(2,1)} %reshape.561), calls=%async_computation.4 | async-start | bytes 10485760 | tf_op jit(solution)/shard_map/all_to_all | solution.py:63
  597.2 187.8 %all-gather.5.cloned.1.call-start = ((), (), s32[]{:S(2)}) async-start(), calls=%async_computation.8 | async-start | bytes 4718592 | tf_op jit(solution)/shard_map/all_gather | solution.py:237
  748.6 167.4 %all-reduce.15.cloned.1.call-start = ((), (), s32[]{:S(2)}) async-start(), calls=%async_computation.11 | async-start | bytes 2097152 | tf_op jit(solution)/shard_map/psum | solution.py:310
  859.2 216.6 %all-reduce.17.cloned.1.call-start = ((), (), s32[]{:S(2)}) async-start(), calls=%async_computation.12 | async-start | bytes 8388608 | tf_op jit(solution)/shard_map/psum | solution.py:306
  871.1 258.3 %reduce-scatter.5.cloned.1.call-start = ((), (), s32[]{:S(2)}) async-start(), calls=%async_computation.9 | async-start | bytes 4718592 | tf_op jit(solution)/shard_map/reduce_scatter | solution.py:288
  884.0 376.6 %all-reduce.13.cloned.1.call-start = ((), (), s32[]{:S(2)}) async-start(), calls=%async_computation.10 | async-start | bytes 524288 | tf_op jit(solution)/shard_map/psum | solution.py:317
  1080.1 49.2 %copy-start.53 = (f32[2048]{0:T(1024)S(1)}, f32[2048]{0:T(1024)}, u32[]{:S(2)}) copy-start(f32[2048]{0:T(1024)} %param.21) | copy-start | bytes 24580
  1080.1 49.2 %copy-start.68 = (f32[128]{0:T(128)S(1)}, f32[128]{0:T(128)}, u32[]{:S(2)}) copy-start(f32[128]{0:T(128)} %copy-done.67) | copy-start | bytes 1540
  1080.2 51.0 %copy-start.72 = (f32[128]{0:T(128)S(1)}, f32[128]{0:T(128)}, u32[]{:S(2)}) copy-start(f32[128]{0:T(128)} %copy-done.71) | copy-start | bytes 1540
  1080.2 51.0 %copy-start.48 = (f32[2048]{0:T(1024)S(1)}, f32[2048]{0:T(1024)}, u32[]{:S(2)}) copy-start(f32[2048]{0:T(1024)} %param.28) | copy-start | bytes 24580
  1080.2 51.0 %copy-start.64 = (f32[128]{0:T(128)S(1)}, f32[128]{0:T(128)}, u32[]{:S(2)}) copy-start(f32[128]{0:T(128)} %copy-done.62) | copy-start | bytes 1540
  1080.2 51.0 %copy-start.70 = (f32[128]{0:T(128)S(1)}, f32[128]{0:T(128)}, u32[]{:S(2)}) copy-start(f32[128]{0:T(128)} %copy-done.69) | copy-start | bytes 1540
  1080.2 182.1 %copy-start.1 = (bf16[1,768,2048]{2,1,0:T(8,128)(2,1)S(1)}, bf16[1,768,2048]{2,1,0:T(8,128)(2,1)}, u32[]{:S(2)}) copy-start(bf16[1,768,2048]{2,1,0:T(8,128)(2,1)} %param.32) | copy-start | bytes 9437188
  1082.7 52.4 %copy-start.59 = (f32[2048]{0:T(1024)S(1)}, f32[2048]{0:T(1024)}, u32[]{:S(2)}) copy-start(f32[2048]{0:T(1024)} %get-tuple-element.369) | copy-start | bytes 24580
  (83 other events, 832.9 us)
Sparse Core Ops, SparseCore 0:
  11.9 39.2 all-gather.2
  115.7 50.9 reduce-scatter.2
  748.8 36.2 all-gather.4
  859.3 56.7 all-reduce.14
  919.6 156.1 all-reduce.16
  1079.0 50.3 reduce-scatter.4
  1136.4 124.1 all-reduce.12
where the time goes:
time: 1280 us; the launch traced here: 1270 us
  waiting for transfers between devices  758 us (59%)
  matrix products  170 us (13%)
  local copies, waits for them, and re-layouts  161 us (13%)
  other arithmetic  96.3 us (8%)
  blocking collectives  39.6 us (3%)
  starting transfers between devices  27.5 us (2%)
  between operations  15.6 us (1%)
    all_to_all x4, waiting for transfers between devices, move_slots(): lax.all_to_all(slot_block, ('expert', 'row', 'col'), split_axis=0, concat...  364 us
    psum x1, waiting for transfers between devices, local(): lax.psum(grad_query.astype(jnp.bfloat16), 'expert').astype(jnp.float32)  156 us
    psum x1, waiting for transfers between devices, local(): lax.psum((grad_norm_attn, grad_q_gain, grad_k_gain, grad_norm_moe, grad_r...  85.9 us
    reduce_scatter x1, waiting for transfers between devices, local(): lax.psum_scatter((times_transposed(grad_query_low, w_query) + jnp.einsum(...  46.6 us
    psum x1, blocking collectives, local(): lax.psum((grad_norm_attn, grad_q_gain, grad_k_gain, grad_norm_moe, grad_r...  39.6 us
    all_gather x1, waiting for transfers between devices, local(): lax.all_gather(grad_attn_low, ('row', 'col'), axis=0, tiled=True)  36.1 us
    reduce_scatter x1, waiting for transfers between devices, local(): lax.psum_scatter(jnp.dot(heads_low, w_out, preferred_element_type=jnp.flo...  36 us
    dot_general x5, matrix products, transposed_times(): lax.dot_general(left, right, (((0,), (0,)), ((), ())), preferred_element_...  32.5 us
  transfers between devices with their start and end apart: 11, of which 11 were waited for; matrix products, arithmetic and copies ran while one was open for 15% of the time, Pallas kernels for 0%

commit v1 on v0

--- a/solution.py
+++ b/solution.py
@@ -6,6 +6,7 @@
 eps_norm = 1e-06
 rope_base = 1000000.0
 highest = lax.Precision.HIGHEST
+chunk_count = 2
 
 
 def rms_scale(values, norm_gain):
@@ -59,10 +60,80 @@
     )
 
 
-def move_slots(slot_block):
-    return lax.all_to_all(
-        slot_block, ("expert", "row", "col"), split_axis=0, concat_axis=0, tiled=True
-    )
+plane_axes = ("row", "col")
+
+
+def move_plane(parts):
+    return lax.all_to_all(parts, plane_axes, split_axis=0, concat_axis=0, tiled=True)
+
+
+def plane_shift(block, step):
+    planes = lax.axis_size("expert")
+    return lax.ppermute(block, "expert", [(i, (i + step) % planes) for i in range(planes)])
+
+
+def gather_planes(block):
+    planes = lax.axis_size("expert")
+    return jnp.concatenate([block] + [plane_shift(block, k) for k in range(1, planes)], axis=0)
+
+
+def sum_everywhere(values):
+    plane_size = lax.axis_size(plane_axes)
+    planes = lax.axis_size("expert")
+    shares = jnp.sum(move_plane(values.reshape(plane_size, -1, 128)), axis=0)
+    shares = lax.all_to_all(
+        jnp.broadcast_to(shares[None], (planes,) + shares.shape), "expert", 0, 0, tiled=True
+    )
+    shares = jnp.sum(shares, axis=0)
+    return move_plane(jnp.broadcast_to(shares[None], (plane_size,) + shares.shape)).reshape(-1)
+
+
+def sum_small(values):
+    plane_size = lax.axis_size(plane_axes)
+    planes = lax.axis_size("expert")
+    values = values.reshape(-1, 128)
+    values = jnp.sum(
+        move_plane(jnp.broadcast_to(values[None], (plane_size,) + values.shape)), axis=0
+    )
+    return jnp.sum(
+        lax.all_to_all(
+            jnp.broadcast_to(values[None], (planes,) + values.shape), "expert", 0, 0, tiled=True
+        ),
+        axis=0,
+    ).reshape(-1)
+
+
+def rotate(block, axis, step):
+    size = lax.axis_size(axis)
+    return lax.ppermute(block, axis, [(i, (i + step) % size) for i in range(size)])
+
+
+def scatter_plane(product):
+    col = lax.axis_index("col")
+    cols = lax.axis_size("col")
+    row = lax.axis_index("row")
+    rows = lax.axis_size("row")
+    moved = [rotate(product((col + k) % cols).astype(jnp.bfloat16), "col", k) for k in range(1, cols)]
+    total = product(col)
+    for part in moved:
+        total = total + part.astype(jnp.float32)
+    low = total.astype(jnp.bfloat16)
+
+    def piece(k):
+        return lax.dynamic_index_in_dim(low, (row + k) % rows, 0, keepdims=False)
+
+    arrived = [rotate(piece(k), "row", k) for k in range(1, rows)]
+    result = piece(0).astype(jnp.float32)
+    for part in arrived:
+        result = result + part.astype(jnp.float32)
+    return result
+
+
+def return_planes(parts):
+    total = parts[0].astype(jnp.float32)
+    for k in range(1, parts.shape[0]):
+        total = total + plane_shift(parts[k], -k).astype(jnp.float32)
+    return total
 
 
 def local(
@@ -92,6 +163,60 @@
     experts = w_router.shape[1]
     top_count = routes.shape[1]
     capacity = tok_dev * top_count * 17 // (16 * experts)
+    planes = lax.axis_size("expert")
+    plane_size = lax.axis_size(plane_axes)
+    plane_index = lax.axis_index("expert")
+    plane_cap = planes * capacity
+    chosen_here = jnp.any(
+        routes[:, :, None] == jnp.arange(experts, dtype=jnp.int32)[None, None, :], axis=1
+    )
+    plane_routes = gather_planes(routes.T[None])
+    plane_experts = plane_index * plane_size + jnp.arange(plane_size, dtype=jnp.int32)
+    chosen_plane = jnp.any(
+        plane_routes[None] == plane_experts[:, None, None, None], axis=2
+    )
+    token_ids = jnp.arange(tok_dev, dtype=jnp.int32)
+    earlier = (token_ids[:, None] < token_ids[None, :]).astype(jnp.bfloat16)
+    slot_rank = jnp.dot(
+        chosen_plane.astype(jnp.bfloat16).reshape(plane_size * planes, tok_dev),
+        earlier,
+        preferred_element_type=jnp.float32,
+    ).astype(jnp.int32).reshape(plane_size, planes, tok_dev)
+    plane_slot = jnp.where(
+        chosen_plane,
+        slot_rank + (jnp.arange(planes, dtype=jnp.int32) * capacity)[None, :, None],
+        -1,
+    ).reshape(plane_size, 1, planes * tok_dev)
+    dispatch = (
+        plane_slot == jnp.arange(plane_cap, dtype=jnp.int32)[None, :, None]
+    ).astype(jnp.bfloat16)
+    chosen_all = jnp.any(
+        plane_routes[:, :, :, None] == jnp.arange(experts, dtype=jnp.int32), axis=1
+    ).reshape(planes * tok_dev, experts).astype(jnp.bfloat16)
+
+    def send_slots(rows_all):
+        return move_plane(
+            jnp.dot(
+                dispatch.reshape(plane_size * plane_cap, -1),
+                rows_all,
+                preferred_element_type=jnp.float32,
+            )
+            .astype(jnp.bfloat16)
+            .reshape(plane_size, plane_cap, rows_all.shape[1])
+        ).reshape(plane_size * plane_cap, rows_all.shape[1])
+
+    slot_chosen = send_slots(chosen_all) > 0.5
+    chunk_width = model_width // chunk_count
+    chunks = [slice(i * chunk_width, (i + 1) * chunk_width) for i in range(chunk_count)]
+    grad_slots = jnp.concatenate(
+        [send_slots(gather_planes(out_grad[:, cut])) for cut in chunks], axis=1
+    )
+
+    def gates_of(all_logits, chosen):
+        top = jnp.max(jnp.where(chosen, all_logits, -3e38), axis=1, keepdims=True)
+        raised = jnp.where(chosen, jnp.exp(jnp.where(chosen, all_logits - top, 0.0)), 0.0)
+        return raised / jnp.maximum(jnp.sum(raised, axis=1, keepdims=True), 1e-30)
+
     input_rows = layer_input.astype(jnp.float32)
     normed_one, norm_one_back = jax.vjp(rms_scale, input_rows, norm_attn)
     normed_low = normed_one.astype(jnp.bfloat16)
@@ -155,78 +280,94 @@
     normed_two, norm_two_back = jax.vjp(rms_scale, mixed_rows, norm_moe)
     moe_input = normed_two.astype(jnp.bfloat16)
     router_logits = jnp.dot(moe_input, w_router, preferred_element_type=jnp.float32)
-
-    def route_gates(all_logits):
-        chosen = jnp.take_along_axis(all_logits, routes, axis=1)
-        chosen = chosen - jnp.max(chosen, axis=1, keepdims=True)
-        raised = jnp.exp(chosen)
-        return raised / jnp.sum(raised, axis=1, keepdims=True)
-
-    gate_values, gates_back = jax.vjp(route_gates, router_logits)
-    picked = routes.reshape(-1)
-    assign_count = picked.shape[0]
-    onehot = (picked[:, None] == jnp.arange(experts, dtype=jnp.int32)[None, :]).astype(jnp.int32)
-    slot_rank = (
-        jnp.sum(jnp.cumsum(onehot, axis=0, dtype=jnp.int32) * onehot, axis=1, dtype=jnp.int32) - 1
-    )
-    slot_index = picked * capacity + slot_rank
-    slot_owner = (
-        jnp.full((experts * capacity,), assign_count, jnp.int32)
-        .at[slot_index]
-        .set(jnp.arange(assign_count, dtype=jnp.int32))
-    )
-    owner_row = slot_owner // top_count
-    padded_input = jnp.concatenate([moe_input, jnp.zeros((1, model_width), jnp.bfloat16)], axis=0)
-    send_rows = padded_input[owner_row].reshape(experts, capacity, model_width)
-    slot_rows = move_slots(send_rows).reshape(experts * capacity, model_width)
+    source_gates = gates_of(router_logits, chosen_here)
+
+    slot_chunks = [send_slots(gather_planes(moe_input[:, cut])) for cut in chunks]
+    moe_slots = jnp.concatenate(slot_chunks, axis=1)
     gate_matrix = w_gate[0]
     up_matrix = w_up[0]
     down_matrix = w_down[0]
-    gate_pre = jnp.dot(slot_rows, gate_matrix, preferred_element_type=jnp.float32)
-    up_pre = jnp.dot(slot_rows, up_matrix, preferred_element_type=jnp.float32)
+
+    def slots_times(weights):
+        return sum(
+            jnp.dot(part, weights[cut], preferred_element_type=jnp.float32)
+            for part, cut in zip(slot_chunks, chunks)
+        )
+
+    slot_logits = slots_times(w_router)
+    own_expert = plane_index * plane_size + lax.axis_index(plane_axes)
+    own_column = jnp.arange(experts, dtype=jnp.int32)[None, :] == own_expert
+    slot_gates = jnp.sum(
+        jnp.where(own_column, gates_of(slot_logits, slot_chosen), 0.0), axis=1, keepdims=True
+    )
+    gate_pre = slots_times(gate_matrix)
+    up_pre = slots_times(up_matrix)
     hidden_low = (jax.nn.silu(gate_pre) * up_pre).astype(jnp.bfloat16)
-    expert_out = jnp.dot(hidden_low, down_matrix, preferred_element_type=jnp.float32).astype(
-        jnp.bfloat16
-    )
-    returned = move_slots(expert_out.reshape(experts, capacity, model_width)).reshape(
-        experts * capacity, model_width
-    )
-    assigned = returned[slot_index].reshape(tok_dev, top_count, model_width)
-    moe_rows = jnp.sum(gate_values[:, :, None] * assigned, axis=1)
-    out_rows = (mixed_rows + moe_rows).astype(jnp.bfloat16)
+    expert_out = (
+        jnp.dot(hidden_low, down_matrix, preferred_element_type=jnp.float32)
+        .astype(jnp.bfloat16)
+        .astype(jnp.float32)
+    )
+    slot_grads_full = grad_slots.astype(jnp.float32)
+    slot_dots = jnp.sum(expert_out * slot_grads_full, axis=1)
+    weighted_out = (expert_out * slot_gates).astype(jnp.bfloat16)
+    grad_out_slots = (slot_grads_full * slot_gates).astype(jnp.bfloat16)
+
+    def combine(slot_values):
+        width = slot_values.shape[1]
+        returned = move_plane(slot_values.reshape(plane_size, plane_cap, width))
+        summed = lax.dot_general(
+            dispatch.reshape(plane_size * plane_cap, -1),
+            returned.reshape(plane_size * plane_cap, width),
+            (((0,), (0,)), ((), ())),
+            preferred_element_type=jnp.float32,
+        ).astype(jnp.bfloat16)
+        return return_planes(summed.reshape(planes, tok_dev, width))
+
+    returned_dots = move_plane(slot_dots.reshape(plane_size, 1, plane_cap)).reshape(
+        plane_size, plane_cap, 1
+    )
+    token_dots = jnp.sum(dispatch.astype(jnp.float32) * returned_dots, axis=1).reshape(
+        plane_size, planes, tok_dev
+    )
+    dot_parts = jnp.stack(
+        [token_dots[:, 0]] + [plane_shift(token_dots[:, k], -k) for k in range(1, planes)], axis=0
+    )
+    dot_parts = lax.dynamic_slice_in_dim(
+        jnp.concatenate([dot_parts, dot_parts], axis=0), planes - plane_index, planes, axis=0
+    )
+    grad_gates = dot_parts.reshape(experts, tok_dev).T
     grad_rows = out_grad.astype(jnp.float32)
-    grad_gates = jnp.sum(assigned * grad_rows[:, None, :], axis=2)
-    grad_assigned = (
-        (gate_values[:, :, None] * grad_rows[:, None, :])
-        .astype(jnp.bfloat16)
-        .reshape(assign_count, model_width)
-    )
-    padded_grad = jnp.concatenate(
-        [grad_assigned, jnp.zeros((1, model_width), jnp.bfloat16)], axis=0
-    )
-    grad_send = padded_grad[slot_owner].reshape(experts, capacity, model_width)
-    grad_out_slots = move_slots(grad_send).reshape(experts * capacity, model_width)
+    grad_logits = source_gates * (
+        grad_gates - jnp.sum(source_gates * grad_gates, axis=1, keepdims=True)
+    )
     grad_hidden = times_transposed(grad_out_slots, down_matrix)
-    grad_down = transposed_times(hidden_low, grad_out_slots)
     sigmoid_gate = jax.nn.sigmoid(gate_pre)
     grad_gate_pre = (
         grad_hidden * up_pre * sigmoid_gate * (1.0 + gate_pre * (1.0 - sigmoid_gate))
     ).astype(jnp.bfloat16)
     grad_up_pre = (grad_hidden * jax.nn.silu(gate_pre)).astype(jnp.bfloat16)
-    grad_gate = transposed_times(slot_rows, grad_gate_pre)
-    grad_up = transposed_times(slot_rows, grad_up_pre)
-    grad_slot_rows = (
-        times_transposed(grad_gate_pre, gate_matrix) + times_transposed(grad_up_pre, up_matrix)
-    ).astype(jnp.bfloat16)
-    grad_back = move_slots(grad_slot_rows.reshape(experts, capacity, model_width)).reshape(
-        experts * capacity, model_width
-    )
-    grad_moe_input = jnp.sum(
-        grad_back[slot_index].reshape(tok_dev, top_count, model_width), axis=1, dtype=jnp.float32
-    )
-    grad_logits = gates_back(grad_gates)[0]
-    grad_router = jnp.einsum(
-        "td,te->de", moe_input, grad_logits, precision=highest, preferred_element_type=jnp.float32
+    grad_moe_input = jnp.concatenate(
+        [
+            combine(
+                (
+                    times_transposed(grad_gate_pre, gate_matrix[cut])
+                    + times_transposed(grad_up_pre, up_matrix[cut])
+                ).astype(jnp.bfloat16)
+            )
+            for cut in chunks
+        ],
+        axis=1,
+    )
+    grad_down = transposed_times(hidden_low, grad_out_slots)
+    grad_gate = transposed_times(moe_slots, grad_gate_pre)
+    grad_up = transposed_times(moe_slots, grad_up_pre)
+    grad_router = lax.dot_general(
+        grad_logits,
+        moe_input.astype(jnp.float32),
+        (((0,), (0,)), ((), ())),
+        precision=highest,
+        preferred_element_type=jnp.float32,
     )
     grad_moe_input = grad_moe_input + jnp.einsum(
         "te,de->td", grad_logits, w_router, precision=highest, preferred_element_type=jnp.float32
@@ -235,7 +376,16 @@
     grad_mixed = grad_rows + grad_mixed_norm
     grad_attn_low = grad_mixed.astype(jnp.bfloat16)
     grad_group = lax.all_gather(grad_attn_low, ("row", "col"), axis=0, tiled=True)
-    grad_out_proj = transposed_times(heads_low, grad_group)
+    weighted_out, grad_group = lax.optimization_barrier((weighted_out, grad_group))
+    out_rows = (mixed_rows + combine(weighted_out)).astype(jnp.bfloat16)
+    grad_out_proj = lax.psum(
+        transposed_times(heads_low, grad_group).astype(jnp.bfloat16), "expert"
+    ).astype(jnp.float32)
+    router_sums = sum_everywhere(
+        jnp.concatenate([grad_router.reshape(-1), grad_norm_moe])
+    )
+    grad_router = router_sums[: experts * model_width].reshape(experts, model_width).T
+    grad_norm_moe = router_sums[experts * model_width :]
     grad_heads = (
         times_transposed(grad_group, w_out)
         .astype(jnp.bfloat16)
@@ -280,44 +430,51 @@
     grad_key_pre, grad_k_gain = key_back(grad_key_post)
     grad_query_low = grad_query_pre.reshape(group_tok, local_heads * head_dim).astype(jnp.bfloat16)
     grad_query = transposed_times(group_rows, grad_query_low)
-    grad_kv = jnp.concatenate([grad_key_pre, grad_value_pre], axis=1)
-    grad_key_value = jnp.einsum(
-        "td,te->de", group_rows, grad_kv, precision=highest, preferred_element_type=jnp.float32
-    )
+    grad_kv = jnp.concatenate([grad_key_pre, grad_value_pre], axis=1).astype(jnp.bfloat16)
+    grad_key_value = transposed_times(group_rows, grad_kv)
     key_value_w = jnp.concatenate([w_key, w_value], axis=1)
-    grad_normed = lax.psum_scatter(
-        (
-            times_transposed(grad_query_low, w_query)
-            + jnp.einsum(
-                "te,de->td",
-                grad_kv,
-                key_value_w,
-                precision=highest,
-                preferred_element_type=jnp.float32,
-            )
-        ).astype(jnp.bfloat16),
-        ("row", "col"),
-        scatter_dimension=0,
-        tiled=True,
-    ).astype(jnp.float32)
-    grad_input_norm, grad_norm_attn = norm_one_back(grad_normed)
+    norm_terms = (
+        jnp.sum(grad_query * w_query.astype(jnp.float32), axis=1)
+        + jnp.sum(grad_key_value * key_value_w.astype(jnp.float32), axis=1)
+    ) / norm_attn
+    cols = lax.axis_size("col")
+    col = lax.axis_index("col")
+    kv_low = grad_key_value.astype(jnp.bfloat16).reshape(cols, model_width // cols, 2 * head_dim)
+    kv_part = lax.dynamic_index_in_dim(kv_low, col, 0, keepdims=False).astype(jnp.float32)
+    for k in range(1, cols):
+        kv_part = kv_part + rotate(
+            lax.dynamic_index_in_dim(kv_low, (col + k) % cols, 0, keepdims=False), "col", k
+        ).astype(jnp.float32)
+    query_low_grad, kv_part, grad_out_proj = lax.optimization_barrier(
+        (grad_query.astype(jnp.bfloat16), kv_part.astype(jnp.bfloat16), grad_out_proj)
+    )
+    grad_query, kv_part = lax.psum((query_low_grad, kv_part), "expert")
+    grad_query = grad_query.astype(jnp.float32)
+    kv_parts = jnp.stack([kv_part] + [rotate(kv_part, "col", k) for k in range(1, cols)], axis=0)
+    kv_parts = lax.dynamic_slice_in_dim(
+        jnp.concatenate([kv_parts[::-1], kv_parts[::-1]], axis=0), cols - 1 - col, cols, axis=0
+    )
+    kv_full = kv_parts.reshape(model_width, 2 * head_dim).astype(jnp.float32)
+    grad_key = kv_full[:, :head_dim]
+    grad_value = kv_full[:, head_dim:]
+    small_sums = sum_small(jnp.concatenate([norm_terms, grad_q_gain, grad_k_gain]))
+    grad_norm_attn = small_sums[:model_width]
+    grad_q_gain = small_sums[model_width : model_width + head_dim]
+    grad_k_gain = small_sums[model_width + head_dim :]
+    left_parts = jnp.concatenate([grad_query_low, grad_kv], axis=1).reshape(
+        -1, cols, tok_dev, grad_query_low.shape[1] + 2 * head_dim
+    )
+    right_all = jnp.concatenate([w_query, key_value_w], axis=1)
+
+    def grad_normed_rows(place):
+        left = lax.dynamic_index_in_dim(left_parts, place, 1, keepdims=False)
+        return lax.dot_general(
+            left, right_all, (((2,), (1,)), ((), ())), preferred_element_type=jnp.float32
+        )
+
+    grad_normed = scatter_plane(grad_normed_rows)
+    grad_input_norm = norm_one_back(grad_normed)[0]
     grad_x = (grad_mixed + grad_input_norm).astype(jnp.bfloat16)
-    grad_query, grad_out_proj = (
-        lax.psum(grad_query.astype(jnp.bfloat16), "expert").astype(jnp.float32),
-        lax.psum(grad_out_proj.astype(jnp.bfloat16), "expert").astype(jnp.float32),
-    )
-    grad_key, grad_value = (
-        lax.psum(grad_key_value[:, :head_dim].astype(jnp.bfloat16), ("expert", "col")).astype(
-            jnp.float32
-        ),
-        lax.psum(grad_key_value[:, head_dim:].astype(jnp.bfloat16), ("expert", "col")).astype(
-            jnp.float32
-        ),
-    )
-    grad_norm_attn, grad_q_gain, grad_k_gain, grad_norm_moe, grad_router = lax.psum(
-        (grad_norm_attn, grad_q_gain, grad_k_gain, grad_norm_moe, grad_router),
-        ("expert", "row", "col"),
-    )
     return (
         out_rows,
         grad_x,

time: 1280 us -> 881 us (0.69)
  waiting for transfers between devices: 758 us -> 383 us
  starting transfers between devices: 27.5 us -> 137 us
  local copies, waits for them, and re-layouts: 161 us -> 69.5 us
  blocking collectives: 39.6 us -> 0 us
  other arithmetic: 96.3 us -> 66.1 us
  matrix products: 170 us -> 197 us
    all_to_all x4 -> x14, waiting for transfers between devices: 364 us -> 31.6 us  [the longest x12 31.6 us: move_plane(): lax.all_to_all(parts, plane_axes, split_axis=0, concat_axis=0, tiled=True)]
    ppermute x0 -> x33, waiting for transfers between devices: none -> 101 us  [the longest x27 87.4 us: plane_shift(): lax.ppermute(block, 'expert', [(i, (i + step) % planes) for i in range(pl...]
    psum x3 -> x2, waiting for transfers between devices: 247 us -> 162 us  [the longest x1 106 us: local(): grad_query, kv_part = lax.psum((query_low_grad, kv_part), 'expert')]
    ppermute x0 -> x33, starting transfers between devices: none -> 60.6 us  [the longest x27 55.8 us: plane_shift(): lax.ppermute(block, 'expert', [(i, (i + step) % planes) for i in range(pl...]
    gather x10 -> x0, local copies, waits for them, and re-layouts: 55.7 us -> none  [the longest x1 13.3 us: local(): grad_send = padded_grad[slot_owner].reshape(experts, capacity, model_width)]
    reshape x8 -> x6, local copies, waits for them, and re-layouts: 58.3 us -> 3.22 us  [the longest x2 1.77 us: send_slots(): return move_plane(jnp.dot(dispatch.reshape(plane_size * plane_cap, -1), r...]
    all_to_all x4 -> x14, starting transfers between devices: 26.9 us -> 76.5 us  [the longest x12 68.4 us: move_plane(): lax.all_to_all(parts, plane_axes, split_axis=0, concat_axis=0, tiled=True)]
    reduce_scatter x1 -> x0, waiting for transfers between devices: 46.6 us -> none  [local(): lax.psum_scatter((times_transposed(grad_query_low, w_query) + jnp.einsum(...]
  transfers between devices with their start and end apart: 11 -> 52, of which waited for: 11 -> 26; matrix products, arithmetic and copies ran while one was open for 15% -> 25% of each run, Pallas kernels for 0% -> 0%
where the time goes in v1:
time: 881 us; the launch traced here: 870 us
  waiting for transfers between devices  383 us (43%)
  matrix products  197 us (22%)
  starting transfers between devices  137 us (16%)
  local copies, waits for them, and re-layouts  69.5 us (8%)
  other arithmetic  66.1 us (8%)
  between operations  15.8 us (2%)
    psum x1, waiting for transfers between devices, local(): grad_query, kv_part = lax.psum((query_low_grad, kv_part), 'expert')  106 us
    ppermute x27, waiting for transfers between devices, plane_shift(): lax.ppermute(block, 'expert', [(i, (i + step) % planes) for i in range(pl...  87.4 us
    all_to_all x12, starting transfers between devices, move_plane(): lax.all_to_all(parts, plane_axes, split_axis=0, concat_axis=0, tiled=True)  68.4 us
    psum x1, waiting for transfers between devices, local(): lax.psum(transposed_times(heads_low, grad_group).astype(jnp.bfloat16), 'e...  56.8 us
    ppermute x27, starting transfers between devices, plane_shift(): lax.ppermute(block, 'expert', [(i, (i + step) % planes) for i in range(pl...  55.8 us
    reduce_scatter x1, waiting for transfers between devices, local(): lax.psum_scatter(jnp.dot(heads_low, w_out, preferred_element_type=jnp.flo...  41.7 us
    dot_general x6, matrix products, transposed_times(): lax.dot_general(left, right, (((0,), (0,)), ((), ())), preferred_element_...  41 us
    dot_general x6, matrix products, times_transposed(): lax.dot_general(left, right, (((1,), (1,)), ((), ())), preferred_element_...  31.9 us
  transfers between devices with their start and end apart: 52, of which 26 were waited for; matrix products, arithmetic and copies ran while one was open for 25% of the time, Pallas kernels for 0%

profile of v1, /device:TPU:1, one launch (start us, length us, event | category | flops | bytes accessed | tf_op | source)
XLA Modules:
  0.0 869.6 jit_solution(17553378968550089610)
XLA Ops:
  12.7 9.1 %fusion.150 = (f32[2,512,128]{1,0,2:T(2,128)}, f32[2,512,128]{1,0,2:T(2,128)}) fusion(f32[2,512,64]{1,0,2:T(2,128)S(1)} %broadcast_multiply_fusion.2), kind=kLoop, calls=%fused_computation.246 | loop fusion | flops 131072 | bytes 1310720 | tf_op jit(solution)/shard_map/cos | solution.py:30
  21.8 28.2 %all-gather.3.cloned.1.call-done = bf16[1024,2048]{1,0:T(8,128)(2,1)} async-done(((bf16[128,2048]{1,0:T(8,128)(2,1)}), bf16[1024,2048]{1,0:T(8,128)(2,1)}) %all-gather.3.cloned.1.call-update) | async-done | bytes 4194320 | tf_op jit(solution)/shard_map/all_gather | solution.py:223
  92.0 16.1 %while.27 = (s32[]{:T(128)}, bf16[2,512,4,128]{3,2,1,0:T(4,128)(2,1)}, f32[2,4,512]{2,1,0:T(4,128)S(1)}, s32[2,512]{1,0:T(2,128)S(1)}, s32[1024]{0:T(1024)S(1)},...) while((s32[]{:T(128)}, ...), condition=%wide.region_8.9_spmd, body=%wide.region_6.8_spmd.sunk | while | flops 1090254848 | bytes 30462168 | solution.py:271
  123.8 41.7 %reduce-scatter.2.cloned.1.call-done = bf16[128,2048]{1,0:T(8,128)(2,1)} async-done(((bf16[1024,2048]{1,0:T(8,128)(2,1)}), bf16[128,2048]{1,0:T(8,128)(2,1)}) %reduce-scatter.2.cloned.1.call-update) | async-done | bytes 524304 | tf_op jit(solution)/shard_map/reduce_scatter | solution.py:273
  182.6 12.8 %collective-permute-done.4 = bf16[128,1024]{1,0:T(8,128)(2,1)} collective-permute-done((bf16[128,1024]{1,0:T(8,128)(2,1)}, bf16[128,1024]{1,0:T(8,128)(2,1)}, u32[]{:S(2)}, u32[]{:S(2)}) %collective-permute-start.4) | collective-permute-done | bytes 262176 | tf_op jit(solution)/shard_map/ppermute | solution.py:72
  213.2 18.1 %collective-permute-done.7 = bf16[128,1024]{1,0:T(8,128)(2,1)S(1)} collective-permute-done((bf16[128,1024]{1,0:T(8,128)(2,1)}, bf16[128,1024]{1,0:T(8,128)(2,1)S(1)}, u32[]{:S(2)}, u32[]{:S(2)}) %collective-permute-start.7) | collective-permute-done | bytes 262176 | tf_op jit(solution)/shard_map/ppermute | solution.py:72
  251.2 14.4 %collective-permute-done.13 = bf16[128,1024]{1,0:T(8,128)(2,1)} collective-permute-done((bf16[128,1024]{1,0:T(8,128)(2,1)}, bf16[128,1024]{1,0:T(8,128)(2,1)}, u32[]{:S(2)}, u32[]{:S(2)}) %collective-permute-start.13) | collective-permute-done | bytes 262176 | tf_op jit(solution)/shard_map/ppermute | solution.py:72
  275.8 12.3 %collective-permute-done.10 = bf16[128,1024]{1,0:T(8,128)(2,1)} collective-permute-done((bf16[128,1024]{1,0:T(8,128)(2,1)}, bf16[128,1024]{1,0:T(8,128)(2,1)}, u32[]{:S(2)}, u32[]{:S(2)}) %collective-permute-start.10) | collective-permute-done | bytes 262176 | tf_op jit(solution)/shard_map/ppermute | solution.py:72
  334.3 8.7 %multiply_convert_fusion = (bf16[1088,768]{1,0:T(8,128)(2,1)}, bf16[1088,768]{1,0:T(8,128)(2,1)S(1)}, bf16[1088,768]{1,0:T(8,128)(2,1)S(1)}) fusion(f32[1088,768]{1,0:T(8,128)} %convolution_add_fusion.3, f32[1088,768]{1,0:T(8,128)} %convolution_add_fusion.2, bf16[1,768,2048]{2,1,0:T(8,128)(2,1)S(1)} %copy-done, f32[1088]{0:T(1024)S(1)} %copy-done.84, ...), kind=kOutput, calls=%fused_computation.84 | convolution fusion | flops 3448455168 | bytes 19304704 | tf_op jit(solution)/shard_map/dot_general | solution.py:52
  347.0 7.8 fusion.51
  381.1 9.3 %collective-permute-start.23 = (f32[8,128]{1,0:T(8,128)S(1)}, f32[8,128]{1,0:T(8,128)S(1)}, u32[]{:S(2)}, u32[]{:S(2)}) collective-permute-start(f32[8,128]{1,0:T(8,128)S(1)} %get-tuple-element.599), channel_id=1, source_target_pairs={{0,8},{8,16},{16,24},{24,0},{1,9},{9,17},{17,25},{25,1},{2,10},{10... | collective-permute-start | bytes 12296 | tf_op jit(solution)/shard_map/ppermute | solution.py:72
  409.1 9.3 %collective-permute-start.20 = (bf16[128,1024]{1,0:T(8,128)(2,1)S(1)}, bf16[128,1024]{1,0:T(8,128)(2,1)S(1)}, u32[]{:S(2)}, u32[]{:S(2)}) collective-permute-start(bf16[128,1024]{1,0:T(8,128)(2,1)S(1)} %get-tuple-element.584), channel_id=1, source_target_pairs={{0,8},{8,16},{16,24},{24,0},{1,9},{9,17},{17,25},{25,1},{2,10},{10... | collective-permute-start | bytes 786440 | tf_op jit(solution)/shard_map/ppermute | solution.py:72
  421.8 8.4 all-to-all-done.5
  433.6 9.3 %collective-permute-start.17 = (bf16[128,1024]{1,0:T(8,128)(2,1)S(1)}, bf16[128,1024]{1,0:T(8,128)(2,1)S(1)}, u32[]{:S(2)}, u32[]{:S(2)}) collective-permute-start(bf16[128,1024]{1,0:T(8,128)(2,1)S(1)} %get-tuple-element.581), channel_id=1, source_target_pairs={{0,8},{8,16},{16,24},{24,0},{1,9},{9,17},{17,25},{25,1},{2,10},{10... | collective-permute-start | bytes 786440 | tf_op jit(solution)/shard_map/ppermute | solution.py:72
  454.1 10.3 %collective-permute-done.16 = bf16[128,1024]{1,0:T(8,128)(2,1)S(1)} collective-permute-done((bf16[128,1024]{1,0:T(8,128)(2,1)S(1)}, bf16[128,1024]{1,0:T(8,128)(2,1)S(1)}, u32[]{:S(2)}, u32[]{:S(2)}) %collective-permute-start.16) | collective-permute-done | bytes 262176 | tf_op jit(solution)/shard_map/ppermute | solution.py:72
  468.3 9.5 %all-to-all-start.11 = ((f32[8,66,128]{2,1,0:T(8,128)}), f32[8,66,128]{2,1,0:T(8,128)S(1)}, u32[]{:S(2)}, u32[]{:S(2)}) async-start(f32[8,66,128]{2,1,0:T(8,128)} %reshape.652), calls=%async_computation.12 | async-start | bytes 589824 | tf_op jit(solution)/shard_map/all_to_all | solution.py:67
  489.2 18.4 %all-gather.5.cloned.1.call-done = bf16[1024,2048]{1,0:T(8,128)(2,1)} async-done(((bf16[128,2048]{1,0:T(8,128)(2,1)}), bf16[1024,2048]{1,0:T(8,128)(2,1)}) %all-gather.5.cloned.1.call-update) | async-done | bytes 4194320 | tf_op jit(solution)/shard_map/all_gather | solution.py:378
  514.1 31.9 %while.28 = (s32[]{:T(128)}, f32[1024,128]{1,0:T(8,128)S(1)}, f32[1024,128]{1,0:T(8,128)}, f32[2,512,4,128]{3,1,0,2:T(8,128)}, s32[2,512]{1,0:T(2,128)S(1)}, /*i...) while((s32[]{:T(128)}, f32[1024,128]{1,0:T(8,128)S(1)}, ...), condition=%wide.region_25.26_spmd.clone, body=%wide.region_23.25_spmd.clone.sunk | while | flops 2718300160 | bytes 93139240 | solution.py:423
  592.6 9.8 %convolution_bitcast_fusion.2 = f32[1,2048,768]{2,1,0:T(8,128)} fusion(bf16[1088,768]{1,0:T(8,128)(2,1)} %get-tuple-element.557, bf16[1088,1024]{1,0:T(8,128)(2,1)} %bitcast.27, bf16[1088,1024]{1,0:T(8,128)(2,1)} %bitcast.24), kind=kOutput, calls=%fused_computation.82 | convolution fusion | flops 3431464960 | bytes 12419072 | tf_op jit(solution)/shard_map/dot_general | solution.py:58
  624.4 9.5 %convolution_bitcast_fusion.3 = f32[1,2048,768]{2,1,0:T(8,128)} fusion(bf16[1088,768]{1,0:T(8,128)(2,1)S(1)} %copy-done.112, bf16[1088,1024]{1,0:T(8,128)(2,1)} %bitcast.27, bf16[1088,1024]{1,0:T(8,128)(2,1)} %bitcast.24), kind=kOutput, calls=%fused_computation.83 | convolution fusion | flops 3431464960 | bytes 12419072 | tf_op jit(solution)/shard_map/dot_general | solution.py:58
  633.9 9.6 %convolution_bitcast_fusion.1 = f32[1,768,2048]{2,1,0:T(8,128)} fusion(bf16[1088,768]{1,0:T(8,128)(2,1)S(1)} %copy-done.115, f32[1088]{0:T(1024)S(1)} %copy-done.85, bf16[1088,1024]{1,0:T(8,128)(2,1)} %bitcast.36, bf16[1088,1024]{1,0:T(8,128)(2,1)} %bitcast.34), kind=kOutput, calls=%fused_computation.81 | convolution fusion | flops 3435921408 | bytes 12423424 | tf_op jit(solution)/shard_map/dot_general | solution.py:58
  647.1 56.8 %all-reduce.8.cloned.1.call-done = bf16[512,2048]{1,0:T(8,128)(2,1)} async-done(((bf16[512,2048]{1,0:T(8,128)(2,1)}), bf16[512,2048]{1,0:T(8,128)(2,1)}) %all-reduce.8.cloned.1.call-update) | async-done | bytes 2097168 | tf_op jit(solution)/shard_map/psum | solution.py:381
  730.8 9.8 %collective-permute-done.30 = bf16[128,2048]{1,0:T(8,128)(2,1)} collective-permute-done((bf16[128,2048]{1,0:T(8,128)(2,1)}, bf16[128,2048]{1,0:T(8,128)(2,1)}, u32[]{:S(2)}, u32[]{:S(2)}) %collective-permute-start.30) | collective-permute-done | bytes 524320 | tf_op jit(solution)/shard_map/ppermute | solution.py:108
  743.4 105.6 %all-reduce.10.cloned.1.call-done = (bf16[2048,512]{0,1:T(8,128)(2,1)}, bf16[1024,256]{1,0:T(8,128)(2,1)}) async-done(((bf16[2048,512]{0,1:T(8,128)(2,1)}, bf16[1024,256]{1,0:T(8,128)(2,1)}), (bf16[2048,512]{0,1:T(8,128)(2,1)}, bf16[1024,256]{1,0:T(8,128)(2,1)})) %all-reduce.10.cloned.1.call-update) | async-done | bytes 2621456 | tf_op jit(solution)/shard_map/psum | solution.py:451
  (537 shorter events, 424.5 us)
Async XLA Ops:
  7.2 42.9 %all-gather.3.cloned.1.call-start = ((), (), s32[]{:S(2)}) async-start(), calls=%async_computation.15 | async-start | bytes 4718592 | tf_op jit(solution)/shard_map/all_gather | solution.py:223
  10.7 154.8 %reduce-scatter.2.cloned.1.call-start = ((), (), s32[]{:S(2)}) async-start(), calls=%async_computation.16 | async-start | bytes 4718592 | tf_op jit(solution)/shard_map/reduce_scatter | solution.py:273
  199.4 35.8 %all-to-all-start = ((bf16[8,136,1024]{2,1,0:T(8,128)(2,1)}), bf16[8,136,1024]{2,1,0:T(8,128)(2,1)}, u32[]{:S(2)}, u32[]{:S(2)}) async-start(bf16[8,136,1024]{2,1,0:T(8,128)(2,1)} %bitcast.429), calls=%async_computation.1 | async-start | bytes 4456448 | tf_op jit(solution)/shard_map/all_to_all | solution.py:67
  205.2 26.2 %collective-permute-start.7 = (bf16[128,1024]{1,0:T(8,128)(2,1)}, bf16[128,1024]{1,0:T(8,128)(2,1)S(1)}, u32[]{:S(2)}, u32[]{:S(2)}) collective-permute-start(bf16[128,1024]{1,0:T(8,128)(2,1)} %get-tuple-element.590), channel_id=1, source_target_pairs={{0,16},{8,24},{16,0},{24,8},{1,17},{9,25},{17,1},{25,9},{2,18},{10... | collective-permute-start | bytes 786440 | tf_op jit(solution)/shard_map/ppermute | solution.py:72
  235.2 34.5 %all-to-all-start.1 = ((bf16[8,136,1024]{2,1,0:T(8,128)(2,1)}), bf16[8,136,1024]{2,1,0:T(8,128)(2,1)}, u32[]{:S(2)}, u32[]{:S(2)}) async-start(bf16[8,136,1024]{2,1,0:T(8,128)(2,1)} %bitcast.425), calls=%async_computation.2 | async-start | bytes 4456448 | tf_op jit(solution)/shard_map/all_to_all | solution.py:67
  243.3 32.5 %collective-permute-start.11 = (bf16[128,1024]{1,0:T(8,128)(2,1)}, bf16[128,1024]{1,0:T(8,128)(2,1)}, u32[]{:S(2)}, u32[]{:S(2)}) collective-permute-start(bf16[128,1024]{1,0:T(8,128)(2,1)} %get-tuple-element.588), channel_id=1, source_target_pairs={{0,24},{8,0},{16,8},{24,16},{1,25},{9,1},{17,9},{25,17},{2,26},{10... | collective-permute-start | bytes 786440 | tf_op jit(solution)/shard_map/ppermute | solution.py:72
  245.4 42.7 %collective-permute-start.10 = (bf16[128,1024]{1,0:T(8,128)(2,1)}, bf16[128,1024]{1,0:T(8,128)(2,1)}, u32[]{:S(2)}, u32[]{:S(2)}) collective-permute-start(bf16[128,1024]{1,0:T(8,128)(2,1)} %get-tuple-element.588), channel_id=1, source_target_pairs={{0,16},{8,24},{16,0},{24,8},{1,17},{9,25},{17,1},{25,9},{2,18},{10... | collective-permute-start | bytes 786440 | tf_op jit(solution)/shard_map/ppermute | solution.py:72
  251.2 36.9 %collective-permute-start.9 = (bf16[128,1024]{1,0:T(8,128)(2,1)}, bf16[128,1024]{1,0:T(8,128)(2,1)}, u32[]{:S(2)}, u32[]{:S(2)}) collective-permute-start(bf16[128,1024]{1,0:T(8,128)(2,1)} %get-tuple-element.588), channel_id=1, source_target_pairs={{0,8},{8,16},{16,24},{24,0},{1,9},{9,17},{17,25},{25,1},{2,10},{10... | collective-permute-start | bytes 786440 | tf_op jit(solution)/shard_map/ppermute | solution.py:72
  269.7 34.9 %all-to-all-start.4 = ((bf16[8,136,1024]{2,1,0:T(8,128)(2,1)}), bf16[8,136,1024]{2,1,0:T(8,128)(2,1)}, u32[]{:S(2)}, u32[]{:S(2)}) async-start(bf16[8,136,1024]{2,1,0:T(8,128)(2,1)} %bitcast.426), calls=%async_computation.5 | async-start | bytes 4456448 | tf_op jit(solution)/shard_map/all_to_all | solution.py:67
  304.6 29.7 %all-to-all-start.3 = ((bf16[8,136,1024]{2,1,0:T(8,128)(2,1)}), bf16[8,136,1024]{2,1,0:T(8,128)(2,1)}, u32[]{:S(2)}, u32[]{:S(2)}) async-start(bf16[8,136,1024]{2,1,0:T(8,128)(2,1)} %bitcast.428), calls=%async_computation.4 | async-start | bytes 4456448 | tf_op jit(solution)/shard_map/all_to_all | solution.py:67
  369.0 28.8 %all-to-all-start.6 = ((bf16[8,136,1024]{2,1,0:T(8,128)(2,1)}), bf16[8,136,1024]{2,1,0:T(8,128)(2,1)S(1)}, u32[]{:S(2)}, u32[]{:S(2)}) async-start(bf16[8,136,1024]{2,1,0:T(8,128)(2,1)} %bitcast.427), calls=%async_computation.7 | async-start | bytes 4456448 | tf_op jit(solution)/shard_map/all_to_all | solution.py:67
  397.8 32.4 %all-to-all-start.5 = ((bf16[8,136,1024]{2,1,0:T(8,128)(2,1)}), bf16[8,136,1024]{2,1,0:T(8,128)(2,1)}, u32[]{:S(2)}, u32[]{:S(2)}) async-start(bf16[8,136,1024]{2,1,0:T(8,128)(2,1)} %bitcast.37), calls=%async_computation.6 | async-start | bytes 4456448 | tf_op jit(solution)/shard_map/all_to_all | solution.py:67
  405.7 101.9 %all-gather.5.cloned.1.call-start = ((), (), s32[]{:S(2)}) async-start(), calls=%async_computation.17 | async-start | bytes 4718592 | tf_op jit(solution)/shard_map/all_gather | solution.py:378
  409.1 33.8 %collective-permute-start.18 = (bf16[128,1024]{1,0:T(8,128)(2,1)}, bf16[128,1024]{1,0:T(8,128)(2,1)S(1)}, u32[]{:S(2)}, u32[]{:S(2)}) collective-permute-start(bf16[128,1024]{1,0:T(8,128)(2,1)} %get-tuple-element.583), channel_id=1, source_target_pairs={{0,24},{8,0},{16,8},{24,16},{1,25},{9,1},{17,9},{25,17},{2,26},{10... | collective-permute-start | bytes 786440 | tf_op jit(solution)/shard_map/ppermute | solution.py:72
  409.1 37.1 %collective-permute-start.20 = (bf16[128,1024]{1,0:T(8,128)(2,1)S(1)}, bf16[128,1024]{1,0:T(8,128)(2,1)S(1)}, u32[]{:S(2)}, u32[]{:S(2)}) collective-permute-start(bf16[128,1024]{1,0:T(8,128)(2,1)S(1)} %get-tuple-element.584), channel_id=1, source_target_pairs={{0,8},{8,16},{16,24},{24,0},{1,9},{9,17},{17,25},{25,1},{2,10},{10... | collective-permute-start | bytes 786440 | tf_op jit(solution)/shard_map/ppermute | solution.py:72
  418.4 28.6 %collective-permute-start.19 = (bf16[128,1024]{1,0:T(8,128)(2,1)S(1)}, bf16[128,1024]{1,0:T(8,128)(2,1)}, u32[]{:S(2)}, u32[]{:S(2)}) collective-permute-start(bf16[128,1024]{1,0:T(8,128)(2,1)S(1)} %get-tuple-element.585), channel_id=1, source_target_pairs={{0,16},{8,24},{16,0},{24,8},{1,17},{9,25},{17,1},{25,9},{2,18},{10... | collective-permute-start | bytes 786440 | tf_op jit(solution)/shard_map/ppermute | solution.py:72
  485.4 83.0 %all-to-all-start.12 = ((f32[4,66,128]{2,1,0:T(8,128)}), f32[4,66,128]{2,1,0:T(8,128)S(1)}, u32[]{:S(2)}, u32[]{:S(2)}) async-start(f32[4,66,128]{2,1,0:T(8,128)} %broadcast_in_dim.219), calls=%async_computation.13 | async-start | bytes 294912 | tf_op jit(solution)/shard_map/all_to_all | solution.py:84
  602.4 116.4 %all-to-all-start.8 = ((bf16[8,136,2048]{2,1,0:T(8,128)(2,1)}), bf16[8,136,2048]{2,1,0:T(8,128)(2,1)}, u32[]{:S(2)}, u32[]{:S(2)}) async-start(bf16[8,136,2048]{2,1,0:T(8,128)(2,1)} %bitcast.423), calls=%async_computation.9 | async-start | bytes 8912896 | tf_op jit(solution)/shard_map/all_to_all | solution.py:67
  608.8 95.1 %all-reduce.8.cloned.1.call-start = ((), (), s32[]{:S(2)}) async-start(), calls=%async_computation.18 | async-start | bytes 4194304 | tf_op jit(solution)/shard_map/psum | solution.py:381
  615.8 233.1 %all-reduce.10.cloned.1.call-start = ((), (), s32[]{:S(2)}) async-start(), calls=%async_computation.19 | async-start | bytes 5242880 | tf_op jit(solution)/shard_map/psum | solution.py:451
  624.1 83.8 %collective-permute-start.27 = (bf16[4,128,2048]{2,1,0:T(8,128)(2,1)}, bf16[4,128,2048]{2,1,0:T(8,128)(2,1)}, u32[]{:S(2)}, u32[]{:S(2)}) collective-permute-start(bf16[4,128,2048]{2,1,0:T(8,128)(2,1)} %convolution_convert_fusion.7), channel_id=1, source_target_pairs={{0,1},{1,0},{2,3},{3,2},{4,5},{5,4},{6,7},{7,6},{8,9},{9,8},{10,11... | collective-permute-start | bytes 6291464 | tf_op jit(solution)/shard_map/ppermute | solution.py:108
  725.6 124.1 %collective-permute-start.24 = (bf16[128,2048]{1,0:T(8,128)(2,1)}, bf16[128,2048]{1,0:T(8,128)(2,1)}, u32[]{:S(2)}, u32[]{:S(2)}) collective-permute-start(bf16[128,2048]{1,0:T(8,128)(2,1)} %get-tuple-element.573), channel_id=1, source_target_pairs={{0,24},{8,0},{16,8},{24,16},{1,25},{9,1},{17,9},{25,17},{2,26},{10... | collective-permute-start | bytes 1572872 | tf_op jit(solution)/shard_map/ppermute | solution.py:72
  726.9 122.8 %collective-permute-start.26 = (bf16[128,2048]{1,0:T(8,128)(2,1)}, bf16[128,2048]{1,0:T(8,128)(2,1)}, u32[]{:S(2)}, u32[]{:S(2)}) collective-permute-start(bf16[128,2048]{1,0:T(8,128)(2,1)} %get-tuple-element.574), channel_id=1, source_target_pairs={{0,8},{8,16},{16,24},{24,0},{1,9},{9,17},{17,25},{25,1},{2,10},{10... | collective-permute-start | bytes 1572872 | tf_op jit(solution)/shard_map/ppermute | solution.py:72
  729.3 120.4 %collective-permute-start.25 = (bf16[128,2048]{1,0:T(8,128)(2,1)}, bf16[128,2048]{1,0:T(8,128)(2,1)}, u32[]{:S(2)}, u32[]{:S(2)}) collective-permute-start(bf16[128,2048]{1,0:T(8,128)(2,1)} %get-tuple-element.575), channel_id=1, source_target_pairs={{0,16},{8,24},{16,0},{24,8},{1,17},{9,25},{17,1},{25,9},{2,18},{10... | collective-permute-start | bytes 1572872 | tf_op jit(solution)/shard_map/ppermute | solution.py:72
  (151 other events, 2532.2 us)
Sparse Core Ops, SparseCore 0:
  10.8 39.2 all-gather.2
  114.5 50.8 reduce-scatter.1
  467.1 40.4 all-gather.4
  616.0 87.8 all-reduce.7
  708.1 140.8 all-reduce.9

commit v2 on v1

v2 whole, which is shorter than its diff:
```python
import functools

import jax
import jax.numpy as jnp
from jax import lax
from jax.experimental import pallas as pl
from jax.experimental.pallas import tpu as pltpu
from jax.sharding import PartitionSpec as P

eps_norm = 1e-06
rope_base = 1000000.0
highest = lax.Precision.HIGHEST
chunk_count = 2
block_slots = 256
expert_steps = 4
expert_vmem = 48 * 1024 * 1024
kernel_vmem = 40 * 1024 * 1024


def rms_scale(values, norm_gain):
    return (
        values * lax.rsqrt(jnp.mean(values * values, axis=-1, keepdims=True) + eps_norm) * norm_gain
    )


def rope_tables(positions, head_dim):
    half_dim = head_dim // 2
    inverse = rope_base ** (-(jnp.arange(half_dim, dtype=jnp.float32) * 2.0 / head_dim))
    angles = positions.astype(jnp.float32)[:, None] * inverse[None, :]
    cosine = jnp.cos(angles)
    sine = jnp.sin(angles)
    return (jnp.concatenate([cosine, cosine], axis=1), jnp.concatenate([-sine, sine], axis=1))


def slot_positions(ends, slot_count):
    slot_ids = jnp.arange(slot_count, dtype=jnp.int32)
    starts = row_starts(slot_ids, [ends[k] for k in range(ends.shape[0])])
    return slot_ids - starts


def row_starts(row_ids, ends):
    starts = jnp.zeros_like(row_ids)
    for end in ends:
        starts = jnp.where(row_ids >= end, end, starts)
    return jnp.where(row_ids >= ends[-1], row_ids, starts)


def lanes_dot(left, right):
    return lax.dot_general(
        left, right, (((1,), (1,)), ((), ())), preferred_element_type=jnp.float32
    )


def turn_halves(values):
    return pltpu.roll(values, values.shape[-1] // 2, axis=1)


def attend_kernel(
    ends_ref,
    rows_ref,
    query_w_ref,
    kv_w_ref,
    out_w_ref,
    query_gain_ref,
    key_gain_ref,
    cosine_ref,
    sine_ref,
    partial_ref,
    query_ref,
    key_ref,
    value_ref,
    heads_ref,
    log_ref,
    scale_ref,
    keys,
    values,
    total,
    sums,
    *,
    head_dim,
):
    step = pl.program_id(0)
    block = rows_ref.shape[0]
    heads = query_w_ref.shape[1] // head_dim
    ends = [ends_ref[k] for k in range(ends_ref.shape[0])]
    softmax_scale = head_dim ** (-0.5)
    rows = rows_ref[...]
    query_pre = jnp.dot(rows, query_w_ref[...], preferred_element_type=jnp.float32)
    kv_pre = jnp.dot(rows, kv_w_ref[...], preferred_element_type=jnp.float32)
    cosine = cosine_ref[...]
    sine = sine_ref[...]
    lanes = lax.broadcasted_iota(jnp.int32, (block, head_dim), 1)
    scales = jnp.zeros((block, head_dim), jnp.float32)

    def prep(vectors, gain):
        scale = lax.rsqrt(jnp.mean(vectors * vectors, axis=-1, keepdims=True) + eps_norm)
        gained = vectors * scale * gain
        return (gained * cosine + turn_halves(gained) * sine).astype(jnp.bfloat16), scale

    stacked = []
    for h in range(heads):
        cut = slice(h * head_dim, (h + 1) * head_dim)
        low, scale = prep(query_pre[:, cut], query_gain_ref[...])
        query_ref[:, cut] = low
        stacked.append(low)
        scales = jnp.where(lanes == h, scale, scales)
    key_low, scale = prep(kv_pre[:, :head_dim], key_gain_ref[...])
    scale_ref[...] = jnp.where(lanes == heads, scale, scales)
    value_low = kv_pre[:, head_dim:].astype(jnp.bfloat16)
    key_ref[...] = key_low
    value_ref[...] = value_low
    own = pl.ds(pl.multiple_of(step * block, block), block)
    keys[own, :] = key_low
    values[own, :head_dim] = value_low
    values[own, head_dim:] = jnp.ones((block, head_dim), jnp.bfloat16)
    queries = jnp.concatenate(stacked, axis=0)
    row_ids = step * block + lax.broadcasted_iota(jnp.int32, (block, 1), 0)
    starts = row_starts(row_ids, ends)
    total[...] = jnp.zeros_like(total)
    sums[...] = jnp.zeros_like(sums)
    ones = jnp.ones((8, block), jnp.bfloat16)

    def one_block(j, carry):
        there = pl.ds(pl.multiple_of(j * block, block), block)
        scores = lanes_dot(queries, keys[there, :]) * softmax_scale
        column_ids = j * block + lax.broadcasted_iota(jnp.int32, (block, block), 1)
        allowed = (column_ids <= row_ids) & (column_ids >= starts)
        weights = jnp.concatenate(
            [
                jnp.where(allowed, jnp.exp(scores[h * block : (h + 1) * block]), 0.0).astype(
                    jnp.bfloat16
                )
                for h in range(heads)
            ],
            axis=0,
        )
        total[...] += jnp.dot(weights, values[there, :], preferred_element_type=jnp.float32)
        sums[...] += lanes_dot(ones, weights)
        return carry

    first = row_starts(step * block, ends) // block
    lax.fori_loop(first, step + 1, one_block, 0)
    log_ref[0] = jnp.log(sums[...])
    outs = (total[:, :head_dim] / total[:, head_dim:]).astype(jnp.bfloat16)
    for h in range(heads):
        heads_ref[:, h * head_dim : (h + 1) * head_dim] = outs[h * block : (h + 1) * block]
    partial_ref[...] = jnp.dot(
        heads_ref[...], out_w_ref[...], preferred_element_type=jnp.float32
    ).astype(jnp.bfloat16)


def attend_rows(ends, rows, w_query, w_kv, w_out, q_gain, k_gain, cosine, sine):
    slots, width = rows.shape
    head_dim = q_gain.shape[0]
    head_width = w_query.shape[1]
    heads = head_width // head_dim
    block = min(block_slots, slots)
    count = slots // block

    def tile(columns):
        return pl.BlockSpec((block, columns), lambda i: (i, 0))

    def whole(array):
        return pl.BlockSpec(array.shape, lambda i: (0, 0))

    shape = pltpu.HBM
    q_gain = q_gain[None]
    k_gain = k_gain[None]
    return pl.pallas_call(
        functools.partial(attend_kernel, head_dim=head_dim),
        grid=(count,),
        in_specs=[
            pl.BlockSpec(memory_space=pltpu.SMEM),
            tile(width),
            whole(w_query),
            whole(w_kv),
            whole(w_out),
            whole(q_gain),
            whole(k_gain),
            tile(head_dim),
            tile(head_dim),
        ],
        out_specs=[
            tile(width),
            tile(head_width),
            tile(head_dim),
            tile(head_dim),
            tile(head_width),
            pl.BlockSpec((1, 8, heads * block), lambda i: (i, 0, 0)),
            tile(head_dim),
        ],
        out_shape=[
            shape((slots, width), jnp.bfloat16),
            shape((slots, head_width), jnp.bfloat16),
            shape((slots, head_dim), jnp.bfloat16),
            shape((slots, head_dim), jnp.bfloat16),
            shape((slots, head_width), jnp.bfloat16),
            shape((count, 8, heads * block), jnp.float32),
            shape((slots, head_dim), jnp.float32),
        ],
        scratch_shapes=[
            pltpu.VMEM((slots, head_dim), jnp.bfloat16),
            pltpu.VMEM((slots, 2 * head_dim), jnp.bfloat16),
            pltpu.VMEM((heads * block, 2 * head_dim), jnp.float32),
            pltpu.VMEM((8, heads * block), jnp.float32),
        ],
        compiler_params=pltpu.CompilerParams(vmem_limit_bytes=kernel_vmem),
        cost_estimate=pl.CostEstimate(
            flops=2 * slots * width * (2 * head_width + 2 * head_dim)
            + 3 * slots * slots * head_width,
            bytes_accessed=4 * slots * width + 4 * width * head_width,
            transcendentals=slots * slots * heads // 2,
        ),
        name="attend_rows",
    )(ends, rows, w_query, w_kv, w_out, q_gain, k_gain, cosine, sine)


def attend_back_kernel(
    ends_ref,
    grad_ref,
    out_w_ref,
    query_ref,
    heads_ref,
    key_ref,
    value_ref,
    log_ref,
    scale_ref,
    query_gain_ref,
    key_gain_ref,
    cosine_ref,
    sine_ref,
    grad_query_ref,
    grad_kv_ref,
    grad_query_gain_ref,
    grad_key_gain_ref,
    grad_keys,
    grad_values,
    grad_queries,
    *,
    head_dim,
):
    step = pl.program_id(0)
    block = query_ref.shape[0]
    heads = query_ref.shape[1] // head_dim
    ends = [ends_ref[k] for k in range(ends_ref.shape[0])]
    softmax_scale = head_dim ** (-0.5)

    @pl.when(step == 0)
    def _():
        grad_keys[...] = jnp.zeros_like(grad_keys)
        grad_values[...] = jnp.zeros_like(grad_values)
        grad_query_gain_ref[...] = jnp.zeros_like(grad_query_gain_ref)

    grad_heads = lanes_dot(grad_ref[...], out_w_ref[...]).astype(jnp.bfloat16)
    query = query_ref[...]
    out = heads_ref[...]
    cuts = [slice(h * head_dim, (h + 1) * head_dim) for h in range(heads)]
    queries = jnp.concatenate([query[:, cut] for cut in cuts], axis=0)
    grads = jnp.concatenate([grad_heads[:, cut] for cut in cuts], axis=0)
    outs = jnp.concatenate([out[:, cut] for cut in cuts], axis=0)
    products = grads.astype(jnp.float32) * outs.astype(jnp.float32)
    high = products.astype(jnp.bfloat16)
    rest = (products - high.astype(jnp.float32)).astype(jnp.bfloat16)
    ones = jnp.ones((8, head_dim), jnp.bfloat16)
    centre = (lanes_dot(ones, high) + lanes_dot(ones, rest))[:1]
    logs = log_ref[0, :1, :]
    column_ids = step * block + lax.broadcasted_iota(jnp.int32, (1, block), 1)
    starts = row_starts(column_ids, ends)
    grad_queries[...] = jnp.zeros_like(grad_queries)

    def one_block(j, carry):
        there = pl.ds(pl.multiple_of(j * block, block), block)
        key = key_ref[there, :]
        value = value_ref[there, :]
        scores = lanes_dot(key, queries) * softmax_scale - logs
        grad_probs = lanes_dot(value, grads) - centre
        row_ids = j * block + lax.broadcasted_iota(jnp.int32, (block, block), 0)
        allowed = (row_ids <= column_ids) & (row_ids >= starts)
        probs = jnp.concatenate(
            [
                jnp.where(allowed, jnp.exp(scores[:, h * block : (h + 1) * block]), 0.0)
                for h in range(heads)
            ],
            axis=1,
        )
        probs_low = probs.astype(jnp.bfloat16)
        grad_scores = (probs * grad_probs).astype(jnp.bfloat16)
        grad_values[there, :] += jnp.dot(probs_low, grads, preferred_element_type=jnp.float32)
        grad_keys[there, :] += jnp.dot(grad_scores, queries, preferred_element_type=jnp.float32)
        grad_queries[...] += lax.dot_general(
            grad_scores, key, (((0,), (0,)), ((), ())), preferred_element_type=jnp.float32
        )
        return carry

    first = row_starts(step * block, ends) // block
    lax.fori_loop(first, step + 1, one_block, 0)

    def prep_back(grad, low, gain, cosine, sine, scale):
        grad = grad * softmax_scale
        low = low.astype(jnp.float32)
        grad_gained = grad * cosine - turn_halves(grad) * sine
        normed = (low * cosine - turn_halves(low) * sine) / gain
        grad_gain = jnp.sum(grad_gained * normed, axis=0, keepdims=True)
        grad_normed = grad_gained * gain
        mean = jnp.mean(grad_normed * normed, axis=-1, keepdims=True)
        return scale * (grad_normed - normed * mean), grad_gain

    own = pl.ds(pl.multiple_of(step * block, block), block)
    cosine = cosine_ref[own, :]
    sine = sine_ref[own, :]
    scales = scale_ref[own, :]
    for h, cut in enumerate(cuts):
        grad_pre, grad_gain = prep_back(
            grad_queries[h * block : (h + 1) * block, :],
            query[:, cut],
            query_gain_ref[...],
            cosine,
            sine,
            scales[:, h : h + 1],
        )
        grad_query_ref[:, cut] = grad_pre.astype(jnp.bfloat16)
        grad_query_gain_ref[...] += grad_gain

    @pl.when(step == pl.num_programs(0) - 1)
    def _():
        grad_pre, grad_gain = prep_back(
            grad_keys[...],
            key_ref[...],
            key_gain_ref[...],
            cosine_ref[...],
            sine_ref[...],
            scale_ref[:, heads : heads + 1],
        )
        grad_kv_ref[:, :head_dim] = grad_pre.astype(jnp.bfloat16)
        grad_kv_ref[:, head_dim:] = grad_values[...].astype(jnp.bfloat16)
        grad_key_gain_ref[...] = grad_gain


def attend_rows_back(
    ends, grad, w_out, query, heads_low, key, value, logs, scales, q_gain, k_gain, cosine, sine
):
    slots, width = grad.shape
    head_dim = q_gain.shape[0]
    head_width = query.shape[1]
    heads = head_width // head_dim
    block = min(block_slots, slots)
    count = slots // block

    def tile(columns):
        return pl.BlockSpec((block, columns), lambda i: (i, 0))

    def whole(array):
        return pl.BlockSpec(array.shape, lambda i: (0, 0))

    shape = pltpu.HBM
    q_gain = q_gain[None]
    k_gain = k_gain[None]
    return pl.pallas_call(
        functools.partial(attend_back_kernel, head_dim=head_dim),
        grid=(count,),
        in_specs=[
            pl.BlockSpec(memory_space=pltpu.SMEM),
            tile(width),
            whole(w_out),
            tile(head_width),
            tile(head_width),
            whole(key),
            whole(value),
            pl.BlockSpec((1, 8, heads * block), lambda i: (i, 0, 0)),
            whole(scales),
            whole(q_gain),
            whole(k_gain),
            whole(cosine),
            whole(sine),
        ],
        out_specs=[
            tile(head_width),
            pl.BlockSpec((slots, 2 * head_dim), lambda i: (0, 0)),
            pl.BlockSpec((1, head_dim), lambda i: (0, 0)),
            pl.BlockSpec((1, head_dim), lambda i: (0, 0)),
        ],
        out_shape=[
            shape((slots, head_width), jnp.bfloat16),
            shape((slots, 2 * head_dim), jnp.bfloat16),
            shape((1, head_dim), jnp.float32),
            shape((1, head_dim), jnp.float32),
        ],
        scratch_shapes=[
            pltpu.VMEM((slots, head_dim), jnp.float32),
            pltpu.VMEM((slots, head_dim), jnp.float32),
            pltpu.VMEM((heads * block, head_dim), jnp.float32),
        ],
        compiler_params=pltpu.CompilerParams(vmem_limit_bytes=kernel_vmem),
        cost_estimate=pl.CostEstimate(
            flops=2 * slots * width * head_width + 6 * slots * slots * head_width,
            bytes_accessed=2 * slots * width + 2 * width * head_width,
            transcendentals=slots * slots * heads // 2,
        ),
        name="attend_rows_back",
    )(ends, grad, w_out, query, heads_low, key, value, logs, scales, q_gain, k_gain, cosine, sine)


def transposed_times(left, right):
    return lax.dot_general(
        left, right, (((0,), (0,)), ((), ())), preferred_element_type=jnp.float32
    )


plane_axes = ("row", "col")


def move_plane(parts):
    return lax.all_to_all(parts, plane_axes, split_axis=0, concat_axis=0, tiled=True)


def rotate(block, axis, step):
    size = lax.axis_size(axis)
    return lax.ppermute(block, axis, [(i, (i + step) % size) for i in range(size)])


def gather_planes(block):
    planes = lax.axis_size("expert")
    return jnp.stack([block] + [rotate(block, "expert", k) for k in range(1, planes)], axis=0)


def return_planes(parts):
    return [parts[0]] + [rotate(parts[k], "expert", -k) for k in range(1, parts.shape[0])]


def together(*values):
    return lax.optimization_barrier(values)


def move_all(parts):
    return lax.all_to_all(
        parts, ("expert",) + plane_axes, split_axis=0, concat_axis=0, tiled=True
    )


def sum_all(values):
    devices = lax.axis_size(("expert",) + plane_axes)
    padded = jnp.pad(values, (0, -values.shape[0] % (devices * 128)))
    total = jnp.sum(move_all(padded.reshape(devices, -1, 128)), axis=0)
    return move_all(jnp.broadcast_to(total[None], (devices,) + total.shape)).reshape(-1)


def line_step(value, step, hop):
    planes = lax.axis_size("expert")
    if hop > 0:
        pairs = [(i, i + 1) for i in range(*step)]
    else:
        pairs = [(planes - 1 - i, planes - 2 - i) for i in range(*step)]
    return lax.ppermute(value, "expert", pairs)


def sum_planes(product):
    planes = lax.axis_size("expert")
    plane = lax.axis_index("expert")
    shares = product.reshape(planes, -1, product.shape[1])

    def share(k):
        return lax.dynamic_index_in_dim(shares, (plane + k) % planes, 0, keepdims=False)

    arrived = [rotate(share(k), "expert", k) for k in range(1, planes)]
    total = share(0).astype(jnp.float32)
    for part in arrived:
        total = total + part.astype(jnp.float32)
    return total.astype(product.dtype)


def spread_planes(total):
    planes = lax.axis_size("expert")
    arrived = []
    for hop in (1, -1):
        message = total
        for k in range(1, planes):
            message = line_step(message, (k - 1, planes - 1), hop)
            arrived.append((k, hop, message))
    arrived.sort(key=lambda entry: -entry[0])
    return [message for _, _, message in arrived] + [total]


def in_plane_order(parts):
    planes = lax.axis_size("expert")
    plane = lax.axis_index("expert")
    rows = parts[0].shape[0]
    result = jnp.zeros((planes * rows, parts[0].shape[1]), jnp.float32)
    places = [plane - hop * k for k in range(planes - 1, 0, -1) for hop in (1, -1)] + [plane]
    for place, part in zip(places, parts):
        result = lax.dynamic_update_slice_in_dim(
            result, part.astype(jnp.float32), jnp.clip(place, 0, planes - 1) * rows, axis=0
        )
    return result


def scatter_cols(product):
    col = lax.axis_index("col")
    cols = lax.axis_size("col")
    moved = [rotate(product((col + k) % cols).astype(jnp.bfloat16), "col", k) for k in range(1, cols)]
    total = product(col)
    for part in moved:
        total = total + part.astype(jnp.float32)
    return total.astype(jnp.bfloat16)


def scatter_rows(parts):
    row = lax.axis_index("row")
    rows = lax.axis_size("row")

    def piece(k):
        return lax.dynamic_index_in_dim(parts, (row + k) % rows, 0, keepdims=False)

    arrived = [rotate(piece(k), "row", k) for k in range(1, rows)]
    result = piece(0).astype(jnp.float32)
    for part in arrived:
        result = result + part.astype(jnp.float32)
    return result


def expert_kernel(ids_ref, router_ref, gate_ref, up_ref, down_ref, *refs, count, experts):
    rows_refs = refs[:count]
    grads_refs = refs[count : 2 * count]
    sends = refs[2 * count : 3 * count]
    weighted = refs[3 * count : 4 * count]
    rows_out, grads_out, hidden_out, grad_gate_out, grad_up_out = refs[4 * count :]
    width = rows_refs[1].shape[1]
    cuts = [slice(i * width, (i + 1) * width) for i in range(count)]
    rows = [ref[...] for ref in rows_refs]
    chosen = grads_refs[0][:, width:].astype(jnp.float32) > 0.5
    lanes = lax.broadcasted_iota(jnp.int32, chosen.shape, 1)

    def times(weights_ref):
        return sum(
            jnp.dot(part, weights_ref[cut, :], preferred_element_type=jnp.float32)
            for part, cut in zip(rows, cuts)
        )

    logits = times(router_ref)
    top = jnp.max(jnp.where(chosen, logits, -3e38), axis=1, keepdims=True)
    raised = jnp.where(chosen, jnp.exp(jnp.where(chosen, logits - top, 0.0)), 0.0)
    own = jnp.sum(jnp.where(lanes == ids_ref[0], raised, 0.0), axis=1, keepdims=True)
    gates = own / jnp.maximum(jnp.sum(raised, axis=1, keepdims=True), 1e-30)
    gate_pre = times(gate_ref)
    up_pre = times(up_ref)
    sigmoid = 1.0 / (1.0 + jnp.exp(-gate_pre))
    silu = gate_pre * sigmoid
    hidden = (silu * up_pre).astype(jnp.bfloat16)
    hidden_out[...] = hidden
    dots = jnp.zeros(gates.shape, jnp.float32)
    grad_hidden = jnp.zeros(gate_pre.shape, jnp.float32)
    for i, cut in enumerate(cuts):
        out = jnp.dot(hidden, down_ref[:, cut], preferred_element_type=jnp.float32)
        out = out.astype(jnp.bfloat16).astype(jnp.float32)
        grads = grads_refs[i][:, :width].astype(jnp.float32)
        dots = dots + jnp.sum(out * grads, axis=1, keepdims=True)
        weighted[i][...] = (out * gates).astype(jnp.bfloat16)
        grads_low = (grads * gates).astype(jnp.bfloat16)
        grads_out[:, cut] = grads_low
        rows_out[:, cut] = rows[i]
        grad_hidden = grad_hidden + lanes_dot(grads_low, down_ref[:, cut])
    grad_gate = (grad_hidden * up_pre * sigmoid * (1.0 + gate_pre * (1.0 - sigmoid))).astype(
        jnp.bfloat16
    )
    grad_up = (grad_hidden * silu).astype(jnp.bfloat16)
    grad_gate_out[...] = grad_gate
    grad_up_out[...] = grad_up
    for i, cut in enumerate(cuts):
        sends[i][:, :width] = (
            lanes_dot(grad_gate, gate_ref[cut, :]) + lanes_dot(grad_up, up_ref[cut, :])
        ).astype(jnp.bfloat16)
    dots_high = dots.astype(jnp.bfloat16).astype(jnp.float32)
    side = jnp.where(lanes == ids_ref[1], dots_high, 0.0) + jnp.where(
        lanes == ids_ref[1] + experts, dots - dots_high, 0.0
    )
    sends[0][:, width:] = side.astype(jnp.bfloat16)


def expert_rows(ids, w_router, w_gate, w_up, w_down, rows, grads, plane_size):
    count = len(rows)
    slots, width = rows[0].shape
    model_width, hidden = w_gate.shape
    side = grads[0].shape[1] - width
    block = slots // expert_steps

    def tile(columns):
        return pl.BlockSpec((block, columns), lambda i: (i, 0))

    def whole(array):
        return pl.BlockSpec(array.shape, lambda i: (0, 0), pipeline_mode=pl.Buffered(1))

    def shape(columns):
        return pltpu.HBM((slots, columns), jnp.bfloat16)

    sides = [width + side] + [width] * (count - 1)
    outs = sides + [width] * count + [model_width, model_width, hidden, hidden, hidden]
    flops = 2 * slots * model_width * hidden * 6
    return pl.pallas_call(
        functools.partial(expert_kernel, count=count, experts=plane_size),
        grid=(expert_steps,),
        in_specs=[pl.BlockSpec(memory_space=pltpu.SMEM)]
        + [whole(array) for array in (w_router, w_gate, w_up, w_down)]
        + [tile(width)] * count
        + [tile(columns) for columns in sides],
        out_specs=[tile(columns) for columns in outs],
        out_shape=[shape(columns) for columns in outs],
        compiler_params=pltpu.CompilerParams(vmem_limit_bytes=expert_vmem),
        cost_estimate=pl.CostEstimate(
            flops=flops, bytes_accessed=6 * model_width * hidden, transcendentals=slots * hidden
        ),
        name="expert_rows",
    )(ids, w_router, w_gate, w_up, w_down, *rows, *grads)


def local(
    layer_input,
    norm_attn,
    w_query,
    w_key,
    w_value,
    q_gain,
    k_gain,
    w_out,
    norm_moe,
    w_router,
    w_gate,
    w_up,
    w_down,
    seq_lengths,
    routes,
    out_grad,
):
    tok_dev = layer_input.shape[0]
    model_width = layer_input.shape[1]
    group_tok = tok_dev * lax.axis_size(("row", "col"))
    head_dim = q_gain.shape[0]
    experts = w_router.shape[1]
    top_count = routes.shape[1]
    capacity = tok_dev * top_count * 17 // (16 * experts)
    planes = lax.axis_size("expert")
    plane_size = lax.axis_size(plane_axes)
    plane_index = lax.axis_index("expert")
    plane_cap = planes * capacity
    chosen_here = jnp.any(
        routes[:, :, None] == jnp.arange(experts, dtype=jnp.int32)[None, None, :], axis=1
    )
    plane_routes = gather_planes(routes.T)
    plane_experts = plane_index * plane_size + jnp.arange(plane_size, dtype=jnp.int32)
    chosen_plane = jnp.any(
        plane_routes[None] == plane_experts[:, None, None, None], axis=2
    )
    token_ids = jnp.arange(tok_dev, dtype=jnp.int32)
    earlier = (token_ids[:, None] < token_ids[None, :]).astype(jnp.bfloat16)
    slot_rank = jnp.dot(
        chosen_plane.astype(jnp.bfloat16).reshape(plane_size * planes, tok_dev),
        earlier,
        preferred_element_type=jnp.float32,
    ).astype(jnp.int32).reshape(plane_size, planes, tok_dev)
    plane_slot = jnp.where(
        chosen_plane,
        slot_rank + (jnp.arange(planes, dtype=jnp.int32) * capacity)[None, :, None],
        -1,
    ).reshape(plane_size, 1, planes * tok_dev)
    dispatch = (
        plane_slot == jnp.arange(plane_cap, dtype=jnp.int32)[None, :, None]
    ).astype(jnp.bfloat16)
    chosen_all = jnp.any(
        plane_routes[:, :, :, None] == jnp.arange(experts, dtype=jnp.int32), axis=1
    ).reshape(planes * tok_dev, experts).astype(jnp.bfloat16)

    def gather_rows(block):
        return gather_planes(block).reshape(planes * tok_dev, block.shape[1])

    def select_slots(rows_all):
        return jnp.dot(
            dispatch.reshape(plane_size * plane_cap, -1),
            rows_all,
            preferred_element_type=jnp.float32,
        ).astype(jnp.bfloat16)

    def to_plane(slot_values):
        width = slot_values.shape[1]
        moved = move_plane(slot_values.reshape(plane_size, plane_cap, width))
        return moved.reshape(plane_size * plane_cap, width)

    chunk_width = model_width // chunk_count
    chunks = [slice(i * chunk_width, (i + 1) * chunk_width) for i in range(chunk_count)]
    side_width = 128
    grad_planes = [gather_rows(out_grad[:, cut]) for cut in chunks]
    grad_planes[0] = jnp.concatenate(
        [grad_planes[0], jnp.pad(chosen_all, ((0, 0), (0, side_width - experts)))], axis=1
    )
    slot_sends = [select_slots(part) for part in grad_planes]
    def gates_of(all_logits, chosen):
        top = jnp.max(jnp.where(chosen, all_logits, -3e38), axis=1, keepdims=True)
        raised = jnp.where(chosen, jnp.exp(jnp.where(chosen, all_logits - top, 0.0)), 0.0)
        return raised / jnp.maximum(jnp.sum(raised, axis=1, keepdims=True), 1e-30)

    input_rows = layer_input.astype(jnp.float32)
    normed_one, norm_one_back = jax.vjp(rms_scale, input_rows, norm_attn)
    normed_low = normed_one.astype(jnp.bfloat16)
    group_rows = lax.all_gather(normed_low, ("row", "col"), axis=0, tiled=True)
    ends = jnp.cumsum(seq_lengths[0], dtype=jnp.int32)
    cosine_table, sine_table = rope_tables(slot_positions(ends, group_tok), head_dim)
    key_value_w = jnp.concatenate([w_key, w_value], axis=1)
    group_rows, slot_sends[0], cosine_table, sine_table, key_value_w = together(
        group_rows, slot_sends[0], cosine_table, sine_table, key_value_w
    )
    grad_slot_chunks = [to_plane(slot_sends[0])]
    attn_partial, query_low, key_low, value_low, heads_low, log_totals, head_scales = attend_rows(
        ends, group_rows, w_query, key_value_w, w_out, q_gain, k_gain, cosine_table, sine_table
    )
    attn_partial, grad_slot_chunks[0] = together(attn_partial, grad_slot_chunks[0])
    col_parts = attn_partial.reshape(-1, lax.axis_size("col"), tok_dev, model_width)
    attn_rows = scatter_rows(
        scatter_cols(lambda place: lax.dynamic_index_in_dim(col_parts, place, 1, keepdims=False))
    )
    attn_rows, *late_sends = together(attn_rows, *slot_sends[1:])
    grad_slot_chunks += [to_plane(part) for part in late_sends]
    attn_rows = attn_rows.astype(jnp.float32)
    mixed_rows = input_rows + attn_rows
    normed_two, norm_two_back = jax.vjp(rms_scale, mixed_rows, norm_moe)
    moe_input = normed_two.astype(jnp.bfloat16)
    router_logits = jnp.dot(moe_input, w_router, preferred_element_type=jnp.float32)
    source_gates = gates_of(router_logits, chosen_here)

    moe_planes = [gather_rows(moe_input[:, cut]) for cut in chunks]
    moe_sends = [select_slots(part) for part in moe_planes]
    moe_sends[0], *grad_slot_chunks[1:] = together(moe_sends[0], *grad_slot_chunks[1:])
    slot_chunks = [to_plane(part) for part in moe_sends]
    place = lax.axis_index(plane_axes)
    ids = jnp.stack([plane_index * plane_size + place, place]).astype(jnp.int32)
    expert_outs = expert_rows(
        ids,
        jnp.pad(w_router, ((0, 0), (0, side_width - experts))),
        w_gate[0],
        w_up[0],
        w_down[0],
        slot_chunks,
        grad_slot_chunks,
        plane_size,
    )
    grad_sends = expert_outs[:chunk_count]
    out_sends = expert_outs[chunk_count : 2 * chunk_count]
    moe_slots, grad_out_slots, hidden_low, grad_gate_pre, grad_up_pre = expert_outs[
        2 * chunk_count :
    ]

    def to_source(returned):
        summed = lax.dot_general(
            dispatch.reshape(plane_size * plane_cap, -1),
            returned,
            (((0,), (0,)), ((), ())),
            preferred_element_type=jnp.float32,
        ).astype(jnp.bfloat16)
        return return_planes(summed.reshape(planes, tok_dev, returned.shape[1]))

    def add_parts(parts):
        return sum(part.astype(jnp.float32) for part in parts)

    grad_rows = out_grad.astype(jnp.float32)
    grad_down = transposed_times(hidden_low, grad_out_slots)
    grad_gate = transposed_times(moe_slots, grad_gate_pre)
    grad_up = transposed_times(moe_slots, grad_up_pre)
    grad_returns = [to_plane(part) for part in grad_sends]
    grad_returns[0], grad_down = together(grad_returns[0], grad_down)
    grad_returns[-1], grad_gate, *out_sends = together(grad_returns[-1], grad_gate, *out_sends)
    out_returns = [to_plane(out_sends[0])]
    grad_parts = [to_source(part) for part in grad_returns]
    grad_parts[-1][-1], grad_up = together(grad_parts[-1][-1], grad_up)
    side_parts = jnp.stack(
        [part[:, chunk_width:].astype(jnp.float32) for part in grad_parts[0]], axis=0
    )
    dot_parts = side_parts[:, :, :plane_size] + side_parts[:, :, plane_size : 2 * plane_size]
    dot_parts = lax.dynamic_slice_in_dim(
        jnp.concatenate([dot_parts, dot_parts], axis=0), planes - plane_index, planes, axis=0
    )
    grad_gates = jnp.swapaxes(dot_parts, 0, 1).reshape(tok_dev, experts)
    grad_logits = source_gates * (
        grad_gates - jnp.sum(source_gates * grad_gates, axis=1, keepdims=True)
    )
    grad_parts[0] = [part[:, :chunk_width] for part in grad_parts[0]]
    grad_moe_input = jnp.concatenate([add_parts(parts) for parts in grad_parts], axis=1)
    grad_router = lax.dot_general(
        grad_logits,
        moe_input.astype(jnp.float32),
        (((0,), (0,)), ((), ())),
        precision=highest,
        preferred_element_type=jnp.float32,
    )
    grad_moe_input = grad_moe_input + jnp.einsum(
        "te,de->td", grad_logits, w_router, precision=highest, preferred_element_type=jnp.float32
    )
    grad_mixed_norm, grad_norm_moe = norm_two_back(grad_moe_input)
    grad_mixed = grad_rows + grad_mixed_norm
    grad_attn_low = grad_mixed.astype(jnp.bfloat16)
    grad_attn_low, out_returns[0] = together(grad_attn_low, out_returns[0])
    grad_group = lax.all_gather(grad_attn_low, ("row", "col"), axis=0, tiled=True)
    out_first = add_parts(to_source(out_returns[0]))
    grad_group, out_first, *out_late = together(grad_group, out_first, *out_sends[1:])
    out_returns += [to_plane(part) for part in out_late]
    grad_out_proj = transposed_times(heads_low, grad_group).astype(jnp.bfloat16)
    grad_out_proj, grad_group = together(grad_out_proj, grad_group)
    out_share = sum_planes(grad_out_proj)
    grad_query_low, grad_kv, grad_q_gain, grad_k_gain = attend_rows_back(
        ends,
        grad_group,
        w_out,
        query_low,
        heads_low,
        key_low,
        value_low,
        log_totals,
        head_scales,
        q_gain,
        k_gain,
        cosine_table,
        sine_table,
    )
    grad_query_low, grad_kv, out_share = together(grad_query_low, grad_kv, out_share)
    grad_query = transposed_times(group_rows, grad_query_low)
    grad_key_value = transposed_times(group_rows, grad_kv)
    norm_terms = (
        jnp.sum(grad_query * w_query.astype(jnp.float32), axis=1)
        + jnp.sum(grad_key_value * key_value_w.astype(jnp.float32), axis=1)
    ) / norm_attn
    cols = lax.axis_size("col")
    col = lax.axis_index("col")
    kv_low = grad_key_value.astype(jnp.bfloat16).reshape(cols, -1, 2 * head_dim)
    kv_part = lax.dynamic_index_in_dim(kv_low, col, 0, keepdims=False).astype(jnp.float32)
    for k in range(1, cols):
        kv_part = kv_part + rotate(
            lax.dynamic_index_in_dim(kv_low, (col + k) % cols, 0, keepdims=False), "col", k
        ).astype(jnp.float32)
    query_kv = jnp.concatenate(
        [
            grad_query.astype(jnp.bfloat16),
            kv_part.astype(jnp.bfloat16).reshape(-1, grad_query.shape[1]),
        ],
        axis=0,
    )
    query_kv = lax.psum(query_kv, "expert")
    left_parts = jnp.concatenate([grad_query_low, grad_kv], axis=1).reshape(
        -1, cols, tok_dev, grad_query_low.shape[1] + 2 * head_dim
    )
    right_all = jnp.concatenate([w_query, key_value_w], axis=1)

    def grad_normed_rows(place):
        left = lax.dynamic_index_in_dim(left_parts, place, 1, keepdims=False)
        return lax.dot_general(
            left, right_all, (((2,), (1,)), ((), ())), preferred_element_type=jnp.float32
        )

    left_parts, *out_returns[1:] = together(left_parts, *out_returns[1:])
    out_shares = spread_planes(out_share)
    out_parts = [out_first] + [add_parts(to_source(part)) for part in out_returns[1:]]
    col_sums = scatter_cols(grad_normed_rows)
    summed_values = jnp.concatenate(
        [grad_router.reshape(-1), grad_norm_moe, norm_terms, grad_q_gain[0], grad_k_gain[0]]
    )
    col_sums, summed_values = together(col_sums, summed_values)
    sums = sum_all(summed_values)
    grad_normed = scatter_rows(col_sums)
    grad_normed, sums, query_kv, *out_parts = together(grad_normed, sums, query_kv, *out_parts)
    out_rows = (mixed_rows + jnp.concatenate(out_parts, axis=1)).astype(jnp.bfloat16)
    grad_out_proj = in_plane_order(out_shares)
    places = (0, experts * model_width, model_width, model_width, head_dim, head_dim)
    ends_at = [sum(places[: k + 1]) for k in range(len(places))]
    grad_router, grad_norm_moe, grad_norm_attn, grad_q_gain, grad_k_gain = [
        sums[low:high] for low, high in zip(ends_at[:-1], ends_at[1:])
    ]
    grad_router = grad_router.reshape(experts, model_width).T
    grad_query = query_kv[:model_width].astype(jnp.float32)
    kv_part = query_kv[model_width:].reshape(-1, 2 * head_dim)
    kv_parts = jnp.stack([kv_part] + [rotate(kv_part, "col", k) for k in range(1, cols)], axis=0)
    kv_parts = lax.dynamic_slice_in_dim(
        jnp.concatenate([kv_parts[::-1], kv_parts[::-1]], axis=0), cols - 1 - col, cols, axis=0
    )
    kv_full = kv_parts.reshape(model_width, 2 * head_dim).astype(jnp.float32)
    grad_key = kv_full[:, :head_dim]
    grad_value = kv_full[:, head_dim:]
    grad_input_norm = norm_one_back(grad_normed)[0]
    grad_x = (grad_mixed + grad_input_norm).astype(jnp.bfloat16)
    return (
        out_rows,
        grad_x,
        grad_norm_attn,
        grad_query,
        grad_key,
        grad_value,
        grad_q_gain,
        grad_k_gain,
        grad_out_proj,
        grad_norm_moe,
        grad_router,
        grad_gate[None],
        grad_up[None],
        grad_down[None],
    )


def solution(mesh):
    placed = (
        P(("expert", "row", "col"), None),
        P(),
        P(None, ("row", "col")),
        P(None, "row"),
        P(None, "row"),
        P(),
        P(),
        P(("row", "col"), None),
        P(),
        P(),
        P(("expert", "row", "col"), None, None),
        P(("expert", "row", "col"), None, None),
        P(("expert", "row", "col"), None, None),
        P("expert", None),
        P(("expert", "row", "col"), None),
        P(("expert", "row", "col"), None),
    )
    return jax.shard_map(
        local,
        mesh=mesh,
        in_specs=placed,
        out_specs=(
            P(("expert", "row", "col"), None),
            P(("expert", "row", "col"), None),
            P(),
            P(None, ("row", "col")),
            P(None, "row"),
            P(None, "row"),
            P(),
            P(),
            P(("row", "col"), None),
            P(),
            P(),
            P(("expert", "row", "col"), None, None),
            P(("expert", "row", "col"), None, None),
            P(("expert", "row", "col"), None, None),
        ),
        check_vma=False,
    )
```

time: 881 us -> 676 us (0.77)
  waiting for transfers between devices: 383 us -> 254 us
  matrix products: 197 us -> 70.9 us
  Pallas kernels: 0 us -> 65.6 us
  local copies, waits for them, and re-layouts: 69.5 us -> 54.3 us
  starting transfers between devices: 137 us -> 146 us
    psum x2 -> x1, waiting for transfers between devices: 162 us -> 20.9 us  [local(): query_kv = lax.psum(query_kv, 'expert')]
    ppermute x6 -> x40, waiting for transfers between devices: 13.3 us -> 136 us  [rotate(): lax.ppermute(block, axis, [(i, (i + step) % size) for i in range(size)])]
    dot_general x39 -> x8, matrix products: 145 us -> 25.6 us  [the longest x4 13.4 us: to_source(): lax.dot_general(dispatch.reshape(plane_size * plane_cap, -1), returned, (...]
    ppermute x6 -> x40, starting transfers between devices: 4.85 us -> 76.9 us  [rotate(): lax.ppermute(block, axis, [(i, (i + step) % size) for i in range(size)])]
    ppermute x27 -> x6, waiting for transfers between devices: 87.4 us -> 19.8 us  [line_step(): return lax.ppermute(value, 'expert', pairs)]
    pallas_call x0 -> x3, Pallas kernels: none -> 65.6 us  [the longest x1 33 us: expert_rows(): pl.pallas_call(functools.partial(expert_kernel, count=count, experts=plan...]
    ppermute x27 -> x6, starting transfers between devices: 55.8 us -> 10.5 us  [line_step(): return lax.ppermute(value, 'expert', pairs)]
    reduce_scatter x1 -> x0, waiting for transfers between devices: 41.7 us -> none  [local(): lax.psum_scatter(jnp.dot(heads_low, w_out, preferred_element_type=jnp.flo...]
  transfers between devices with their start and end apart: 52 -> 59, of which waited for: 26 -> 26; matrix products, arithmetic and copies ran while one was open for 25% -> 21% of each run, Pallas kernels for 0% -> 5%
where the time goes in v2:
time: 676 us; the launch traced here: 666 us
  waiting for transfers between devices  254 us (38%)
  starting transfers between devices  146 us (22%)
  matrix products  70.9 us (10%)
  Pallas kernels  65.6 us (10%)
  other arithmetic  59.9 us (9%)
  local copies, waits for them, and re-layouts  54.3 us (8%)
  between operations  15.4 us (2%)
    ppermute x40, waiting for transfers between devices, rotate(): lax.ppermute(block, axis, [(i, (i + step) % size) for i in range(size)])  136 us
    ppermute x40, starting transfers between devices, rotate(): lax.ppermute(block, axis, [(i, (i + step) % size) for i in range(size)])  76.9 us
    all_to_all x8, starting transfers between devices, move_plane(): lax.all_to_all(parts, plane_axes, split_axis=0, concat_axis=0, tiled=True)  50.3 us
    all_to_all x8, waiting for transfers between devices, move_plane(): lax.all_to_all(parts, plane_axes, split_axis=0, concat_axis=0, tiled=True)  48.3 us
    dot_general x6, matrix products, transposed_times(): lax.dot_general(left, right, (((0,), (0,)), ((), ())), preferred_element_...  34.6 us
    pallas_call x1, Pallas kernels, expert_rows(): pl.pallas_call(functools.partial(expert_kernel, count=count, experts=plan...  33 us
    psum x1, waiting for transfers between devices, local(): query_kv = lax.psum(query_kv, 'expert')  20.9 us
    unnamed x153, local copies, waits for them, and re-layouts  20.7 us
  transfers between devices with their start and end apart: 59, of which 26 were waited for; matrix products, arithmetic and copies ran while one was open for 21% of the time, Pallas kernels for 5%

profile of v2, /device:TPU:1, one launch (start us, length us, event | category | flops | bytes accessed | tf_op | source)
XLA Modules:
  0.0 666.1 jit_solution(4767384436675032400)
XLA Ops:
  29.0 13.5 %collective-permute-done.4 = bf16[128,1024]{1,0:T(8,128)(2,1)} collective-permute-done((bf16[128,1024]{1,0:T(8,128)(2,1)}, bf16[128,1024]{1,0:T(8,128)(2,1)}, u32[]{:S(2)}, u32[]{:S(2)}) %collective-permute-start.4) | collective-permute-done | bytes 262176 | tf_op jit(solution)/shard_map/ppermute | solution.py:418
  60.0 14.9 %attend_rows.1 = (bf16[1024,2048]{1,0:T(8,128)(2,1)}, bf16[1024,512]{1,0:T(8,128)(2,1)}, bf16[1024,128]{1,0:T(8,128)(2,1)}, bf16[1024,128]{1,0:T(8,128)(2,1)}, b...) custom-call(s32[4]{0:T(128)S(1)} %bitcast.189, bf16[1024,2048]{1,0:T(8,128)(2,1)S(1)} %copy-done.5, ...), custom_call_target="tpu_custom_call" | custom-call | flops 6979321856 | bytes 12582912 | tf_op jit(solution)/shard_map/attend_rows/pallas_call | solution.py:169
  98.8 16.2 %collective-permute-done.11 = bf16[128,1024]{1,0:T(8,128)(2,1)} collective-permute-done((bf16[128,1024]{1,0:T(8,128)(2,1)}, bf16[128,1024]{1,0:T(8,128)(2,1)}, u32[]{:S(2)}, u32[]{:S(2)}) %collective-permute-start.11) | collective-permute-done | bytes 262176 | tf_op jit(solution)/shard_map/ppermute | solution.py:418
  136.9 17.3 %collective-permute-done.17 = bf16[128,1024]{1,0:T(8,128)(2,1)S(1)} collective-permute-done((bf16[128,1024]{1,0:T(8,128)(2,1)S(1)}, bf16[128,1024]{1,0:T(8,128)(2,1)S(1)}, u32[]{:S(2)}, u32[]{:S(2)}) %collective-permute-start.17) | collective-permute-done | bytes 262176 | tf_op jit(solution)/shard_map/ppermute | solution.py:418
  170.1 17.5 %collective-permute-done.14 = bf16[128,1024]{1,0:T(8,128)(2,1)S(1)} collective-permute-done((bf16[128,1024]{1,0:T(8,128)(2,1)}, bf16[128,1024]{1,0:T(8,128)(2,1)S(1)}, u32[]{:S(2)}, u32[]{:S(2)}) %collective-permute-start.14) | collective-permute-done | bytes 262176 | tf_op jit(solution)/shard_map/ppermute | solution.py:418
  199.9 21.5 %all-to-all-done.2 = bf16[8,136,1024]{2,1,0:T(8,128)(2,1)} async-done(((bf16[8,136,1024]{2,1,0:T(8,128)(2,1)}), bf16[8,136,1024]{2,1,0:T(8,128)(2,1)}, u32[]{:S(2)}, u32[]{:S(2)}) %all-to-all-start.2) | async-done | bytes 2228256 | tf_op jit(solution)/shard_map/all_to_all | solution.py:413
  222.4 33.0 %expert_rows.1 = (bf16[1088,1152]{1,0:T(8,128)(2,1)}, bf16[1088,1024]{1,0:T(8,128)(2,1)}, bf16[1088,1024]{1,0:T(8,128)(2,1)}, bf16[1088,1024]{1,0:T(8,128)(2,1)}...) custom-call(s32[2]{0:T(128)S(1)} %pad_add_fusion.1.ids_ref, ...), custom_call_target="tpu_custom_call" | custom-call | flops 20535312384 | bytes 9437184 | tf_op jit(solution)/shard_map/expert_rows/pallas_call | solution.py:597
  255.5 8.0 %all-to-all-start.5 = ((bf16[8,136,1024]{2,1,0:T(8,128)(2,1)}), bf16[8,136,1024]{2,1,0:T(8,128)(2,1)}, u32[]{:S(2)}, u32[]{:S(2)}) async-start(bf16[8,136,1024]{2,1,0:T(8,128)(2,1)} %bitcast.202), calls=%async_computation.5 | async-start | bytes 4456448 | tf_op jit(solution)/shard_map/all_to_all | solution.py:413
  263.9 9.8 %fusion.59 = f32[2048,768]{1,0:T(8,128)} fusion(bf16[1088,2048]{1,0:T(8,128)(2,1)} %get-tuple-element.90, bf16[1088,768]{1,0:T(8,128)(2,1)} %get-tuple-element.91), kind=kOutput, calls=%fused_computation.173 | convolution fusion | flops 3422552064 | bytes 12419072 | tf_op jit(solution)/shard_map/dot_general | solution.py:404
  273.7 14.3 %all-to-all-done.5 = bf16[8,136,1024]{2,1,0:T(8,128)(2,1)} async-done(((bf16[8,136,1024]{2,1,0:T(8,128)(2,1)}), bf16[8,136,1024]{2,1,0:T(8,128)(2,1)}, u32[]{:S(2)}, u32[]{:S(2)}) %all-to-all-start.5) | async-done | bytes 2228256 | tf_op jit(solution)/shard_map/all_to_all | solution.py:413
  288.0 8.3 %all-to-all-start.4 = ((bf16[8,136,1152]{2,1,0:T(8,128)(2,1)}), bf16[8,136,1152]{2,1,0:T(8,128)(2,1)}, u32[]{:S(2)}, u32[]{:S(2)}) async-start(bf16[8,136,1152]{2,1,0:T(8,128)(2,1)} %bitcast.197), calls=%async_computation.4 | async-start | bytes 5013504 | tf_op jit(solution)/shard_map/all_to_all | solution.py:413
  296.3 8.5 %fusion.60 = f32[2048,768]{1,0:T(8,128)} fusion(bf16[1088,2048]{1,0:T(8,128)(2,1)} %get-tuple-element.90, bf16[1088,768]{1,0:T(8,128)(2,1)S(1)} %copy-done.71), kind=kOutput, calls=%fused_computation.174 | convolution fusion | flops 3422552064 | bytes 12419072 | tf_op jit(solution)/shard_map/dot_general | solution.py:404
  323.8 7.9 %all-to-all-start.6 = ((bf16[8,136,1024]{2,1,0:T(8,128)(2,1)}), bf16[8,136,1024]{2,1,0:T(8,128)(2,1)}, u32[]{:S(2)}, u32[]{:S(2)}) async-start(bf16[8,136,1024]{2,1,0:T(8,128)(2,1)} %bitcast.68), calls=%async_computation.6 | async-start | bytes 4456448 | tf_op jit(solution)/shard_map/all_to_all | solution.py:413
  345.7 14.3 %collective-permute-done.20 = bf16[128,1152]{1,0:T(8,128)(2,1)S(1)} collective-permute-done((bf16[128,1152]{1,0:T(8,128)(2,1)S(1)}, bf16[128,1152]{1,0:T(8,128)(2,1)S(1)}, u32[]{:S(2)}, u32[]{:S(2)}) %collective-permute-start.20) | collective-permute-done | bytes 294944 | tf_op jit(solution)/shard_map/ppermute | solution.py:418
  384.2 12.2 %collective-permute-done.26 = bf16[128,1024]{1,0:T(8,128)(2,1)S(1)} collective-permute-done((bf16[128,1024]{1,0:T(8,128)(2,1)S(1)}, bf16[128,1024]{1,0:T(8,128)(2,1)S(1)}, u32[]{:S(2)}, u32[]{:S(2)}) %collective-permute-start.26) | collective-permute-done | bytes 262176 | tf_op jit(solution)/shard_map/ppermute | solution.py:418
  397.4 11.5 %all-gather.5.cloned.1.call-done.grad_ref = bf16[1024,2048]{1,0:T(8,128)(2,1)} async-done(((bf16[128,2048]{1,0:T(8,128)(2,1)}), bf16[1024,2048]{1,0:T(8,128)(2,1)}) %all-gather.5.cloned.1.call-update) | async-done | bytes 4194320 | tf_op jit(solution)/shard_map/all_gather | solution.py:797
  432.6 17.6 %attend_rows_back.1 = (bf16[1024,512]{1,0:T(8,128)(2,1)}, bf16[1024,256]{1,0:T(8,128)(2,1)}, f32[1,128]{1,0:T(1,128)}, f32[1,128]{1,0:T(1,128)}) custom-call(s32[4]{0:T(128)S(1)} %bitcast.190, bf16[1024,2048]{1,0:T(8,128)(2,1)S(1)} %copy-done.7, bf16[512,2048]{1,0:T(8,128)(2,1)S(1)} %copy-done.9, bf16[1024,512]{1,0:T(8,128)(2,1)S(1)} %copy-done.15, ...), custom_call_target="tpu_custom_call" | custom-call | flops 5368709120 | bytes 6291456 | tf_op jit(solution)/shard_map/attend_rows_back/pallas_call | solution.py:358
  450.2 14.1 %collective-permute-done.29 = bf16[128,2048]{1,0:T(8,128)(2,1)} collective-permute-done((bf16[128,2048]{1,0:T(8,128)(2,1)}, bf16[128,2048]{1,0:T(8,128)(2,1)}, u32[]{:S(2)}, u32[]{:S(2)}) %collective-permute-start.29) | collective-permute-done | bytes 524320 | tf_op jit(solution)/shard_map/ppermute | solution.py:418
  493.0 10.1 %collective-permute-done.44 = bf16[128,2048]{1,0:T(8,128)(2,1)} collective-permute-done((bf16[128,2048]{1,0:T(8,128)(2,1)}, bf16[128,2048]{1,0:T(8,128)(2,1)}, u32[]{:S(2)}, u32[]{:S(2)}) %collective-permute-start.44) | collective-permute-done | bytes 524320 | tf_op jit(solution)/shard_map/ppermute | solution.py:453
  515.9 24.6 %collective-permute-start.36 = (bf16[128,1024]{1,0:T(8,128)(2,1)}, bf16[128,1024]{1,0:T(8,128)(2,1)}, u32[]{:S(2)}, u32[]{:S(2)}) collective-permute-start(bf16[128,1024]{1,0:T(8,128)(2,1)} %get-tuple-element.156), channel_id=1, source_target_pairs={{0,24},{8,0},{16,8},{24,16},{1,25},{9,1},{17,9},{25,17},{2,26},{10... | collective-permute-start | bytes 786440 | tf_op jit(solution)/shard_map/ppermute | solution.py:418
  545.2 9.8 %collective-permute-done.45 = bf16[128,2048]{1,0:T(8,128)(2,1)} collective-permute-done((bf16[128,2048]{1,0:T(8,128)(2,1)}, bf16[128,2048]{1,0:T(8,128)(2,1)}, u32[]{:S(2)}, u32[]{:S(2)}) %collective-permute-start.45) | collective-permute-done | bytes 524320 | tf_op jit(solution)/shard_map/ppermute | solution.py:453
  578.8 7.6 %all-to-all-done.8 = f32[32,18,128]{2,1,0:T(8,128)S(1)} async-done(((f32[32,18,128]{2,1,0:T(8,128)}), f32[32,18,128]{2,1,0:T(8,128)S(1)}, u32[]{:S(2)}, u32[]{:S(2)}) %all-to-all-start.8) | async-done | bytes 294944 | tf_op jit(solution)/shard_map/all_to_all | solution.py:435
  594.7 11.6 %collective-permute-done.32 = bf16[128,2048]{1,0:T(8,128)(2,1)} collective-permute-done((bf16[128,2048]{1,0:T(8,128)(2,1)S(1)}, bf16[128,2048]{1,0:T(8,128)(2,1)}, u32[]{:S(2)}, u32[]{:S(2)}) %collective-permute-start.32) | collective-permute-done | bytes 524320 | tf_op jit(solution)/shard_map/ppermute | solution.py:418
  615.8 20.9 %all-reduce.5.cloned.1.call-done = bf16[2560,512]{1,0:T(8,128)(2,1)} async-done(((bf16[2560,512]{1,0:T(8,128)(2,1)}), bf16[2560,512]{1,0:T(8,128)(2,1)}) %all-reduce.5.cloned.1.call-update) | async-done | bytes 2621456 | tf_op jit(solution)/shard_map/psum | solution.py:841
  (377 shorter events, 305.8 us)
Async XLA Ops:
  7.2 42.7 %all-gather.3.cloned.1.call-start = ((), (), s32[]{:S(2)}) async-start(), calls=%async_computation.10 | async-start | bytes 4718592 | tf_op jit(solution)/shard_map/all_gather | solution.py:701
  49.9 32.2 %all-to-all-start = ((bf16[8,136,1152]{2,1,0:T(8,128)(2,1)}), bf16[8,136,1152]{2,1,0:T(8,128)(2,1)}, u32[]{:S(2)}, u32[]{:S(2)}) async-start(bf16[8,136,1152]{2,1,0:T(8,128)(2,1)} %bitcast.198), calls=%async_computation | async-start | bytes 5013504 | tf_op jit(solution)/shard_map/all_to_all | solution.py:413
  120.1 37.0 %all-to-all-start.1 = ((bf16[8,136,1024]{2,1,0:T(8,128)(2,1)}), bf16[8,136,1024]{2,1,0:T(8,128)(2,1)}, u32[]{:S(2)}, u32[]{:S(2)}) async-start(bf16[8,136,1024]{2,1,0:T(8,128)(2,1)} %bitcast.200), calls=%async_computation.1 | async-start | bytes 4456448 | tf_op jit(solution)/shard_map/all_to_all | solution.py:413
  157.1 34.4 %all-to-all-start.3 = ((bf16[8,136,1024]{2,1,0:T(8,128)(2,1)}), bf16[8,136,1024]{2,1,0:T(8,128)(2,1)S(1)}, u32[]{:S(2)}, u32[]{:S(2)}) async-start(bf16[8,136,1024]{2,1,0:T(8,128)(2,1)} %bitcast.201), calls=%async_computation.3 | async-start | bytes 4456448 | tf_op jit(solution)/shard_map/all_to_all | solution.py:413
  161.9 25.7 %collective-permute-start.14 = (bf16[128,1024]{1,0:T(8,128)(2,1)}, bf16[128,1024]{1,0:T(8,128)(2,1)S(1)}, u32[]{:S(2)}, u32[]{:S(2)}) collective-permute-start(bf16[128,1024]{1,0:T(8,128)(2,1)} %get-tuple-element.168), channel_id=1, source_target_pairs={{0,16},{8,24},{16,0},{24,8},{1,17},{9,25},{17,1},{25,9},{2,18},{10... | collective-permute-start | bytes 786440 | tf_op jit(solution)/shard_map/ppermute | solution.py:418
  191.5 29.9 %all-to-all-start.2 = ((bf16[8,136,1024]{2,1,0:T(8,128)(2,1)}), bf16[8,136,1024]{2,1,0:T(8,128)(2,1)}, u32[]{:S(2)}, u32[]{:S(2)}) async-start(bf16[8,136,1024]{2,1,0:T(8,128)(2,1)} %bitcast.203), calls=%async_computation.2 | async-start | bytes 4456448 | tf_op jit(solution)/shard_map/all_to_all | solution.py:413
  255.5 32.6 %all-to-all-start.5 = ((bf16[8,136,1024]{2,1,0:T(8,128)(2,1)}), bf16[8,136,1024]{2,1,0:T(8,128)(2,1)}, u32[]{:S(2)}, u32[]{:S(2)}) async-start(bf16[8,136,1024]{2,1,0:T(8,128)(2,1)} %bitcast.202), calls=%async_computation.5 | async-start | bytes 4456448 | tf_op jit(solution)/shard_map/all_to_all | solution.py:413
  288.0 35.8 %all-to-all-start.4 = ((bf16[8,136,1152]{2,1,0:T(8,128)(2,1)}), bf16[8,136,1152]{2,1,0:T(8,128)(2,1)}, u32[]{:S(2)}, u32[]{:S(2)}) async-start(bf16[8,136,1152]{2,1,0:T(8,128)(2,1)} %bitcast.197), calls=%async_computation.4 | async-start | bytes 5013504 | tf_op jit(solution)/shard_map/all_to_all | solution.py:413
  323.8 42.7 %all-to-all-start.6 = ((bf16[8,136,1024]{2,1,0:T(8,128)(2,1)}), bf16[8,136,1024]{2,1,0:T(8,128)(2,1)}, u32[]{:S(2)}, u32[]{:S(2)}) async-start(bf16[8,136,1024]{2,1,0:T(8,128)(2,1)} %bitcast.68), calls=%async_computation.6 | async-start | bytes 4456448 | tf_op jit(solution)/shard_map/all_to_all | solution.py:413
  331.7 77.2 %all-gather.5.cloned.1.call-start = ((), (), s32[]{:S(2)}) async-start(), calls=%async_computation.11 | async-start | bytes 4718592 | tf_op jit(solution)/shard_map/all_gather | solution.py:797
  335.4 24.6 %collective-permute-start.20 = (bf16[128,1152]{1,0:T(8,128)(2,1)S(1)}, bf16[128,1152]{1,0:T(8,128)(2,1)S(1)}, u32[]{:S(2)}, u32[]{:S(2)}) collective-permute-start(bf16[128,1152]{1,0:T(8,128)(2,1)S(1)} %get-tuple-element.153), channel_id=1, source_target_pairs={{0,16},{8,24},{16,0},{24,8},{1,17},{9,25},{17,1},{25,9},{2,18},{10... | collective-permute-start | bytes 884744 | tf_op jit(solution)/shard_map/ppermute | solution.py:418
  415.9 34.2 %collective-permute-start.30 = (bf16[128,2048]{1,0:T(8,128)(2,1)}, bf16[128,2048]{1,0:T(8,128)(2,1)}, u32[]{:S(2)}, u32[]{:S(2)}) collective-permute-start(bf16[128,2048]{1,0:T(8,128)(2,1)} %get-tuple-element.146), channel_id=1, source_target_pairs={{0,24},{8,0},{16,8},{24,16},{1,25},{9,1},{17,9},{25,17},{2,26},{10... | collective-permute-start | bytes 1572872 | tf_op jit(solution)/shard_map/ppermute | solution.py:418
  419.0 45.2 %collective-permute-start.29 = (bf16[128,2048]{1,0:T(8,128)(2,1)}, bf16[128,2048]{1,0:T(8,128)(2,1)}, u32[]{:S(2)}, u32[]{:S(2)}) collective-permute-start(bf16[128,2048]{1,0:T(8,128)(2,1)} %get-tuple-element.147), channel_id=1, source_target_pairs={{0,16},{8,24},{16,0},{24,8},{1,17},{9,25},{17,1},{25,9},{2,18},{10... | collective-permute-start | bytes 1572872 | tf_op jit(solution)/shard_map/ppermute | solution.py:418
  419.1 45.2 %collective-permute-start.28 = (bf16[128,2048]{1,0:T(8,128)(2,1)}, bf16[128,2048]{1,0:T(8,128)(2,1)}, u32[]{:S(2)}, u32[]{:S(2)}) collective-permute-start(bf16[128,2048]{1,0:T(8,128)(2,1)} %get-tuple-element.145), channel_id=1, source_target_pairs={{0,8},{8,16},{16,24},{24,0},{1,9},{9,17},{17,25},{25,1},{2,10},{10... | collective-permute-start | bytes 1572872 | tf_op jit(solution)/shard_map/ppermute | solution.py:418
  420.2 84.4 %all-to-all-start.7 = ((bf16[8,136,1024]{2,1,0:T(8,128)(2,1)}), bf16[8,136,1024]{2,1,0:T(8,128)(2,1)}, u32[]{:S(2)}, u32[]{:S(2)}) async-start(bf16[8,136,1024]{2,1,0:T(8,128)(2,1)} %bitcast.199), calls=%async_computation.7 | async-start | bytes 4456448 | tf_op jit(solution)/shard_map/all_to_all | solution.py:413
  425.5 211.2 %all-reduce.5.cloned.1.call-start = ((), (), s32[]{:S(2)}) async-start(), calls=%async_computation.12 | async-start | bytes 5242880 | tf_op jit(solution)/shard_map/psum | solution.py:841
  491.5 24.4 %collective-permute-start.42 = (bf16[128,2048]{1,0:T(8,128)(2,1)}, bf16[128,2048]{1,0:T(8,128)(2,1)}, u32[]{:S(2)}, u32[]{:S(2)}) collective-permute-start(bf16[128,2048]{1,0:T(8,128)(2,1)} %collective-permute-done.41), channel_id=1, source_target_pairs={{16,24},{17,25},{18,26},{19,27},{20,28},{21,29},{22,30},{23,31}} | collective-permute-start | bytes 1572872 | tf_op jit(solution)/shard_map/ppermute | solution.py:453
  503.0 51.9 %collective-permute-start.45 = (bf16[128,2048]{1,0:T(8,128)(2,1)}, bf16[128,2048]{1,0:T(8,128)(2,1)}, u32[]{:S(2)}, u32[]{:S(2)}) collective-permute-start(bf16[128,2048]{1,0:T(8,128)(2,1)} %collective-permute-done.44), channel_id=1, source_target_pairs={{8,0},{9,1},{10,2},{11,3},{12,4},{13,5},{14,6},{15,7}} | collective-permute-start | bytes 1572872 | tf_op jit(solution)/shard_map/ppermute | solution.py:453
  507.6 58.0 %collective-permute-start.31 = (bf16[4,128,2048]{2,1,0:T(8,128)(2,1)S(1)}, bf16[4,128,2048]{2,1,0:T(8,128)(2,1)S(1)}, u32[]{:S(2)}, u32[]{:S(2)}) collective-permute-start(bf16[4,128,2048]{2,1,0:T(8,128)(2,1)S(1)} %convolution_convert_fusion.5), channel_id=1, source_target_pairs={{0,1},{1,0},{2,3},{3,2},{4,5},{5,4},{6,7},{7,6},{8,9},{9,8},{10,11... | collective-permute-start | bytes 6291464 | tf_op jit(solution)/shard_map/ppermute | solution.py:418
  512.8 64.7 %collective-permute-start.38 = (bf16[128,1024]{1,0:T(8,128)(2,1)}, bf16[128,1024]{1,0:T(8,128)(2,1)S(1)}, u32[]{:S(2)}, u32[]{:S(2)}) collective-permute-start(bf16[128,1024]{1,0:T(8,128)(2,1)} %get-tuple-element.157), channel_id=1, source_target_pairs={{0,8},{8,16},{16,24},{24,0},{1,9},{9,17},{17,25},{25,1},{2,10},{10... | collective-permute-start | bytes 786440 | tf_op jit(solution)/shard_map/ppermute | solution.py:418
  515.9 76.6 %collective-permute-start.37 = (bf16[128,1024]{1,0:T(8,128)(2,1)}, bf16[128,1024]{1,0:T(8,128)(2,1)}, u32[]{:S(2)}, u32[]{:S(2)}) collective-permute-start(bf16[128,1024]{1,0:T(8,128)(2,1)} %get-tuple-element.158), channel_id=1, source_target_pairs={{0,16},{8,24},{16,0},{24,8},{1,17},{9,25},{17,1},{25,9},{2,18},{10... | collective-permute-start | bytes 786440 | tf_op jit(solution)/shard_map/ppermute | solution.py:418
  515.9 76.6 %collective-permute-start.36 = (bf16[128,1024]{1,0:T(8,128)(2,1)}, bf16[128,1024]{1,0:T(8,128)(2,1)}, u32[]{:S(2)}, u32[]{:S(2)}) collective-permute-start(bf16[128,1024]{1,0:T(8,128)(2,1)} %get-tuple-element.156), channel_id=1, source_target_pairs={{0,24},{8,0},{16,8},{24,16},{1,25},{9,1},{17,9},{25,17},{2,26},{10... | collective-permute-start | bytes 786440 | tf_op jit(solution)/shard_map/ppermute | solution.py:418
  577.5 28.8 %collective-permute-start.32 = (bf16[128,2048]{1,0:T(8,128)(2,1)S(1)}, bf16[128,2048]{1,0:T(8,128)(2,1)}, u32[]{:S(2)}, u32[]{:S(2)}) collective-permute-start(bf16[128,2048]{1,0:T(8,128)(2,1)S(1)} %get-tuple-element.142), channel_id=1, source_target_pairs={{0,2},{2,4},{4,6},{6,0},{1,3},{3,5},{5,7},{7,1},{8,10},{10,12},{12... | collective-permute-start | bytes 1572872 | tf_op jit(solution)/shard_map/ppermute | solution.py:418
  587.2 28.5 %all-to-all-start.9 = ((f32[32,18,128]{2,1,0:T(8,128)}), f32[32,18,128]{2,1,0:T(8,128)S(1)}, u32[]{:S(2)}, u32[]{:S(2)}) async-start(f32[32,18,128]{2,1,0:T(8,128)} %broadcast_in_dim.78), calls=%async_computation.9 | async-start | bytes 786432 | tf_op jit(solution)/shard_map/all_to_all | solution.py:435
  (109 other events, 1384.7 us)
Sparse Core Ops, SparseCore 0:
  10.7 39.2 all-gather.2
  366.6 42.1 all-gather.4
  491.6 145.0 all-reduce.4

commit v3 on v2

--- a/solution.py
+++ b/solution.py
@@ -11,9 +11,8 @@
 rope_base = 1000000.0
 highest = lax.Precision.HIGHEST
 chunk_count = 2
-block_slots = 256
-expert_steps = 4
-expert_vmem = 48 * 1024 * 1024
+expert_steps = 2
+expert_vmem = 56 * 1024 * 1024
 kernel_vmem = 40 * 1024 * 1024
 
 
@@ -55,8 +54,13 @@
     return pltpu.roll(values, values.shape[-1] // 2, axis=1)
 
 
+def keep(array):
+    return pltpu.with_memory_space_constraint(array, pltpu.HBM)
+
+
 def attend_kernel(
     ends_ref,
+    place_ref,
     rows_ref,
     query_w_ref,
     kv_w_ref,
@@ -65,7 +69,8 @@
     key_gain_ref,
     cosine_ref,
     sine_ref,
-    partial_ref,
+    kept_ref,
+    sent_ref,
     query_ref,
     key_ref,
     value_ref,
@@ -76,6 +81,7 @@
     values,
     total,
     sums,
+    partial,
     *,
     head_dim,
 ):
@@ -144,17 +150,21 @@
     outs = (total[:, :head_dim] / total[:, head_dim:]).astype(jnp.bfloat16)
     for h in range(heads):
         heads_ref[:, h * head_dim : (h + 1) * head_dim] = outs[h * block : (h + 1) * block]
-    partial_ref[...] = jnp.dot(
+    partial[...] = jnp.dot(
         heads_ref[...], out_w_ref[...], preferred_element_type=jnp.float32
     ).astype(jnp.bfloat16)
-
-
-def attend_rows(ends, rows, w_query, w_kv, w_out, q_gain, k_gain, cosine, sine):
+    share = kept_ref.shape[0]
+    kept = pl.multiple_of(place_ref[0] * share, share)
+    sent = pl.multiple_of((1 - place_ref[0]) * share, share)
+    kept_ref[...] = partial[pl.ds(kept, share), :]
+    sent_ref[...] = partial[pl.ds(sent, share), :]
+
+
+def attend_rows(ends, place, rows, w_query, w_kv, w_out, q_gain, k_gain, cosine, sine, block):
     slots, width = rows.shape
     head_dim = q_gain.shape[0]
     head_width = w_query.shape[1]
     heads = head_width // head_dim
-    block = min(block_slots, slots)
     count = slots // block
 
     def tile(columns):
@@ -162,6 +172,9 @@
 
     def whole(array):
         return pl.BlockSpec(array.shape, lambda i: (0, 0))
+
+    def half(columns):
+        return pl.BlockSpec((block // 2, columns), lambda i: (i, 0))
 
     shape = pltpu.HBM
     q_gain = q_gain[None]
@@ -170,6 +183,7 @@
         functools.partial(attend_kernel, head_dim=head_dim),
         grid=(count,),
         in_specs=[
+            pl.BlockSpec(memory_space=pltpu.SMEM),
             pl.BlockSpec(memory_space=pltpu.SMEM),
             tile(width),
             whole(w_query),
@@ -181,7 +195,8 @@
             tile(head_dim),
         ],
         out_specs=[
-            tile(width),
+            half(width),
+            half(width),
             tile(head_width),
             tile(head_dim),
             tile(head_dim),
@@ -190,7 +205,8 @@
             tile(head_dim),
         ],
         out_shape=[
-            shape((slots, width), jnp.bfloat16),
+            shape((slots // 2, width), jnp.bfloat16),
+            shape((slots // 2, width), jnp.bfloat16),
             shape((slots, head_width), jnp.bfloat16),
             shape((slots, head_dim), jnp.bfloat16),
             shape((slots, head_dim), jnp.bfloat16),
@@ -203,6 +219,7 @@
             pltpu.VMEM((slots, 2 * head_dim), jnp.bfloat16),
             pltpu.VMEM((heads * block, 2 * head_dim), jnp.float32),
             pltpu.VMEM((8, heads * block), jnp.float32),
+            pltpu.VMEM((block, width), jnp.bfloat16),
         ],
         compiler_params=pltpu.CompilerParams(vmem_limit_bytes=kernel_vmem),
         cost_estimate=pl.CostEstimate(
@@ -212,7 +229,18 @@
             transcendentals=slots * slots * heads // 2,
         ),
         name="attend_rows",
-    )(ends, rows, w_query, w_kv, w_out, q_gain, k_gain, cosine, sine)
+    )(
+        ends,
+        place,
+        keep(rows),
+        keep(w_query),
+        keep(w_kv),
+        keep(w_out),
+        q_gain,
+        k_gain,
+        keep(cosine),
+        keep(sine),
+    )
 
 
 def attend_back_kernel(
@@ -337,13 +365,12 @@
 
 
 def attend_rows_back(
-    ends, grad, w_out, query, heads_low, key, value, logs, scales, q_gain, k_gain, cosine, sine
+    ends, grad, w_out, query, heads_low, key, value, logs, scales, q_gain, k_gain, cosine, sine, block
 ):
     slots, width = grad.shape
     head_dim = q_gain.shape[0]
     head_width = query.shape[1]
     heads = head_width // head_dim
-    block = min(block_slots, slots)
     count = slots // block
 
     def tile(columns):
@@ -397,7 +424,21 @@
             transcendentals=slots * slots * heads // 2,
         ),
         name="attend_rows_back",
-    )(ends, grad, w_out, query, heads_low, key, value, logs, scales, q_gain, k_gain, cosine, sine)
+    )(
+        ends,
+        keep(grad),
+        keep(w_out),
+        keep(query),
+        keep(heads_low),
+        keep(key),
+        keep(value),
+        keep(logs),
+        keep(scales),
+        q_gain,
+        k_gain,
+        keep(cosine),
+        keep(sine),
+    )
 
 
 def transposed_times(left, right):
@@ -453,7 +494,7 @@
     return lax.ppermute(value, "expert", pairs)
 
 
-def sum_planes(product):
+def send_planes(product):
     planes = lax.axis_size("expert")
     plane = lax.axis_index("expert")
     shares = product.reshape(planes, -1, product.shape[1])
@@ -461,11 +502,7 @@
     def share(k):
         return lax.dynamic_index_in_dim(shares, (plane + k) % planes, 0, keepdims=False)
 
-    arrived = [rotate(share(k), "expert", k) for k in range(1, planes)]
-    total = share(0).astype(jnp.float32)
-    for part in arrived:
-        total = total + part.astype(jnp.float32)
-    return total.astype(product.dtype)
+    return [share(0)] + [rotate(share(k), "expert", k) for k in range(1, planes)]
 
 
 def spread_planes(total):
@@ -702,18 +739,18 @@
     ends = jnp.cumsum(seq_lengths[0], dtype=jnp.int32)
     cosine_table, sine_table = rope_tables(slot_positions(ends, group_tok), head_dim)
     key_value_w = jnp.concatenate([w_key, w_value], axis=1)
-    group_rows, slot_sends[0], cosine_table, sine_table, key_value_w = together(
-        group_rows, slot_sends[0], cosine_table, sine_table, key_value_w
+    cosine_table, sine_table, key_value_w, slot_sends[0] = together(
+        cosine_table, sine_table, key_value_w, slot_sends[0]
     )
     grad_slot_chunks = [to_plane(slot_sends[0])]
-    attn_partial, query_low, key_low, value_low, heads_low, log_totals, head_scales = attend_rows(
-        ends, group_rows, w_query, key_value_w, w_out, q_gain, k_gain, cosine_table, sine_table
-    )
-    attn_partial, grad_slot_chunks[0] = together(attn_partial, grad_slot_chunks[0])
-    col_parts = attn_partial.reshape(-1, lax.axis_size("col"), tok_dev, model_width)
-    attn_rows = scatter_rows(
-        scatter_cols(lambda place: lax.dynamic_index_in_dim(col_parts, place, 1, keepdims=False))
-    )
+    col = lax.axis_index("col")
+    kept, sent, query_low, key_low, value_low, heads_low, log_totals, head_scales = attend_rows(
+        ends, col.astype(jnp.int32)[None], group_rows, w_query, key_value_w, w_out, q_gain, k_gain, cosine_table, sine_table,
+        2 * tok_dev,
+    )
+    sent, kept, grad_slot_chunks[0] = together(sent, kept, grad_slot_chunks[0])
+    col_sums = kept.astype(jnp.float32) + rotate(sent, "col", 1).astype(jnp.float32)
+    attn_rows = scatter_rows(col_sums.astype(jnp.bfloat16).reshape(-1, tok_dev, model_width))
     attn_rows, *late_sends = together(attn_rows, *slot_sends[1:])
     grad_slot_chunks += [to_plane(part) for part in late_sends]
     attn_rows = attn_rows.astype(jnp.float32)
@@ -800,7 +837,7 @@
     out_returns += [to_plane(part) for part in out_late]
     grad_out_proj = transposed_times(heads_low, grad_group).astype(jnp.bfloat16)
     grad_out_proj, grad_group = together(grad_out_proj, grad_group)
-    out_share = sum_planes(grad_out_proj)
+    out_terms = send_planes(grad_out_proj)
     grad_query_low, grad_kv, grad_q_gain, grad_k_gain = attend_rows_back(
         ends,
         grad_group,
@@ -815,8 +852,11 @@
         k_gain,
         cosine_table,
         sine_table,
-    )
-    grad_query_low, grad_kv, out_share = together(grad_query_low, grad_kv, out_share)
+        2 * tok_dev,
+    )
+    grad_query_low, grad_kv, out_terms[1], out_terms[-1] = together(
+        grad_query_low, grad_kv, out_terms[1], out_terms[-1]
+    )
     grad_query = transposed_times(group_rows, grad_query_low)
     grad_key_value = transposed_times(group_rows, grad_kv)
     norm_terms = (
@@ -831,10 +871,13 @@
         kv_part = kv_part + rotate(
             lax.dynamic_index_in_dim(kv_low, (col + k) % cols, 0, keepdims=False), "col", k
         ).astype(jnp.float32)
+    lane_parts = grad_query.shape[1] // (2 * head_dim)
     query_kv = jnp.concatenate(
         [
             grad_query.astype(jnp.bfloat16),
-            kv_part.astype(jnp.bfloat16).reshape(-1, grad_query.shape[1]),
+            *[
+                jnp.concatenate(jnp.split(kv_part.astype(jnp.bfloat16), lane_parts), axis=1)
+            ],
         ],
         axis=0,
     )
@@ -850,7 +893,8 @@
             left, right_all, (((2,), (1,)), ((), ())), preferred_element_type=jnp.float32
         )
 
-    left_parts, *out_returns[1:] = together(left_parts, *out_returns[1:])
+    out_share = add_parts(out_terms).astype(jnp.bfloat16)
+    left_parts, out_share, *out_returns[1:] = together(left_parts, out_share, *out_returns[1:])
     out_shares = spread_planes(out_share)
     out_parts = [out_first] + [add_parts(to_source(part)) for part in out_returns[1:]]
     col_sums = scatter_cols(grad_normed_rows)
@@ -870,14 +914,16 @@
     ]
     grad_router = grad_router.reshape(experts, model_width).T
     grad_query = query_kv[:model_width].astype(jnp.float32)
-    kv_part = query_kv[model_width:].reshape(-1, 2 * head_dim)
-    kv_parts = jnp.stack([kv_part] + [rotate(kv_part, "col", k) for k in range(1, cols)], axis=0)
-    kv_parts = lax.dynamic_slice_in_dim(
-        jnp.concatenate([kv_parts[::-1], kv_parts[::-1]], axis=0), cols - 1 - col, cols, axis=0
-    )
-    kv_full = kv_parts.reshape(model_width, 2 * head_dim).astype(jnp.float32)
-    grad_key = kv_full[:, :head_dim]
-    grad_value = kv_full[:, head_dim:]
+    kv_part = query_kv[model_width:]
+    kv_parts = [kv_part] + [rotate(kv_part, "col", k) for k in range(1, cols)]
+    kv_blocks = []
+    for place in range(cols):
+        block = kv_parts[0]
+        for k in range(1, cols):
+            block = jnp.where((col - k) % cols == place, kv_parts[k], block)
+        kv_blocks += jnp.split(block.astype(jnp.float32), lane_parts, axis=1)
+    grad_key = jnp.concatenate([block[:, :head_dim] for block in kv_blocks], axis=0)
+    grad_value = jnp.concatenate([block[:, head_dim:] for block in kv_blocks], axis=0)
     grad_input_norm = norm_one_back(grad_normed)[0]
     grad_x = (grad_mixed + grad_input_norm).astype(jnp.bfloat16)
     return (

time: 676 us -> 656 us (0.970)
  local copies, waits for them, and re-layouts: 54.3 us -> 22.8 us
  waiting for transfers between devices: 254 us -> 282 us
  starting transfers between devices: 146 us -> 131 us
    ppermute x40, waiting for transfers between devices: 136 us -> 162 us  [rotate(): lax.ppermute(block, axis, [(i, (i + step) % size) for i in range(size)])]
    psum x1, waiting for transfers between devices: 20.9 us -> 0.01 us  [local(): query_kv = lax.psum(query_kv, 'expert')]
    ppermute x40, starting transfers between devices: 76.9 us -> 58.5 us  [rotate(): lax.ppermute(block, axis, [(i, (i + step) % size) for i in range(size)])]
    unnamed x153 -> x97, local copies, waits for them, and re-layouts: 20.7 us -> 2.47 us
    ppermute x6, waiting for transfers between devices: 19.8 us -> 32.2 us  [line_step(): return lax.ppermute(value, 'expert', pairs)]
    all_to_all x2, waiting for transfers between devices: 14.4 us -> 24.4 us  [move_all(): lax.all_to_all(parts, ('expert',) + plane_axes, split_axis=0, concat_axis...]
  transfers between devices with their start and end apart: 59 -> 59, of which waited for: 26 -> 27; matrix products, arithmetic and copies ran while one was open for 21% -> 19% of each run, Pallas kernels for 5% -> 6%
where the time goes in v3:
time: 656 us; the launch traced here: 647 us
  waiting for transfers between devices  282 us (43%)
  starting transfers between devices  131 us (20%)
  Pallas kernels  71.2 us (11%)
  matrix products  70.2 us (11%)
  other arithmetic  55.3 us (8%)
  local copies, waits for them, and re-layouts  22.8 us (3%)
  between operations  15 us (2%)
    ppermute x40, waiting for transfers between devices, rotate(): lax.ppermute(block, axis, [(i, (i + step) % size) for i in range(size)])  162 us
    ppermute x40, starting transfers between devices, rotate(): lax.ppermute(block, axis, [(i, (i + step) % size) for i in range(size)])  58.5 us
    all_to_all x8, starting transfers between devices, move_plane(): lax.all_to_all(parts, plane_axes, split_axis=0, concat_axis=0, tiled=True)  52.6 us
    all_to_all x8, waiting for transfers between devices, move_plane(): lax.all_to_all(parts, plane_axes, split_axis=0, concat_axis=0, tiled=True)  50.7 us
    dot_general x6, matrix products, transposed_times(): lax.dot_general(left, right, (((0,), (0,)), ((), ())), preferred_element_...  37.5 us
    pallas_call x1, Pallas kernels, expert_rows(): pl.pallas_call(functools.partial(expert_kernel, count=count, experts=plan...  33.6 us
    ppermute x6, waiting for transfers between devices, line_step(): return lax.ppermute(value, 'expert', pairs)  32.2 us
    all_to_all x2, waiting for transfers between devices, move_all(): lax.all_to_all(parts, ('expert',) + plane_axes, split_axis=0, concat_axis...  24.4 us
  transfers between devices with their start and end apart: 59, of which 27 were waited for; matrix products, arithmetic and copies ran while one was open for 19% of the time, Pallas kernels for 6%

profile of v3, /device:TPU:1, one launch (start us, length us, event | category | flops | bytes accessed | tf_op | source)
XLA Modules:
  0.0 646.9 jit_solution(17636768924786412742)
XLA Ops:
  29.4 13.0 %collective-permute-done.4 = bf16[128,1024]{1,0:T(8,128)(2,1)} collective-permute-done((bf16[128,1024]{1,0:T(8,128)(2,1)}, bf16[128,1024]{1,0:T(8,128)(2,1)}, u32[]{:S(2)}, u32[]{:S(2)}) %collective-permute-start.4) | collective-permute-done | bytes 262176 | tf_op jit(solution)/shard_map/ppermute | solution.py:459
  53.6 17.6 %attend_rows.1 = (bf16[512,2048]{1,0:T(8,128)(2,1)}, bf16[512,2048]{1,0:T(8,128)(2,1)}, bf16[1024,512]{1,0:T(8,128)(2,1)}, bf16[1024,128]{1,0:T(8,128)(2,1)}, bf...) custom-call(s32[4]{0:T(128)S(1)} %bitcast.178, ...), custom_call_target="tpu_custom_call" | custom-call | flops 6979321856 | bytes 12582912 | tf_op jit(solution)/shard_map/attend_rows/pallas_call | solution.py:182
  71.2 9.9 %all-to-all-done = bf16[8,136,1152]{2,1,0:T(8,128)(2,1)} async-done(((bf16[8,136,1152]{2,1,0:T(8,128)(2,1)}), bf16[8,136,1152]{2,1,0:T(8,128)(2,1)}, u32[]{:S(2)}, u32[]{:S(2)}) %all-to-all-start) | async-done | bytes 2506784 | tf_op jit(solution)/shard_map/all_to_all | solution.py:454
  94.4 15.0 %collective-permute-done.11 = bf16[128,1024]{1,0:T(8,128)(2,1)S(1)} collective-permute-done((bf16[128,1024]{1,0:T(8,128)(2,1)S(1)}, bf16[128,1024]{1,0:T(8,128)(2,1)S(1)}, u32[]{:S(2)}, u32[]{:S(2)}) %collective-permute-start.11) | collective-permute-done | bytes 262176 | tf_op jit(solution)/shard_map/ppermute | solution.py:459
  131.1 16.7 %collective-permute-done.17 = bf16[128,1024]{1,0:T(8,128)(2,1)S(1)} collective-permute-done((bf16[128,1024]{1,0:T(8,128)(2,1)S(1)}, bf16[128,1024]{1,0:T(8,128)(2,1)S(1)}, u32[]{:S(2)}, u32[]{:S(2)}) %collective-permute-start.17) | collective-permute-done | bytes 262176 | tf_op jit(solution)/shard_map/ppermute | solution.py:459
  163.5 17.3 %collective-permute-done.14 = bf16[128,1024]{1,0:T(8,128)(2,1)S(1)} collective-permute-done((bf16[128,1024]{1,0:T(8,128)(2,1)S(1)}, bf16[128,1024]{1,0:T(8,128)(2,1)S(1)}, u32[]{:S(2)}, u32[]{:S(2)}) %collective-permute-start.14) | collective-permute-done | bytes 262176 | tf_op jit(solution)/shard_map/ppermute | solution.py:459
  191.0 22.7 %all-to-all-done.2 = bf16[8,136,1024]{2,1,0:T(8,128)(2,1)} async-done(((bf16[8,136,1024]{2,1,0:T(8,128)(2,1)}), bf16[8,136,1024]{2,1,0:T(8,128)(2,1)}, u32[]{:S(2)}, u32[]{:S(2)}) %all-to-all-start.2) | async-done | bytes 2228256 | tf_op jit(solution)/shard_map/all_to_all | solution.py:454
  213.7 33.6 %expert_rows.1 = (bf16[1088,1152]{1,0:T(8,128)(2,1)}, bf16[1088,1024]{1,0:T(8,128)(2,1)}, bf16[1088,1024]{1,0:T(8,128)(2,1)}, bf16[1088,1024]{1,0:T(8,128)(2,1)}...) custom-call(s32[2]{0:T(128)} %pad_add_fusion.1.ids_ref, ...), custom_call_target="tpu_custom_call" | custom-call | flops 20535312384 | bytes 9437184 | tf_op jit(solution)/shard_map/expert_rows/pallas_call | solution.py:634
  247.3 8.1 %all-to-all-start.5 = ((bf16[8,136,1024]{2,1,0:T(8,128)(2,1)}), bf16[8,136,1024]{2,1,0:T(8,128)(2,1)}, u32[]{:S(2)}, u32[]{:S(2)}) async-start(bf16[8,136,1024]{2,1,0:T(8,128)(2,1)} %bitcast.192), calls=%async_computation.5 | async-start | bytes 4456448 | tf_op jit(solution)/shard_map/all_to_all | solution.py:454
  255.8 9.8 %fusion.59 = f32[2048,768]{1,0:T(8,128)} fusion(bf16[1088,2048]{1,0:T(8,128)(2,1)} %get-tuple-element.94, bf16[1088,768]{1,0:T(8,128)(2,1)} %get-tuple-element.95), kind=kOutput, calls=%fused_computation.172 | convolution fusion | flops 3422552064 | bytes 12419072 | tf_op jit(solution)/shard_map/dot_general | solution.py:445
  265.7 14.3 %all-to-all-done.5 = bf16[8,136,1024]{2,1,0:T(8,128)(2,1)} async-done(((bf16[8,136,1024]{2,1,0:T(8,128)(2,1)}), bf16[8,136,1024]{2,1,0:T(8,128)(2,1)}, u32[]{:S(2)}, u32[]{:S(2)}) %all-to-all-start.5) | async-done | bytes 2228256 | tf_op jit(solution)/shard_map/all_to_all | solution.py:454
  280.0 8.0 %all-to-all-start.4 = ((bf16[8,136,1152]{2,1,0:T(8,128)(2,1)}), bf16[8,136,1152]{2,1,0:T(8,128)(2,1)}, u32[]{:S(2)}, u32[]{:S(2)}) async-start(bf16[8,136,1152]{2,1,0:T(8,128)(2,1)} %bitcast.186), calls=%async_computation.4 | async-start | bytes 5013504 | tf_op jit(solution)/shard_map/all_to_all | solution.py:454
  288.0 10.0 %fusion.60 = f32[2048,768]{1,0:T(8,128)} fusion(bf16[1088,2048]{1,0:T(8,128)(2,1)} %get-tuple-element.94, bf16[1088,768]{1,0:T(8,128)(2,1)} %get-tuple-element.99), kind=kOutput, calls=%fused_computation.173 | convolution fusion | flops 3422552064 | bytes 12419072 | tf_op jit(solution)/shard_map/dot_general | solution.py:445
  337.7 15.4 %collective-permute-done.20 = bf16[128,1152]{1,0:T(8,128)(2,1)S(1)} collective-permute-done((bf16[128,1152]{1,0:T(8,128)(2,1)S(1)}, bf16[128,1152]{1,0:T(8,128)(2,1)S(1)}, u32[]{:S(2)}, u32[]{:S(2)}) %collective-permute-start.20) | collective-permute-done | bytes 294944 | tf_op jit(solution)/shard_map/ppermute | solution.py:459
  376.0 12.3 %collective-permute-done.26 = bf16[128,1024]{1,0:T(8,128)(2,1)S(1)} collective-permute-done((bf16[128,1024]{1,0:T(8,128)(2,1)S(1)}, bf16[128,1024]{1,0:T(8,128)(2,1)S(1)}, u32[]{:S(2)}, u32[]{:S(2)}) %collective-permute-start.26) | collective-permute-done | bytes 262176 | tf_op jit(solution)/shard_map/ppermute | solution.py:459
  389.2 12.7 %all-gather.5.cloned.1.call-done.grad_ref = bf16[1024,2048]{1,0:T(8,128)(2,1)} async-done(((bf16[128,2048]{1,0:T(8,128)(2,1)}), bf16[1024,2048]{1,0:T(8,128)(2,1)}) %all-gather.5.cloned.1.call-update) | async-done | bytes 4194320 | tf_op jit(solution)/shard_map/all_gather | solution.py:834
  418.6 20.0 %attend_rows_back.1 = (bf16[1024,512]{1,0:T(8,128)(2,1)}, bf16[1024,256]{1,0:T(8,128)(2,1)}, f32[1,128]{1,0:T(1,128)}, f32[1,128]{1,0:T(1,128)}) custom-call(s32[4]{0:T(128)S(1)} %bitcast.179, bf16[1024,2048]{1,0:T(8,128)(2,1)} %all-gather.5.cloned.1.call-done.grad_ref, bf16[512,2048]{1,0:T(8,128)(2,1)} %out_w_ref.3, ...), custom_call_target="tpu_custom_call" | custom-call | flops 5368709120 | bytes 6291456 | tf_op jit(solution)/shard_map/attend_rows_back/pallas_call | solution.py:385
  446.9 11.9 %collective-permute-done.30 = bf16[128,2048]{1,0:T(8,128)(2,1)} collective-permute-done((bf16[128,2048]{1,0:T(8,128)(2,1)S(1)}, bf16[128,2048]{1,0:T(8,128)(2,1)}, u32[]{:S(2)}, u32[]{:S(2)}) %collective-permute-start.30) | collective-permute-done | bytes 524320 | tf_op jit(solution)/shard_map/ppermute | solution.py:459
  499.5 9.2 %collective-permute-start.31 = (bf16[4,128,2048]{2,1,0:T(8,128)(2,1)S(1)}, bf16[4,128,2048]{2,1,0:T(8,128)(2,1)S(1)}, u32[]{:S(2)}, u32[]{:S(2)}) collective-permute-start(bf16[4,128,2048]{2,1,0:T(8,128)(2,1)S(1)} %convolution_convert_fusion.5), channel_id=1, source_target_pairs={{0,1},{1,0},{2,3},{3,2},{4,5},{5,4},{6,7},{7,6},{8,9},{9,8},{10,11... | collective-permute-start | bytes 6291464 | tf_op jit(solution)/shard_map/ppermute | solution.py:459
  508.7 11.0 %collective-permute-done.44 = bf16[128,2048]{1,0:T(8,128)(2,1)S(1)} collective-permute-done((bf16[128,2048]{1,0:T(8,128)(2,1)}, bf16[128,2048]{1,0:T(8,128)(2,1)S(1)}, u32[]{:S(2)}, u32[]{:S(2)}) %collective-permute-start.44) | collective-permute-done | bytes 524320 | tf_op jit(solution)/shard_map/ppermute | solution.py:494
  521.2 26.1 %collective-permute-done.37 = bf16[128,1024]{1,0:T(8,128)(2,1)S(1)} collective-permute-done((bf16[128,1024]{1,0:T(8,128)(2,1)S(1)}, bf16[128,1024]{1,0:T(8,128)(2,1)S(1)}, u32[]{:S(2)}, u32[]{:S(2)}) %collective-permute-start.37) | collective-permute-done | bytes 262176 | tf_op jit(solution)/shard_map/ppermute | solution.py:459
  551.8 9.1 %collective-permute-done.45 = bf16[128,2048]{1,0:T(8,128)(2,1)S(1)} collective-permute-done((bf16[128,2048]{1,0:T(8,128)(2,1)S(1)}, bf16[128,2048]{1,0:T(8,128)(2,1)S(1)}, u32[]{:S(2)}, u32[]{:S(2)}) %collective-permute-start.45) | collective-permute-done | bytes 524320 | tf_op jit(solution)/shard_map/ppermute | solution.py:494
  584.2 13.9 %all-to-all-done.8 = f32[32,18,128]{2,1,0:T(8,128)S(1)} async-done(((f32[32,18,128]{2,1,0:T(8,128)}), f32[32,18,128]{2,1,0:T(8,128)S(1)}, u32[]{:S(2)}, u32[]{:S(2)}) %all-to-all-start.8) | async-done | bytes 294944 | tf_op jit(solution)/shard_map/all_to_all | solution.py:476
  611.8 10.4 %all-to-all-done.9 = f32[32,18,128]{2,1,0:T(8,128)S(1)} async-done(((f32[32,18,128]{2,1,0:T(8,128)}), f32[32,18,128]{2,1,0:T(8,128)S(1)}, u32[]{:S(2)}, u32[]{:S(2)}) %all-to-all-start.9) | async-done | bytes 294944 | tf_op jit(solution)/shard_map/all_to_all | solution.py:476
  (318 shorter events, 283.7 us)
Async XLA Ops:
  7.2 46.4 %all-gather.3.cloned.1.call-start = ((), (), s32[]{:S(2)}) async-start(), calls=%async_computation.10 | async-start | bytes 4718592 | tf_op jit(solution)/shard_map/all_gather | solution.py:738
  46.7 34.4 %all-to-all-start = ((bf16[8,136,1152]{2,1,0:T(8,128)(2,1)}), bf16[8,136,1152]{2,1,0:T(8,128)(2,1)}, u32[]{:S(2)}, u32[]{:S(2)}) async-start(bf16[8,136,1152]{2,1,0:T(8,128)(2,1)} %bitcast.187), calls=%async_computation | async-start | bytes 5013504 | tf_op jit(solution)/shard_map/all_to_all | solution.py:454
  116.8 33.9 %all-to-all-start.1 = ((bf16[8,136,1024]{2,1,0:T(8,128)(2,1)}), bf16[8,136,1024]{2,1,0:T(8,128)(2,1)}, u32[]{:S(2)}, u32[]{:S(2)}) async-start(bf16[8,136,1024]{2,1,0:T(8,128)(2,1)} %bitcast.190), calls=%async_computation.1 | async-start | bytes 4456448 | tf_op jit(solution)/shard_map/all_to_all | solution.py:454
  150.7 32.9 %all-to-all-start.3 = ((bf16[8,136,1024]{2,1,0:T(8,128)(2,1)}), bf16[8,136,1024]{2,1,0:T(8,128)(2,1)}, u32[]{:S(2)}, u32[]{:S(2)}) async-start(bf16[8,136,1024]{2,1,0:T(8,128)(2,1)} %bitcast.191), calls=%async_computation.3 | async-start | bytes 4456448 | tf_op jit(solution)/shard_map/all_to_all | solution.py:454
  183.6 30.0 %all-to-all-start.2 = ((bf16[8,136,1024]{2,1,0:T(8,128)(2,1)}), bf16[8,136,1024]{2,1,0:T(8,128)(2,1)}, u32[]{:S(2)}, u32[]{:S(2)}) async-start(bf16[8,136,1024]{2,1,0:T(8,128)(2,1)} %bitcast.193), calls=%async_computation.2 | async-start | bytes 4456448 | tf_op jit(solution)/shard_map/all_to_all | solution.py:454
  247.3 32.6 %all-to-all-start.5 = ((bf16[8,136,1024]{2,1,0:T(8,128)(2,1)}), bf16[8,136,1024]{2,1,0:T(8,128)(2,1)}, u32[]{:S(2)}, u32[]{:S(2)}) async-start(bf16[8,136,1024]{2,1,0:T(8,128)(2,1)} %bitcast.192), calls=%async_computation.5 | async-start | bytes 4456448 | tf_op jit(solution)/shard_map/all_to_all | solution.py:454
  280.0 35.6 %all-to-all-start.4 = ((bf16[8,136,1152]{2,1,0:T(8,128)(2,1)}), bf16[8,136,1152]{2,1,0:T(8,128)(2,1)}, u32[]{:S(2)}, u32[]{:S(2)}) async-start(bf16[8,136,1152]{2,1,0:T(8,128)(2,1)} %bitcast.186), calls=%async_computation.4 | async-start | bytes 5013504 | tf_op jit(solution)/shard_map/all_to_all | solution.py:454
  315.5 43.2 %all-to-all-start.6 = ((bf16[8,136,1024]{2,1,0:T(8,128)(2,1)}), bf16[8,136,1024]{2,1,0:T(8,128)(2,1)}, u32[]{:S(2)}, u32[]{:S(2)}) async-start(bf16[8,136,1024]{2,1,0:T(8,128)(2,1)} %bitcast.189), calls=%async_computation.6 | async-start | bytes 4456448 | tf_op jit(solution)/shard_map/all_to_all | solution.py:454
  323.4 78.5 %all-gather.5.cloned.1.call-start = ((), (), s32[]{:S(2)}) async-start(), calls=%async_computation.11 | async-start | bytes 4718592 | tf_op jit(solution)/shard_map/all_gather | solution.py:834
  409.2 29.4 %collective-permute-start.28 = (bf16[128,2048]{1,0:T(8,128)(2,1)}, bf16[128,2048]{1,0:T(8,128)(2,1)}, u32[]{:S(2)}, u32[]{:S(2)}) collective-permute-start(bf16[128,2048]{1,0:T(8,128)(2,1)} %get-tuple-element.153), channel_id=1, source_target_pairs={{0,8},{8,16},{16,24},{24,0},{1,9},{9,17},{17,25},{25,1},{2,10},{10... | collective-permute-start | bytes 1572872 | tf_op jit(solution)/shard_map/ppermute | solution.py:459
  410.4 28.2 %collective-permute-start.29 = (bf16[128,2048]{1,0:T(8,128)(2,1)}, bf16[128,2048]{1,0:T(8,128)(2,1)}, u32[]{:S(2)}, u32[]{:S(2)}) collective-permute-start(bf16[128,2048]{1,0:T(8,128)(2,1)} %get-tuple-element.152), channel_id=1, source_target_pairs={{0,24},{8,0},{16,8},{24,16},{1,25},{9,1},{17,9},{25,17},{2,26},{10... | collective-permute-start | bytes 1572872 | tf_op jit(solution)/shard_map/ppermute | solution.py:459
  412.5 46.4 %collective-permute-start.30 = (bf16[128,2048]{1,0:T(8,128)(2,1)S(1)}, bf16[128,2048]{1,0:T(8,128)(2,1)}, u32[]{:S(2)}, u32[]{:S(2)}) collective-permute-start(bf16[128,2048]{1,0:T(8,128)(2,1)S(1)} %get-tuple-element.151), channel_id=1, source_target_pairs={{0,16},{8,24},{16,0},{24,8},{1,17},{9,25},{17,1},{25,9},{2,18},{10... | collective-permute-start | bytes 1572872 | tf_op jit(solution)/shard_map/ppermute | solution.py:459
  412.8 48.9 %all-to-all-start.7 = ((bf16[8,136,1024]{2,1,0:T(8,128)(2,1)}), bf16[8,136,1024]{2,1,0:T(8,128)(2,1)}, u32[]{:S(2)}, u32[]{:S(2)}) async-start(bf16[8,136,1024]{2,1,0:T(8,128)(2,1)} %bitcast.188), calls=%async_computation.7 | async-start | bytes 4456448 | tf_op jit(solution)/shard_map/all_to_all | solution.py:454
  418.1 204.9 %all-reduce.5.cloned.1.call-start = ((), (), s32[]{:S(2)}) async-start(), calls=%async_computation.12 | async-start | bytes 5242880 | tf_op jit(solution)/shard_map/psum | solution.py:884
  481.2 38.5 %collective-permute-start.44 = (bf16[128,2048]{1,0:T(8,128)(2,1)}, bf16[128,2048]{1,0:T(8,128)(2,1)S(1)}, u32[]{:S(2)}, u32[]{:S(2)}) collective-permute-start(bf16[128,2048]{1,0:T(8,128)(2,1)} %collective-permute-done.43), channel_id=1, source_target_pairs={{16,8},{8,0},{17,9},{9,1},{18,10},{10,2},{19,11},{11,3},{20,12},{1... | collective-permute-start | bytes 1572872 | tf_op jit(solution)/shard_map/ppermute | solution.py:494
  488.0 59.2 %collective-permute-start.37 = (bf16[128,1024]{1,0:T(8,128)(2,1)S(1)}, bf16[128,1024]{1,0:T(8,128)(2,1)S(1)}, u32[]{:S(2)}, u32[]{:S(2)}) collective-permute-start(bf16[128,1024]{1,0:T(8,128)(2,1)S(1)} %get-tuple-element.172), channel_id=1, source_target_pairs={{0,16},{8,24},{16,0},{24,8},{1,17},{9,25},{17,1},{25,9},{2,18},{10... | collective-permute-start | bytes 786440 | tf_op jit(solution)/shard_map/ppermute | solution.py:459
  488.1 59.2 %collective-permute-start.36 = (bf16[128,1024]{1,0:T(8,128)(2,1)S(1)}, bf16[128,1024]{1,0:T(8,128)(2,1)S(1)}, u32[]{:S(2)}, u32[]{:S(2)}) collective-permute-start(bf16[128,1024]{1,0:T(8,128)(2,1)S(1)} %get-tuple-element.170), channel_id=1, source_target_pairs={{0,24},{8,0},{16,8},{24,16},{1,25},{9,1},{17,9},{25,17},{2,26},{10... | collective-permute-start | bytes 786440 | tf_op jit(solution)/shard_map/ppermute | solution.py:459
  490.2 58.0 %collective-permute-start.42 = (bf16[128,2048]{1,0:T(8,128)(2,1)S(1)}, bf16[128,2048]{1,0:T(8,128)(2,1)S(1)}, u32[]{:S(2)}, u32[]{:S(2)}) collective-permute-start(bf16[128,2048]{1,0:T(8,128)(2,1)S(1)} %collective-permute-done.41), channel_id=1, source_target_pairs={{16,24},{17,25},{18,26},{19,27},{20,28},{21,29},{22,30},{23,31}} | collective-permute-start | bytes 1572872 | tf_op jit(solution)/shard_map/ppermute | solution.py:494
  499.5 66.8 %collective-permute-start.31 = (bf16[4,128,2048]{2,1,0:T(8,128)(2,1)S(1)}, bf16[4,128,2048]{2,1,0:T(8,128)(2,1)S(1)}, u32[]{:S(2)}, u32[]{:S(2)}) collective-permute-start(bf16[4,128,2048]{2,1,0:T(8,128)(2,1)S(1)} %convolution_convert_fusion.5), channel_id=1, source_target_pairs={{0,1},{1,0},{2,3},{3,2},{4,5},{5,4},{6,7},{7,6},{8,9},{9,8},{10,11... | collective-permute-start | bytes 6291464 | tf_op jit(solution)/shard_map/ppermute | solution.py:459
  519.7 41.3 %collective-permute-start.45 = (bf16[128,2048]{1,0:T(8,128)(2,1)S(1)}, bf16[128,2048]{1,0:T(8,128)(2,1)S(1)}, u32[]{:S(2)}, u32[]{:S(2)}) collective-permute-start(bf16[128,2048]{1,0:T(8,128)(2,1)S(1)} %collective-permute-done.44), channel_id=1, source_target_pairs={{8,0},{9,1},{10,2},{11,3},{12,4},{13,5},{14,6},{15,7}} | collective-permute-start | bytes 1572872 | tf_op jit(solution)/shard_map/ppermute | solution.py:494
  570.3 27.9 %all-to-all-start.8 = ((f32[32,18,128]{2,1,0:T(8,128)}), f32[32,18,128]{2,1,0:T(8,128)S(1)}, u32[]{:S(2)}, u32[]{:S(2)}) async-start(f32[32,18,128]{2,1,0:T(8,128)} %reshape.404), calls=%async_computation.8 | async-start | bytes 786432 | tf_op jit(solution)/shard_map/all_to_all | solution.py:476
  579.3 27.6 %collective-permute-start.34 = (bf16[128,2048]{1,0:T(8,128)(2,1)}, bf16[128,2048]{1,0:T(8,128)(2,1)}, u32[]{:S(2)}, u32[]{:S(2)}) collective-permute-start(bf16[128,2048]{1,0:T(8,128)(2,1)} %get-tuple-element.149), channel_id=1, source_target_pairs={{0,6},{2,0},{4,2},{6,4},{1,7},{3,1},{5,3},{7,5},{8,14},{10,8},{12,... | collective-permute-start | bytes 1572872 | tf_op jit(solution)/shard_map/ppermute | solution.py:459
  581.5 27.5 %collective-permute-start.33 = (bf16[128,2048]{1,0:T(8,128)(2,1)}, bf16[128,2048]{1,0:T(8,128)(2,1)}, u32[]{:S(2)}, u32[]{:S(2)}) collective-permute-start(bf16[128,2048]{1,0:T(8,128)(2,1)} %get-tuple-element.150), channel_id=1, source_target_pairs={{0,4},{2,6},{4,0},{6,2},{1,5},{3,7},{5,1},{7,3},{8,12},{10,14},{12... | collective-permute-start | bytes 1572872 | tf_op jit(solution)/shard_map/ppermute | solution.py:459
  581.8 27.2 %collective-permute-start.32 = (bf16[128,2048]{1,0:T(8,128)(2,1)}, bf16[128,2048]{1,0:T(8,128)(2,1)}, u32[]{:S(2)}, u32[]{:S(2)}) collective-permute-start(bf16[128,2048]{1,0:T(8,128)(2,1)} %get-tuple-element.148), channel_id=1, source_target_pairs={{0,2},{2,4},{4,6},{6,0},{1,3},{3,5},{5,7},{7,1},{8,10},{10,12},{12... | collective-permute-start | bytes 1572872 | tf_op jit(solution)/shard_map/ppermute | solution.py:459
  (81 other events, 1103.4 us)
Sparse Core Ops, SparseCore 0:
  10.7 39.2 all-gather.2
  358.9 42.8 all-gather.4
  468.5 151.7 all-reduce.4

commit v4 on v3

--- a/solution.py
+++ b/solution.py
@@ -11,6 +11,8 @@
 rope_base = 1000000.0
 highest = lax.Precision.HIGHEST
 chunk_count = 2
+grads_first = 7
+weighted_first = 9
 expert_steps = 2
 expert_vmem = 56 * 1024 * 1024
 kernel_vmem = 40 * 1024 * 1024
@@ -468,6 +470,10 @@
     return [parts[0]] + [rotate(parts[k], "expert", -k) for k in range(1, parts.shape[0])]
 
 
+def parts_of(width, sixteenths):
+    return [width * sixteenths // 16, width - width * sixteenths // 16]
+
+
 def together(*values):
     return lax.optimization_barrier(values)
 
@@ -554,16 +560,36 @@
     return result
 
 
-def expert_kernel(ids_ref, router_ref, gate_ref, up_ref, down_ref, *refs, count, experts):
-    rows_refs = refs[:count]
-    grads_refs = refs[count : 2 * count]
-    sends = refs[2 * count : 3 * count]
-    weighted = refs[3 * count : 4 * count]
-    rows_out, grads_out, hidden_out, grad_gate_out, grad_up_out = refs[4 * count :]
-    width = rows_refs[1].shape[1]
+def split_columns(refs, widths, low, high):
+    base = 0
+    for ref, width in zip(refs, widths):
+        first, last = max(low, base), min(high, base + width)
+        if first < last:
+            yield ref, slice(first - base, last - base), slice(first - low, last - low)
+        base += width
+
+
+def expert_kernel(
+    ids_ref,
+    router_ref,
+    gate_ref,
+    up_ref,
+    down_ref,
+    *refs,
+    count,
+    grads_widths,
+    weighted_widths,
+    experts,
+):
+    rows_refs, refs = refs[:count], refs[count:]
+    grads_refs, refs = refs[: len(grads_widths)], refs[len(grads_widths) :]
+    sends, refs = refs[:count], refs[count:]
+    weighted, refs = refs[: len(weighted_widths)], refs[len(weighted_widths) :]
+    rows_out, grads_out, hidden_out, grad_gate_out, grad_up_out = refs
+    width = rows_refs[0].shape[1]
     cuts = [slice(i * width, (i + 1) * width) for i in range(count)]
     rows = [ref[...] for ref in rows_refs]
-    chosen = grads_refs[0][:, width:].astype(jnp.float32) > 0.5
+    chosen = grads_refs[0][:, grads_widths[0] :].astype(jnp.float32) > 0.5
     lanes = lax.broadcasted_iota(jnp.int32, chosen.shape, 1)
 
     def times(weights_ref):
@@ -588,9 +614,17 @@
     for i, cut in enumerate(cuts):
         out = jnp.dot(hidden, down_ref[:, cut], preferred_element_type=jnp.float32)
         out = out.astype(jnp.bfloat16).astype(jnp.float32)
-        grads = grads_refs[i][:, :width].astype(jnp.float32)
+        grads = jnp.concatenate(
+            [
+                ref[:, part].astype(jnp.float32)
+                for ref, part, _ in split_columns(grads_refs, grads_widths, cut.start, cut.stop)
+            ],
+            axis=1,
+        )
         dots = dots + jnp.sum(out * grads, axis=1, keepdims=True)
-        weighted[i][...] = (out * gates).astype(jnp.bfloat16)
+        gated = (out * gates).astype(jnp.bfloat16)
+        for ref, part, own in split_columns(weighted, weighted_widths, cut.start, cut.stop):
+            ref[:, part] = gated[:, own]
         grads_low = (grads * gates).astype(jnp.bfloat16)
         grads_out[:, cut] = grads_low
         rows_out[:, cut] = rows[i]
@@ -612,11 +646,13 @@
     sends[0][:, width:] = side.astype(jnp.bfloat16)
 
 
-def expert_rows(ids, w_router, w_gate, w_up, w_down, rows, grads, plane_size):
+def expert_rows(
+    ids, w_router, w_gate, w_up, w_down, rows, grads, grads_widths, weighted_widths, plane_size
+):
     count = len(rows)
     slots, width = rows[0].shape
     model_width, hidden = w_gate.shape
-    side = grads[0].shape[1] - width
+    side = grads[0].shape[1] - grads_widths[0]
     block = slots // expert_steps
 
     def tile(columns):
@@ -629,15 +665,21 @@
         return pltpu.HBM((slots, columns), jnp.bfloat16)
 
     sides = [width + side] + [width] * (count - 1)
-    outs = sides + [width] * count + [model_width, model_width, hidden, hidden, hidden]
+    outs = sides + list(weighted_widths) + [model_width, model_width, hidden, hidden, hidden]
     flops = 2 * slots * model_width * hidden * 6
     return pl.pallas_call(
-        functools.partial(expert_kernel, count=count, experts=plane_size),
+        functools.partial(
+            expert_kernel,
+            count=count,
+            grads_widths=tuple(grads_widths),
+            weighted_widths=tuple(weighted_widths),
+            experts=plane_size,
+        ),
         grid=(expert_steps,),
         in_specs=[pl.BlockSpec(memory_space=pltpu.SMEM)]
         + [whole(array) for array in (w_router, w_gate, w_up, w_down)]
         + [tile(width)] * count
-        + [tile(columns) for columns in sides],
+        + [tile(array.shape[1]) for array in grads],
         out_specs=[tile(columns) for columns in outs],
         out_shape=[shape(columns) for columns in outs],
         compiler_params=pltpu.CompilerParams(vmem_limit_bytes=expert_vmem),
@@ -722,7 +764,9 @@
     chunk_width = model_width // chunk_count
     chunks = [slice(i * chunk_width, (i + 1) * chunk_width) for i in range(chunk_count)]
     side_width = 128
-    grad_planes = [gather_rows(out_grad[:, cut]) for cut in chunks]
+    grads_widths = parts_of(model_width, grads_first)
+    weighted_widths = parts_of(model_width, weighted_first)
+    grad_planes = [gather_rows(part) for part in jnp.split(out_grad, [grads_widths[0]], axis=1)]
     grad_planes[0] = jnp.concatenate(
         [grad_planes[0], jnp.pad(chosen_all, ((0, 0), (0, side_width - experts)))], axis=1
     )
@@ -774,12 +818,14 @@
         w_down[0],
         slot_chunks,
         grad_slot_chunks,
+        grads_widths,
+        weighted_widths,
         plane_size,
     )
     grad_sends = expert_outs[:chunk_count]
-    out_sends = expert_outs[chunk_count : 2 * chunk_count]
+    out_sends = expert_outs[chunk_count : chunk_count + len(weighted_widths)]
     moe_slots, grad_out_slots, hidden_low, grad_gate_pre, grad_up_pre = expert_outs[
-        2 * chunk_count :
+        chunk_count + len(weighted_widths) :
     ]
 
     def to_source(returned):
@@ -894,15 +940,15 @@
         )
 
     out_share = add_parts(out_terms).astype(jnp.bfloat16)
-    left_parts, out_share, *out_returns[1:] = together(left_parts, out_share, *out_returns[1:])
-    out_shares = spread_planes(out_share)
-    out_parts = [out_first] + [add_parts(to_source(part)) for part in out_returns[1:]]
-    col_sums = scatter_cols(grad_normed_rows)
     summed_values = jnp.concatenate(
         [grad_router.reshape(-1), grad_norm_moe, norm_terms, grad_q_gain[0], grad_k_gain[0]]
     )
-    col_sums, summed_values = together(col_sums, summed_values)
+    left_parts, out_share, summed_values = together(left_parts, out_share, summed_values)
     sums = sum_all(summed_values)
+    out_shares = spread_planes(out_share)
+    col_sums = scatter_cols(grad_normed_rows)
+    col_sums, *out_returns[1:] = together(col_sums, *out_returns[1:])
+    out_parts = [out_first] + [add_parts(to_source(part)) for part in out_returns[1:]]
     grad_normed = scatter_rows(col_sums)
     grad_normed, sums, query_kv, *out_parts = together(grad_normed, sums, query_kv, *out_parts)
     out_rows = (mixed_rows + jnp.concatenate(out_parts, axis=1)).astype(jnp.bfloat16)

time: 656 us -> 641 us (0.977)
  waiting for transfers between devices: 282 us -> 256 us
  starting transfers between devices: 131 us -> 138 us
    psum x1, waiting for transfers between devices: 0.01 us -> 44.2 us  [local(): query_kv = lax.psum(query_kv, 'expert')]
    ppermute x6, waiting for transfers between devices: 32.2 us -> 9.14 us  [line_step(): return lax.ppermute(value, 'expert', pairs)]
    ppermute x40, waiting for transfers between devices: 162 us -> 139 us  [rotate(): lax.ppermute(block, axis, [(i, (i + step) % size) for i in range(size)])]
    all_to_all x2, waiting for transfers between devices: 24.4 us -> 6.28 us  [move_all(): lax.all_to_all(parts, ('expert',) + plane_axes, split_axis=0, concat_axis...]
  transfers between devices with their start and end apart: 59 -> 59, of which waited for: 27 -> 28; matrix products, arithmetic and copies ran while one was open for 19% -> 20% of each run, Pallas kernels for 6% -> 6%
where the time goes in v4:
time: 641 us; the launch traced here: 632 us
  waiting for transfers between devices  256 us (40%)
  starting transfers between devices  138 us (22%)
  matrix products  76.6 us (12%)
  Pallas kernels  71.7 us (11%)
  other arithmetic  54.8 us (9%)
  local copies, waits for them, and re-layouts  20.4 us (3%)
  between operations  14.9 us (2%)
    ppermute x40, waiting for transfers between devices, rotate(): lax.ppermute(block, axis, [(i, (i + step) % size) for i in range(size)])  139 us
    ppermute x40, starting transfers between devices, rotate(): lax.ppermute(block, axis, [(i, (i + step) % size) for i in range(size)])  64.3 us
    all_to_all x8, starting transfers between devices, move_plane(): lax.all_to_all(parts, plane_axes, split_axis=0, concat_axis=0, tiled=True)  54.8 us
    all_to_all x8, waiting for transfers between devices, move_plane(): lax.all_to_all(parts, plane_axes, split_axis=0, concat_axis=0, tiled=True)  44.8 us
    psum x1, waiting for transfers between devices, local(): query_kv = lax.psum(query_kv, 'expert')  44.2 us
    dot_general x6, matrix products, transposed_times(): lax.dot_general(left, right, (((0,), (0,)), ((), ())), preferred_element_...  38.6 us
    pallas_call x1, Pallas kernels, expert_rows(): pl.pallas_call(functools.partial(expert_kernel, count=count, grads_widths...  34.1 us
    pallas_call x1, Pallas kernels, attend_rows_back(): pl.pallas_call(functools.partial(attend_back_kernel, head_dim=head_dim),...  20 us
  transfers between devices with their start and end apart: 59, of which 28 were waited for; matrix products, arithmetic and copies ran while one was open for 20% of the time, Pallas kernels for 6%

profile of v4, /device:TPU:1, one launch (start us, length us, event | category | flops | bytes accessed | tf_op | source)
XLA Modules:
  0.0 631.6 jit_solution(13073289976935020720)
XLA Ops:
  29.3 9.3 %collective-permute-done.4 = bf16[128,896]{1,0:T(8,128)(2,1)S(1)} collective-permute-done((bf16[128,896]{1,0:T(8,128)(2,1)S(1)}, bf16[128,896]{1,0:T(8,128)(2,1)S(1)}, u32[]{:S(2)}, u32[]{:S(2)}) %collective-permute-start.4) | collective-permute-done | bytes 229408 | tf_op jit(solution)/shard_map/ppermute | solution.py:461
  41.4 6.8 %all-to-all-start = ((bf16[8,136,1024]{2,1,0:T(8,128)(2,1)}), bf16[8,136,1024]{2,1,0:T(8,128)(2,1)}, u32[]{:S(2)}, u32[]{:S(2)}) async-start(bf16[8,136,1024]{2,1,0:T(8,128)(2,1)} %bitcast.192), calls=%async_computation | async-start | bytes 4456448 | tf_op jit(solution)/shard_map/all_to_all | solution.py:456
  49.9 17.6 %attend_rows.1 = (bf16[512,2048]{1,0:T(8,128)(2,1)}, bf16[512,2048]{1,0:T(8,128)(2,1)}, bf16[1024,512]{1,0:T(8,128)(2,1)}, bf16[1024,128]{1,0:T(8,128)(2,1)}, bf...) custom-call(s32[4]{0:T(128)S(1)} %bitcast.178, ...), custom_call_target="tpu_custom_call" | custom-call | flops 6979321856 | bytes 12582912 | tf_op jit(solution)/shard_map/attend_rows/pallas_call | solution.py:184
  85.7 18.3 %collective-permute-done.11 = bf16[128,1152]{1,0:T(8,128)(2,1)S(1)} collective-permute-done((bf16[128,1152]{1,0:T(8,128)(2,1)S(1)}, bf16[128,1152]{1,0:T(8,128)(2,1)S(1)}, u32[]{:S(2)}, u32[]{:S(2)}) %collective-permute-start.11) | collective-permute-done | bytes 294944 | tf_op jit(solution)/shard_map/ppermute | solution.py:461
  123.3 16.8 %collective-permute-done.17 = bf16[128,1024]{1,0:T(8,128)(2,1)S(1)} collective-permute-done((bf16[128,1024]{1,0:T(8,128)(2,1)S(1)}, bf16[128,1024]{1,0:T(8,128)(2,1)S(1)}, u32[]{:S(2)}, u32[]{:S(2)}) %collective-permute-start.17) | collective-permute-done | bytes 262176 | tf_op jit(solution)/shard_map/ppermute | solution.py:461
  143.0 7.0 %all-to-all-start.3 = ((bf16[8,136,1024]{2,1,0:T(8,128)(2,1)}), bf16[8,136,1024]{2,1,0:T(8,128)(2,1)}, u32[]{:S(2)}, u32[]{:S(2)}) async-start(bf16[8,136,1024]{2,1,0:T(8,128)(2,1)} %bitcast.189), calls=%async_computation.3 | async-start | bytes 4456448 | tf_op jit(solution)/shard_map/all_to_all | solution.py:456
  157.8 16.9 %collective-permute-done.14 = bf16[128,1024]{1,0:T(8,128)(2,1)S(1)} collective-permute-done((bf16[128,1024]{1,0:T(8,128)(2,1)S(1)}, bf16[128,1024]{1,0:T(8,128)(2,1)S(1)}, u32[]{:S(2)}, u32[]{:S(2)}) %collective-permute-start.14) | collective-permute-done | bytes 262176 | tf_op jit(solution)/shard_map/ppermute | solution.py:461
  184.9 22.7 %all-to-all-done.2 = bf16[8,136,1024]{2,1,0:T(8,128)(2,1)} async-done(((bf16[8,136,1024]{2,1,0:T(8,128)(2,1)}), bf16[8,136,1024]{2,1,0:T(8,128)(2,1)}, u32[]{:S(2)}, u32[]{:S(2)}) %all-to-all-start.2) | async-done | bytes 2228256 | tf_op jit(solution)/shard_map/all_to_all | solution.py:456
  207.6 34.1 %expert_rows.1 = (bf16[1088,1152]{1,0:T(8,128)(2,1)}, bf16[1088,1024]{1,0:T(8,128)(2,1)}, bf16[1088,1152]{1,0:T(8,128)(2,1)}, bf16[1088,896]{1,0:T(8,128)(2,1)},...) custom-call(s32[2]{0:T(128)} %pad_add_fusion.1.ids_ref, ...), custom_call_target="tpu_custom_call" | custom-call | flops 20535312384 | bytes 9437184 | tf_op jit(solution)/shard_map/expert_rows/pallas_call | solution.py:670
  241.7 8.1 %all-to-all-start.5 = ((bf16[8,136,1024]{2,1,0:T(8,128)(2,1)}), bf16[8,136,1024]{2,1,0:T(8,128)(2,1)}, u32[]{:S(2)}, u32[]{:S(2)}) async-start(bf16[8,136,1024]{2,1,0:T(8,128)(2,1)} %bitcast.190), calls=%async_computation.5 | async-start | bytes 4456448 | tf_op jit(solution)/shard_map/all_to_all | solution.py:456
  250.2 9.8 %fusion.59 = f32[2048,768]{1,0:T(8,128)} fusion(bf16[1088,2048]{1,0:T(8,128)(2,1)} %get-tuple-element.94, bf16[1088,768]{1,0:T(8,128)(2,1)} %get-tuple-element.95), kind=kOutput, calls=%fused_computation.172 | convolution fusion | flops 3422552064 | bytes 12419072 | tf_op jit(solution)/shard_map/dot_general | solution.py:447
  260.0 14.3 %all-to-all-done.5 = bf16[8,136,1024]{2,1,0:T(8,128)(2,1)} async-done(((bf16[8,136,1024]{2,1,0:T(8,128)(2,1)}), bf16[8,136,1024]{2,1,0:T(8,128)(2,1)}, u32[]{:S(2)}, u32[]{:S(2)}) %all-to-all-start.5) | async-done | bytes 2228256 | tf_op jit(solution)/shard_map/all_to_all | solution.py:456
  274.3 8.0 %all-to-all-start.4 = ((bf16[8,136,1152]{2,1,0:T(8,128)(2,1)}), bf16[8,136,1152]{2,1,0:T(8,128)(2,1)}, u32[]{:S(2)}, u32[]{:S(2)}) async-start(bf16[8,136,1152]{2,1,0:T(8,128)(2,1)} %bitcast.187), calls=%async_computation.4 | async-start | bytes 5013504 | tf_op jit(solution)/shard_map/all_to_all | solution.py:456
  282.4 10.0 %fusion.60 = f32[2048,768]{1,0:T(8,128)} fusion(bf16[1088,2048]{1,0:T(8,128)(2,1)} %get-tuple-element.94, bf16[1088,768]{1,0:T(8,128)(2,1)} %get-tuple-element.99), kind=kOutput, calls=%fused_computation.173 | convolution fusion | flops 3422552064 | bytes 12419072 | tf_op jit(solution)/shard_map/dot_general | solution.py:447
  309.9 7.9 %all-to-all-start.6 = ((bf16[8,136,1152]{2,1,0:T(8,128)(2,1)}), bf16[8,136,1152]{2,1,0:T(8,128)(2,1)}, u32[]{:S(2)}, u32[]{:S(2)}) async-start(bf16[8,136,1152]{2,1,0:T(8,128)(2,1)} %bitcast.186), calls=%async_computation.6 | async-start | bytes 5013504 | tf_op jit(solution)/shard_map/all_to_all | solution.py:456
  332.1 15.7 %collective-permute-done.20 = bf16[128,1152]{1,0:T(8,128)(2,1)S(1)} collective-permute-done((bf16[128,1152]{1,0:T(8,128)(2,1)S(1)}, bf16[128,1152]{1,0:T(8,128)(2,1)S(1)}, u32[]{:S(2)}, u32[]{:S(2)}) %collective-permute-start.20) | collective-permute-done | bytes 294944 | tf_op jit(solution)/shard_map/ppermute | solution.py:461
  357.8 6.5 %collective-permute-start.27 = (bf16[128,1152]{1,0:T(8,128)(2,1)S(1)}, bf16[128,1152]{1,0:T(8,128)(2,1)S(1)}, u32[]{:S(2)}, u32[]{:S(2)}) collective-permute-start(bf16[128,1152]{1,0:T(8,128)(2,1)S(1)} %get-tuple-element.158), channel_id=1, source_target_pairs={{0,8},{8,16},{16,24},{24,0},{1,9},{9,17},{17,25},{25,1},{2,10},{10... | collective-permute-start | bytes 884744 | tf_op jit(solution)/shard_map/ppermute | solution.py:461
  372.5 13.7 %collective-permute-done.26 = bf16[128,1152]{1,0:T(8,128)(2,1)S(1)} collective-permute-done((bf16[128,1152]{1,0:T(8,128)(2,1)S(1)}, bf16[128,1152]{1,0:T(8,128)(2,1)S(1)}, u32[]{:S(2)}, u32[]{:S(2)}) %collective-permute-start.26) | collective-permute-done | bytes 294944 | tf_op jit(solution)/shard_map/ppermute | solution.py:461
  387.2 10.2 %all-gather.5.cloned.1.call-done.grad_ref = bf16[1024,2048]{1,0:T(8,128)(2,1)} async-done(((bf16[128,2048]{1,0:T(8,128)(2,1)}), bf16[1024,2048]{1,0:T(8,128)(2,1)}) %all-gather.5.cloned.1.call-update) | async-done | bytes 4194320 | tf_op jit(solution)/shard_map/all_gather | solution.py:880
  406.5 20.0 %attend_rows_back.1 = (bf16[1024,512]{1,0:T(8,128)(2,1)}, bf16[1024,256]{1,0:T(8,128)(2,1)}, f32[1,128]{1,0:T(1,128)}, f32[1,128]{1,0:T(1,128)}) custom-call(s32[4]{0:T(128)S(1)} %bitcast.179, bf16[1024,2048]{1,0:T(8,128)(2,1)} %all-gather.5.cloned.1.call-done.grad_ref, bf16[512,2048]{1,0:T(8,128)(2,1)} %out_w_ref.3, ...), custom_call_target="tpu_custom_call" | custom-call | flops 5368709120 | bytes 6291456 | tf_op jit(solution)/shard_map/attend_rows_back/pallas_call | solution.py:387
  438.7 13.1 %collective-permute-done.30 = bf16[128,2048]{1,0:T(8,128)(2,1)S(1)} collective-permute-done((bf16[128,2048]{1,0:T(8,128)(2,1)S(1)}, bf16[128,2048]{1,0:T(8,128)(2,1)S(1)}, u32[]{:S(2)}, u32[]{:S(2)}) %collective-permute-start.30) | collective-permute-done | bytes 524320 | tf_op jit(solution)/shard_map/ppermute | solution.py:461
  491.7 6.3 all-to-all-done.9
  508.8 6.9 %collective-permute-done.45 = bf16[128,2048]{1,0:T(8,128)(2,1)S(1)} collective-permute-done((bf16[128,2048]{1,0:T(8,128)(2,1)}, bf16[128,2048]{1,0:T(8,128)(2,1)S(1)}, u32[]{:S(2)}, u32[]{:S(2)}) %collective-permute-start.45) | collective-permute-done | bytes 524320 | tf_op jit(solution)/shard_map/ppermute | solution.py:500
  563.5 44.2 %all-reduce.5.cloned.1.call-done = bf16[2560,512]{1,0:T(8,128)(2,1)} async-done(((bf16[2560,512]{1,0:T(8,128)(2,1)}), bf16[2560,512]{1,0:T(8,128)(2,1)}) %all-reduce.5.cloned.1.call-update) | async-done | bytes 2621456 | tf_op jit(solution)/shard_map/psum | solution.py:930
  (329 shorter events, 272.6 us)
Async XLA Ops:
  7.2 42.7 %all-gather.3.cloned.1.call-start = ((), (), s32[]{:S(2)}) async-start(), calls=%async_computation.10 | async-start | bytes 4718592 | tf_op jit(solution)/shard_map/all_gather | solution.py:782
  41.4 31.3 %all-to-all-start = ((bf16[8,136,1024]{2,1,0:T(8,128)(2,1)}), bf16[8,136,1024]{2,1,0:T(8,128)(2,1)}, u32[]{:S(2)}, u32[]{:S(2)}) async-start(bf16[8,136,1024]{2,1,0:T(8,128)(2,1)} %bitcast.192), calls=%async_computation | async-start | bytes 4456448 | tf_op jit(solution)/shard_map/all_to_all | solution.py:456
  76.8 27.2 %collective-permute-start.11 = (bf16[128,1152]{1,0:T(8,128)(2,1)S(1)}, bf16[128,1152]{1,0:T(8,128)(2,1)S(1)}, u32[]{:S(2)}, u32[]{:S(2)}) collective-permute-start(bf16[128,1152]{1,0:T(8,128)(2,1)S(1)} %get-tuple-element.186), channel_id=1, source_target_pairs={{0,16},{8,24},{16,0},{24,8},{1,17},{9,25},{17,1},{25,9},{2,18},{10... | collective-permute-start | bytes 884744 | tf_op jit(solution)/shard_map/ppermute | solution.py:461
  77.8 26.3 %collective-permute-start.10 = (bf16[128,1152]{1,0:T(8,128)(2,1)S(1)}, bf16[128,1152]{1,0:T(8,128)(2,1)S(1)}, u32[]{:S(2)}, u32[]{:S(2)}) collective-permute-start(bf16[128,1152]{1,0:T(8,128)(2,1)S(1)} %get-tuple-element.186), channel_id=1, source_target_pairs={{0,8},{8,16},{16,24},{24,0},{1,9},{9,17},{17,25},{25,1},{2,10},{10... | collective-permute-start | bytes 884744 | tf_op jit(solution)/shard_map/ppermute | solution.py:461
  108.4 34.5 %all-to-all-start.1 = ((bf16[8,136,1152]{2,1,0:T(8,128)(2,1)}), bf16[8,136,1152]{2,1,0:T(8,128)(2,1)}, u32[]{:S(2)}, u32[]{:S(2)}) async-start(bf16[8,136,1152]{2,1,0:T(8,128)(2,1)} %bitcast.188), calls=%async_computation.1 | async-start | bytes 5013504 | tf_op jit(solution)/shard_map/all_to_all | solution.py:456
  143.0 34.6 %all-to-all-start.3 = ((bf16[8,136,1024]{2,1,0:T(8,128)(2,1)}), bf16[8,136,1024]{2,1,0:T(8,128)(2,1)}, u32[]{:S(2)}, u32[]{:S(2)}) async-start(bf16[8,136,1024]{2,1,0:T(8,128)(2,1)} %bitcast.189), calls=%async_computation.3 | async-start | bytes 4456448 | tf_op jit(solution)/shard_map/all_to_all | solution.py:456
  151.0 23.7 %collective-permute-start.14 = (bf16[128,1024]{1,0:T(8,128)(2,1)S(1)}, bf16[128,1024]{1,0:T(8,128)(2,1)S(1)}, u32[]{:S(2)}, u32[]{:S(2)}) collective-permute-start(bf16[128,1024]{1,0:T(8,128)(2,1)S(1)} %get-tuple-element.184), channel_id=1, source_target_pairs={{0,16},{8,24},{16,0},{24,8},{1,17},{9,25},{17,1},{25,9},{2,18},{10... | collective-permute-start | bytes 786440 | tf_op jit(solution)/shard_map/ppermute | solution.py:461
  177.5 30.1 %all-to-all-start.2 = ((bf16[8,136,1024]{2,1,0:T(8,128)(2,1)}), bf16[8,136,1024]{2,1,0:T(8,128)(2,1)}, u32[]{:S(2)}, u32[]{:S(2)}) async-start(bf16[8,136,1024]{2,1,0:T(8,128)(2,1)} %bitcast.191), calls=%async_computation.2 | async-start | bytes 4456448 | tf_op jit(solution)/shard_map/all_to_all | solution.py:456
  241.7 32.6 %all-to-all-start.5 = ((bf16[8,136,1024]{2,1,0:T(8,128)(2,1)}), bf16[8,136,1024]{2,1,0:T(8,128)(2,1)}, u32[]{:S(2)}, u32[]{:S(2)}) async-start(bf16[8,136,1024]{2,1,0:T(8,128)(2,1)} %bitcast.190), calls=%async_computation.5 | async-start | bytes 4456448 | tf_op jit(solution)/shard_map/all_to_all | solution.py:456
  274.3 35.6 %all-to-all-start.4 = ((bf16[8,136,1152]{2,1,0:T(8,128)(2,1)}), bf16[8,136,1152]{2,1,0:T(8,128)(2,1)}, u32[]{:S(2)}, u32[]{:S(2)}) async-start(bf16[8,136,1152]{2,1,0:T(8,128)(2,1)} %bitcast.187), calls=%async_computation.4 | async-start | bytes 5013504 | tf_op jit(solution)/shard_map/all_to_all | solution.py:456
  309.9 43.5 %all-to-all-start.6 = ((bf16[8,136,1152]{2,1,0:T(8,128)(2,1)}), bf16[8,136,1152]{2,1,0:T(8,128)(2,1)}, u32[]{:S(2)}, u32[]{:S(2)}) async-start(bf16[8,136,1152]{2,1,0:T(8,128)(2,1)} %bitcast.186), calls=%async_computation.6 | async-start | bytes 5013504 | tf_op jit(solution)/shard_map/all_to_all | solution.py:456
  317.8 79.5 %all-gather.5.cloned.1.call-start = ((), (), s32[]{:S(2)}) async-start(), calls=%async_computation.11 | async-start | bytes 4718592 | tf_op jit(solution)/shard_map/all_gather | solution.py:880
  322.1 25.7 %collective-permute-start.20 = (bf16[128,1152]{1,0:T(8,128)(2,1)S(1)}, bf16[128,1152]{1,0:T(8,128)(2,1)S(1)}, u32[]{:S(2)}, u32[]{:S(2)}) collective-permute-start(bf16[128,1152]{1,0:T(8,128)(2,1)S(1)} %get-tuple-element.162), channel_id=1, source_target_pairs={{0,16},{8,24},{16,0},{24,8},{1,17},{9,25},{17,1},{25,9},{2,18},{10... | collective-permute-start | bytes 884744 | tf_op jit(solution)/shard_map/ppermute | solution.py:461
  324.1 23.7 %collective-permute-start.19 = (bf16[128,1152]{1,0:T(8,128)(2,1)S(1)}, bf16[128,1152]{1,0:T(8,128)(2,1)S(1)}, u32[]{:S(2)}, u32[]{:S(2)}) collective-permute-start(bf16[128,1152]{1,0:T(8,128)(2,1)S(1)} %get-tuple-element.160), channel_id=1, source_target_pairs={{0,24},{8,0},{16,8},{24,16},{1,25},{9,1},{17,9},{25,17},{2,26},{10... | collective-permute-start | bytes 884744 | tf_op jit(solution)/shard_map/ppermute | solution.py:461
  402.4 24.0 %collective-permute-start.28 = (bf16[128,2048]{1,0:T(8,128)(2,1)S(1)}, bf16[128,2048]{1,0:T(8,128)(2,1)S(1)}, u32[]{:S(2)}, u32[]{:S(2)}) collective-permute-start(bf16[128,2048]{1,0:T(8,128)(2,1)S(1)} %get-tuple-element.153), channel_id=1, source_target_pairs={{0,8},{8,16},{16,24},{24,0},{1,9},{9,17},{17,25},{25,1},{2,10},{10... | collective-permute-start | bytes 1572872 | tf_op jit(solution)/shard_map/ppermute | solution.py:461
  403.7 25.2 %collective-permute-start.29 = (bf16[128,2048]{1,0:T(8,128)(2,1)S(1)}, bf16[128,2048]{1,0:T(8,128)(2,1)S(1)}, u32[]{:S(2)}, u32[]{:S(2)}) collective-permute-start(bf16[128,2048]{1,0:T(8,128)(2,1)S(1)} %get-tuple-element.152), channel_id=1, source_target_pairs={{0,24},{8,0},{16,8},{24,16},{1,25},{9,1},{17,9},{25,17},{2,26},{10... | collective-permute-start | bytes 1572872 | tf_op jit(solution)/shard_map/ppermute | solution.py:461
  406.1 45.7 %collective-permute-start.30 = (bf16[128,2048]{1,0:T(8,128)(2,1)S(1)}, bf16[128,2048]{1,0:T(8,128)(2,1)S(1)}, u32[]{:S(2)}, u32[]{:S(2)}) collective-permute-start(bf16[128,2048]{1,0:T(8,128)(2,1)S(1)} %get-tuple-element.151), channel_id=1, source_target_pairs={{0,16},{8,24},{16,0},{24,8},{1,17},{9,25},{17,1},{25,9},{2,18},{10... | collective-permute-start | bytes 1572872 | tf_op jit(solution)/shard_map/ppermute | solution.py:461
  475.9 49.5 %collective-permute-start.31 = (bf16[4,128,2048]{2,1,0:T(8,128)(2,1)}, bf16[4,128,2048]{2,1,0:T(8,128)(2,1)}, u32[]{:S(2)}, u32[]{:S(2)}) collective-permute-start(bf16[4,128,2048]{2,1,0:T(8,128)(2,1)} %convolution_convert_fusion.5), channel_id=1, source_target_pairs={{0,1},{1,0},{2,3},{3,2},{4,5},{5,4},{6,7},{7,6},{8,9},{9,8},{10,11... | collective-permute-start | bytes 6291464 | tf_op jit(solution)/shard_map/ppermute | solution.py:461
  485.5 122.1 %all-reduce.5.cloned.1.call-start = ((), (), s32[]{:S(2)}) async-start(), calls=%async_computation.12 | async-start | bytes 5242880 | tf_op jit(solution)/shard_map/psum | solution.py:930
  487.1 28.6 %collective-permute-start.45 = (bf16[128,2048]{1,0:T(8,128)(2,1)}, bf16[128,2048]{1,0:T(8,128)(2,1)S(1)}, u32[]{:S(2)}, u32[]{:S(2)}) collective-permute-start(bf16[128,2048]{1,0:T(8,128)(2,1)} %collective-permute-done.44), channel_id=1, source_target_pairs={{8,0},{9,1},{10,2},{11,3},{12,4},{13,5},{14,6},{15,7}} | collective-permute-start | bytes 1572872 | tf_op jit(solution)/shard_map/ppermute | solution.py:500
  498.0 32.3 %all-to-all-start.7 = ((bf16[8,136,896]{2,1,0:T(8,128)(2,1)}), bf16[8,136,896]{2,1,0:T(8,128)(2,1)}, u32[]{:S(2)}, u32[]{:S(2)}) async-start(bf16[8,136,896]{2,1,0:T(8,128)(2,1)} %bitcast.195), calls=%async_computation.7 | async-start | bytes 3899392 | tf_op jit(solution)/shard_map/all_to_all | solution.py:456
  533.9 28.3 %collective-permute-start.34 = (bf16[128,2048]{1,0:T(8,128)(2,1)S(1)}, bf16[128,2048]{1,0:T(8,128)(2,1)S(1)}, u32[]{:S(2)}, u32[]{:S(2)}) collective-permute-start(bf16[128,2048]{1,0:T(8,128)(2,1)S(1)} %get-tuple-element.149), channel_id=1, source_target_pairs={{0,6},{2,0},{4,2},{6,4},{1,7},{3,1},{5,3},{7,5},{8,14},{10,8},{12,... | collective-permute-start | bytes 1572872 | tf_op jit(solution)/shard_map/ppermute | solution.py:461
  538.1 24.0 %collective-permute-start.33 = (bf16[128,2048]{1,0:T(8,128)(2,1)S(1)}, bf16[128,2048]{1,0:T(8,128)(2,1)S(1)}, u32[]{:S(2)}, u32[]{:S(2)}) collective-permute-start(bf16[128,2048]{1,0:T(8,128)(2,1)S(1)} %get-tuple-element.150), channel_id=1, source_target_pairs={{0,4},{2,6},{4,0},{6,2},{1,5},{3,7},{5,1},{7,3},{8,12},{10,14},{12... | collective-permute-start | bytes 1572872 | tf_op jit(solution)/shard_map/ppermute | solution.py:461
  538.1 24.0 %collective-permute-start.32 = (bf16[128,2048]{1,0:T(8,128)(2,1)S(1)}, bf16[128,2048]{1,0:T(8,128)(2,1)S(1)}, u32[]{:S(2)}, u32[]{:S(2)}) collective-permute-start(bf16[128,2048]{1,0:T(8,128)(2,1)S(1)} %get-tuple-element.148), channel_id=1, source_target_pairs={{0,2},{2,4},{4,6},{6,0},{1,3},{3,5},{5,7},{7,1},{8,10},{10,12},{12... | collective-permute-start | bytes 1572872 | tf_op jit(solution)/shard_map/ppermute | solution.py:461
  (86 other events, 1429.9 us)
Sparse Core Ops, SparseCore 0:
  10.7 39.2 all-gather.2
  353.6 43.7 all-gather.4
  491.8 115.7 all-reduce.4

commit v5 on v4

--- a/solution.py
+++ b/solution.py
@@ -12,7 +12,7 @@
 highest = lax.Precision.HIGHEST
 chunk_count = 2
 grads_first = 7
-weighted_first = 9
+weighted_first = 12
 expert_steps = 2
 expert_vmem = 56 * 1024 * 1024
 kernel_vmem = 40 * 1024 * 1024
@@ -950,7 +950,8 @@
     col_sums, *out_returns[1:] = together(col_sums, *out_returns[1:])
     out_parts = [out_first] + [add_parts(to_source(part)) for part in out_returns[1:]]
     grad_normed = scatter_rows(col_sums)
-    grad_normed, sums, query_kv, *out_parts = together(grad_normed, sums, query_kv, *out_parts)
+    grad_input_norm = norm_one_back(grad_normed)[0]
+    grad_x = (grad_mixed + grad_input_norm).astype(jnp.bfloat16)
     out_rows = (mixed_rows + jnp.concatenate(out_parts, axis=1)).astype(jnp.bfloat16)
     grad_out_proj = in_plane_order(out_shares)
     places = (0, experts * model_width, model_width, model_width, head_dim, head_dim)
@@ -959,6 +960,7 @@
         sums[low:high] for low, high in zip(ends_at[:-1], ends_at[1:])
     ]
     grad_router = grad_router.reshape(experts, model_width).T
+    grad_x, out_rows, grad_router, query_kv = together(grad_x, out_rows, grad_router, query_kv)
     grad_query = query_kv[:model_width].astype(jnp.float32)
     kv_part = query_kv[model_width:]
     kv_parts = [kv_part] + [rotate(kv_part, "col", k) for k in range(1, cols)]
@@ -970,8 +972,6 @@
         kv_blocks += jnp.split(block.astype(jnp.float32), lane_parts, axis=1)
     grad_key = jnp.concatenate([block[:, :head_dim] for block in kv_blocks], axis=0)
     grad_value = jnp.concatenate([block[:, head_dim:] for block in kv_blocks], axis=0)
-    grad_input_norm = norm_one_back(grad_normed)[0]
-    grad_x = (grad_mixed + grad_input_norm).astype(jnp.bfloat16)
     return (
         out_rows,
         grad_x,

time: 641 us -> 638 us (level)
    psum x1, waiting for transfers between devices: 44.2 us -> 31.9 us  [local(): query_kv = lax.psum(query_kv, 'expert')]
    ppermute x40, waiting for transfers between devices: 139 us -> 149 us  [rotate(): lax.ppermute(block, axis, [(i, (i + step) % size) for i in range(size)])]
    all_to_all x2, waiting for transfers between devices: 6.28 us -> 15.4 us  [move_all(): lax.all_to_all(parts, ('expert',) + plane_axes, split_axis=0, concat_axis...]
    all_gather x1, waiting for transfers between devices: 10.2 us -> 3 us  [local(): lax.all_gather(grad_attn_low, ('row', 'col'), axis=0, tiled=True)]
  transfers between devices with their start and end apart: 59 -> 59, of which waited for: 28 -> 31; matrix products, arithmetic and copies ran while one was open for 20% -> 21% of each run, Pallas kernels for 6% -> 6%
where the time goes in v5:
time: 638 us; the launch traced here: 629 us
  waiting for transfers between devices  259 us (41%)
  starting transfers between devices  138 us (22%)
  matrix products  75.5 us (12%)
  Pallas kernels  71.9 us (11%)
  other arithmetic  54.1 us (8%)
  local copies, waits for them, and re-layouts  15.2 us (2%)
  between operations  15.1 us (2%)
    ppermute x40, waiting for transfers between devices, rotate(): lax.ppermute(block, axis, [(i, (i + step) % size) for i in range(size)])  149 us
    ppermute x40, starting transfers between devices, rotate(): lax.ppermute(block, axis, [(i, (i + step) % size) for i in range(size)])  59.9 us
    all_to_all x8, starting transfers between devices, move_plane(): lax.all_to_all(parts, plane_axes, split_axis=0, concat_axis=0, tiled=True)  56.3 us
    all_to_all x8, waiting for transfers between devices, move_plane(): lax.all_to_all(parts, plane_axes, split_axis=0, concat_axis=0, tiled=True)  45.9 us
    dot_general x6, matrix products, transposed_times(): lax.dot_general(left, right, (((0,), (0,)), ((), ())), preferred_element_...  37.7 us
    pallas_call x1, Pallas kernels, expert_rows(): pl.pallas_call(functools.partial(expert_kernel, count=count, grads_widths...  34.3 us
    psum x1, waiting for transfers between devices, local(): query_kv = lax.psum(query_kv, 'expert')  31.9 us
    pallas_call x1, Pallas kernels, attend_rows_back(): pl.pallas_call(functools.partial(attend_back_kernel, head_dim=head_dim),...  20 us
  transfers between devices with their start and end apart: 59, of which 31 were waited for; matrix products, arithmetic and copies ran while one was open for 21% of the time, Pallas kernels for 6%

profile of v5, /device:TPU:1, one launch (start us, length us, event | category | flops | bytes accessed | tf_op | source)
XLA Modules:
  0.0 628.8 jit_solution(15671394020644954816)
XLA Ops:
  29.3 9.3 %collective-permute-done.4 = bf16[128,896]{1,0:T(8,128)(2,1)S(1)} collective-permute-done((bf16[128,896]{1,0:T(8,128)(2,1)S(1)}, bf16[128,896]{1,0:T(8,128)(2,1)S(1)}, u32[]{:S(2)}, u32[]{:S(2)}) %collective-permute-start.4) | collective-permute-done | bytes 229408 | tf_op jit(solution)/shard_map/ppermute | solution.py:461
  49.9 17.6 %attend_rows.1 = (bf16[512,2048]{1,0:T(8,128)(2,1)}, bf16[512,2048]{1,0:T(8,128)(2,1)}, bf16[1024,512]{1,0:T(8,128)(2,1)}, bf16[1024,128]{1,0:T(8,128)(2,1)}, bf...) custom-call(s32[4]{0:T(128)S(1)} %bitcast.183, ...), custom_call_target="tpu_custom_call" | custom-call | flops 6979321856 | bytes 12582912 | tf_op jit(solution)/shard_map/attend_rows/pallas_call | solution.py:184
  85.7 18.3 %collective-permute-done.11 = bf16[128,1152]{1,0:T(8,128)(2,1)S(1)} collective-permute-done((bf16[128,1152]{1,0:T(8,128)(2,1)S(1)}, bf16[128,1152]{1,0:T(8,128)(2,1)S(1)}, u32[]{:S(2)}, u32[]{:S(2)}) %collective-permute-start.11) | collective-permute-done | bytes 294944 | tf_op jit(solution)/shard_map/ppermute | solution.py:461
  123.3 16.8 %collective-permute-done.17 = bf16[128,1024]{1,0:T(8,128)(2,1)S(1)} collective-permute-done((bf16[128,1024]{1,0:T(8,128)(2,1)S(1)}, bf16[128,1024]{1,0:T(8,128)(2,1)S(1)}, u32[]{:S(2)}, u32[]{:S(2)}) %collective-permute-start.17) | collective-permute-done | bytes 262176 | tf_op jit(solution)/shard_map/ppermute | solution.py:461
  142.9 7.0 %all-to-all-start.3 = ((bf16[8,136,1024]{2,1,0:T(8,128)(2,1)}), bf16[8,136,1024]{2,1,0:T(8,128)(2,1)}, u32[]{:S(2)}, u32[]{:S(2)}) async-start(bf16[8,136,1024]{2,1,0:T(8,128)(2,1)} %bitcast.194), calls=%async_computation.3 | async-start | bytes 4456448 | tf_op jit(solution)/shard_map/all_to_all | solution.py:456
  157.7 16.9 %collective-permute-done.14 = bf16[128,1024]{1,0:T(8,128)(2,1)S(1)} collective-permute-done((bf16[128,1024]{1,0:T(8,128)(2,1)S(1)}, bf16[128,1024]{1,0:T(8,128)(2,1)S(1)}, u32[]{:S(2)}, u32[]{:S(2)}) %collective-permute-start.14) | collective-permute-done | bytes 262176 | tf_op jit(solution)/shard_map/ppermute | solution.py:461
  184.9 22.7 %all-to-all-done.2 = bf16[8,136,1024]{2,1,0:T(8,128)(2,1)} async-done(((bf16[8,136,1024]{2,1,0:T(8,128)(2,1)}), bf16[8,136,1024]{2,1,0:T(8,128)(2,1)}, u32[]{:S(2)}, u32[]{:S(2)}) %all-to-all-start.2) | async-done | bytes 2228256 | tf_op jit(solution)/shard_map/all_to_all | solution.py:456
  207.6 34.3 %expert_rows.1 = (bf16[1088,1152]{1,0:T(8,128)(2,1)}, bf16[1088,1024]{1,0:T(8,128)(2,1)}, bf16[1088,1536]{1,0:T(8,128)(2,1)}, bf16[1088,512]{1,0:T(8,128)(2,1)},...) custom-call(s32[2]{0:T(128)} %pad_add_fusion.1.ids_ref, ...), custom_call_target="tpu_custom_call" | custom-call | flops 20535312384 | bytes 9437184 | tf_op jit(solution)/shard_map/expert_rows/pallas_call | solution.py:670
  241.9 8.1 %all-to-all-start.5 = ((bf16[8,136,1024]{2,1,0:T(8,128)(2,1)}), bf16[8,136,1024]{2,1,0:T(8,128)(2,1)}, u32[]{:S(2)}, u32[]{:S(2)}) async-start(bf16[8,136,1024]{2,1,0:T(8,128)(2,1)} %bitcast.195), calls=%async_computation.5 | async-start | bytes 4456448 | tf_op jit(solution)/shard_map/all_to_all | solution.py:456
  250.4 9.8 %fusion.60 = f32[2048,768]{1,0:T(8,128)} fusion(bf16[1088,2048]{1,0:T(8,128)(2,1)} %get-tuple-element.92, bf16[1088,768]{1,0:T(8,128)(2,1)} %get-tuple-element.93), kind=kOutput, calls=%fused_computation.174 | convolution fusion | flops 3422552064 | bytes 12419072 | tf_op jit(solution)/shard_map/dot_general | solution.py:447
  260.2 14.3 %all-to-all-done.5 = bf16[8,136,1024]{2,1,0:T(8,128)(2,1)} async-done(((bf16[8,136,1024]{2,1,0:T(8,128)(2,1)}), bf16[8,136,1024]{2,1,0:T(8,128)(2,1)}, u32[]{:S(2)}, u32[]{:S(2)}) %all-to-all-start.5) | async-done | bytes 2228256 | tf_op jit(solution)/shard_map/all_to_all | solution.py:456
  274.5 8.0 %all-to-all-start.4 = ((bf16[8,136,1152]{2,1,0:T(8,128)(2,1)}), bf16[8,136,1152]{2,1,0:T(8,128)(2,1)}, u32[]{:S(2)}, u32[]{:S(2)}) async-start(bf16[8,136,1152]{2,1,0:T(8,128)(2,1)} %bitcast.192), calls=%async_computation.4 | async-start | bytes 5013504 | tf_op jit(solution)/shard_map/all_to_all | solution.py:456
  282.5 10.0 %fusion.61 = f32[2048,768]{1,0:T(8,128)} fusion(bf16[1088,2048]{1,0:T(8,128)(2,1)} %get-tuple-element.92, bf16[1088,768]{1,0:T(8,128)(2,1)} %get-tuple-element.97), kind=kOutput, calls=%fused_computation.175 | convolution fusion | flops 3422552064 | bytes 12419072 | tf_op jit(solution)/shard_map/dot_general | solution.py:447
  310.1 8.0 %all-to-all-start.6 = ((bf16[8,136,1536]{2,1,0:T(8,128)(2,1)}), bf16[8,136,1536]{2,1,0:T(8,128)(2,1)}, u32[]{:S(2)}, u32[]{:S(2)}) async-start(bf16[8,136,1536]{2,1,0:T(8,128)(2,1)} %bitcast.191), calls=%async_computation.6 | async-start | bytes 6684672 | tf_op jit(solution)/shard_map/all_to_all | solution.py:456
  332.3 15.4 %collective-permute-done.20 = bf16[128,1152]{1,0:T(8,128)(2,1)S(1)} collective-permute-done((bf16[128,1152]{1,0:T(8,128)(2,1)S(1)}, bf16[128,1152]{1,0:T(8,128)(2,1)S(1)}, u32[]{:S(2)}, u32[]{:S(2)}) %collective-permute-start.20) | collective-permute-done | bytes 294944 | tf_op jit(solution)/shard_map/ppermute | solution.py:461
  367.3 8.4 %collective-permute-done.27 = bf16[128,1536]{1,0:T(8,128)(2,1)S(1)} collective-permute-done((bf16[128,1536]{1,0:T(8,128)(2,1)S(1)}, bf16[128,1536]{1,0:T(8,128)(2,1)S(1)}, u32[]{:S(2)}, u32[]{:S(2)}) %collective-permute-start.27) | collective-permute-done | bytes 393248 | tf_op jit(solution)/shard_map/ppermute | solution.py:461
  375.7 17.7 %collective-permute-done.26 = bf16[128,1536]{1,0:T(8,128)(2,1)S(1)} collective-permute-done((bf16[128,1536]{1,0:T(8,128)(2,1)S(1)}, bf16[128,1536]{1,0:T(8,128)(2,1)S(1)}, u32[]{:S(2)}, u32[]{:S(2)}) %collective-permute-start.26) | collective-permute-done | bytes 393248 | tf_op jit(solution)/shard_map/ppermute | solution.py:461
  410.0 20.0 %attend_rows_back.1 = (bf16[1024,512]{1,0:T(8,128)(2,1)}, bf16[1024,256]{1,0:T(8,128)(2,1)}, f32[1,128]{1,0:T(1,128)}, f32[1,128]{1,0:T(1,128)}) custom-call(s32[4]{0:T(128)S(1)} %bitcast.184, bf16[1024,2048]{1,0:T(8,128)(2,1)} %all-gather.5.cloned.1.call-done.grad_ref, bf16[512,2048]{1,0:T(8,128)(2,1)} %out_w_ref.3, ...), custom_call_target="tpu_custom_call" | custom-call | flops 5368709120 | bytes 6291456 | tf_op jit(solution)/shard_map/attend_rows_back/pallas_call | solution.py:387
  439.8 13.4 %collective-permute-done.30 = bf16[128,2048]{1,0:T(8,128)(2,1)S(1)} collective-permute-done((bf16[128,2048]{1,0:T(8,128)(2,1)S(1)}, bf16[128,2048]{1,0:T(8,128)(2,1)S(1)}, u32[]{:S(2)}, u32[]{:S(2)}) %collective-permute-start.30) | collective-permute-done | bytes 524320 | tf_op jit(solution)/shard_map/ppermute | solution.py:461
  460.5 7.4 %all-to-all-start.8 = ((f32[32,18,128]{2,1,0:T(8,128)}), f32[32,18,128]{2,1,0:T(8,128)}, u32[]{:S(2)}, u32[]{:S(2)}) async-start(f32[32,18,128]{2,1,0:T(8,128)} %reshape.398), calls=%async_computation.8 | async-start | bytes 786432 | tf_op jit(solution)/shard_map/all_to_all | solution.py:482
  495.0 11.3 %all-to-all-done.9 = f32[32,18,128]{2,1,0:T(8,128)S(1)} async-done(((f32[32,18,128]{2,1,0:T(8,128)}), f32[32,18,128]{2,1,0:T(8,128)S(1)}, u32[]{:S(2)}, u32[]{:S(2)}) %all-to-all-start.9) | async-done | bytes 294944 | tf_op jit(solution)/shard_map/all_to_all | solution.py:482
  519.8 12.1 %collective-permute-done.45 = bf16[128,2048]{1,0:T(8,128)(2,1)} collective-permute-done((bf16[128,2048]{1,0:T(8,128)(2,1)}, bf16[128,2048]{1,0:T(8,128)(2,1)}, u32[]{:S(2)}, u32[]{:S(2)}) %collective-permute-start.45) | collective-permute-done | bytes 524320 | tf_op jit(solution)/shard_map/ppermute | solution.py:500
  550.0 7.9 %collective-permute-start.36 = (bf16[128,512]{1,0:T(8,128)(2,1)S(1)}, bf16[128,512]{1,0:T(8,128)(2,1)S(1)}, u32[]{:S(2)}, u32[]{:S(2)}) collective-permute-start(bf16[128,512]{1,0:T(8,128)(2,1)S(1)} %get-tuple-element.178), channel_id=1, source_target_pairs={{0,16},{8,24},{16,0},{24,8},{1,17},{9,25},{17,1},{25,9},{2,18},{10... | collective-permute-start | bytes 393224 | tf_op jit(solution)/shard_map/ppermute | solution.py:461
  581.0 31.9 %all-reduce.5.cloned.1.call-done = bf16[2560,512]{1,0:T(8,128)(2,1)} async-done(((bf16[2560,512]{1,0:T(8,128)(2,1)}), bf16[2560,512]{1,0:T(8,128)(2,1)}) %all-reduce.5.cloned.1.call-update) | async-done | bytes 2621456 | tf_op jit(solution)/shard_map/psum | solution.py:930
  (330 shorter events, 267.1 us)
Async XLA Ops:
  7.2 42.7 %all-gather.3.cloned.1.call-start = ((), (), s32[]{:S(2)}) async-start(), calls=%async_computation.10 | async-start | bytes 4718592 | tf_op jit(solution)/shard_map/all_gather | solution.py:782
  41.4 31.3 %all-to-all-start = ((bf16[8,136,1024]{2,1,0:T(8,128)(2,1)}), bf16[8,136,1024]{2,1,0:T(8,128)(2,1)}, u32[]{:S(2)}, u32[]{:S(2)}) async-start(bf16[8,136,1024]{2,1,0:T(8,128)(2,1)} %bitcast.197), calls=%async_computation | async-start | bytes 4456448 | tf_op jit(solution)/shard_map/all_to_all | solution.py:456
  76.9 27.2 %collective-permute-start.11 = (bf16[128,1152]{1,0:T(8,128)(2,1)S(1)}, bf16[128,1152]{1,0:T(8,128)(2,1)S(1)}, u32[]{:S(2)}, u32[]{:S(2)}) collective-permute-start(bf16[128,1152]{1,0:T(8,128)(2,1)S(1)} %get-tuple-element.184), channel_id=1, source_target_pairs={{0,16},{8,24},{16,0},{24,8},{1,17},{9,25},{17,1},{25,9},{2,18},{10... | collective-permute-start | bytes 884744 | tf_op jit(solution)/shard_map/ppermute | solution.py:461
  77.8 26.3 %collective-permute-start.10 = (bf16[128,1152]{1,0:T(8,128)(2,1)S(1)}, bf16[128,1152]{1,0:T(8,128)(2,1)S(1)}, u32[]{:S(2)}, u32[]{:S(2)}) collective-permute-start(bf16[128,1152]{1,0:T(8,128)(2,1)S(1)} %get-tuple-element.184), channel_id=1, source_target_pairs={{0,8},{8,16},{16,24},{24,0},{1,9},{9,17},{17,25},{25,1},{2,10},{10... | collective-permute-start | bytes 884744 | tf_op jit(solution)/shard_map/ppermute | solution.py:461
  83.7 23.6 %collective-permute-start.9 = (bf16[128,2048]{1,0:T(8,128)(2,1)S(1)}, bf16[128,2048]{1,0:T(8,128)(2,1)S(1)}, u32[]{:S(2)}, u32[]{:S(2)}) collective-permute-start(bf16[128,2048]{1,0:T(8,128)(2,1)S(1)} %get-tuple-element.153), channel_id=1, source_target_pairs={{0,6},{2,0},{4,2},{6,4},{1,7},{3,1},{5,3},{7,5},{8,14},{10,8},{12,... | collective-permute-start | bytes 1572872 | tf_op jit(solution)/shard_map/ppermute | solution.py:461
  108.4 34.5 %all-to-all-start.1 = ((bf16[8,136,1152]{2,1,0:T(8,128)(2,1)}), bf16[8,136,1152]{2,1,0:T(8,128)(2,1)}, u32[]{:S(2)}, u32[]{:S(2)}) async-start(bf16[8,136,1152]{2,1,0:T(8,128)(2,1)} %bitcast.193), calls=%async_computation.1 | async-start | bytes 5013504 | tf_op jit(solution)/shard_map/all_to_all | solution.py:456
  116.5 23.6 %collective-permute-start.17 = (bf16[128,1024]{1,0:T(8,128)(2,1)S(1)}, bf16[128,1024]{1,0:T(8,128)(2,1)S(1)}, u32[]{:S(2)}, u32[]{:S(2)}) collective-permute-start(bf16[128,1024]{1,0:T(8,128)(2,1)S(1)} %get-tuple-element.181), channel_id=1, source_target_pairs={{0,16},{8,24},{16,0},{24,8},{1,17},{9,25},{17,1},{25,9},{2,18},{10... | collective-permute-start | bytes 786440 | tf_op jit(solution)/shard_map/ppermute | solution.py:461
  142.9 34.5 %all-to-all-start.3 = ((bf16[8,136,1024]{2,1,0:T(8,128)(2,1)}), bf16[8,136,1024]{2,1,0:T(8,128)(2,1)}, u32[]{:S(2)}, u32[]{:S(2)}) async-start(bf16[8,136,1024]{2,1,0:T(8,128)(2,1)} %bitcast.194), calls=%async_computation.3 | async-start | bytes 4456448 | tf_op jit(solution)/shard_map/all_to_all | solution.py:456
  151.0 23.7 %collective-permute-start.14 = (bf16[128,1024]{1,0:T(8,128)(2,1)S(1)}, bf16[128,1024]{1,0:T(8,128)(2,1)S(1)}, u32[]{:S(2)}, u32[]{:S(2)}) collective-permute-start(bf16[128,1024]{1,0:T(8,128)(2,1)S(1)} %get-tuple-element.182), channel_id=1, source_target_pairs={{0,16},{8,24},{16,0},{24,8},{1,17},{9,25},{17,1},{25,9},{2,18},{10... | collective-permute-start | bytes 786440 | tf_op jit(solution)/shard_map/ppermute | solution.py:461
  177.5 30.1 %all-to-all-start.2 = ((bf16[8,136,1024]{2,1,0:T(8,128)(2,1)}), bf16[8,136,1024]{2,1,0:T(8,128)(2,1)}, u32[]{:S(2)}, u32[]{:S(2)}) async-start(bf16[8,136,1024]{2,1,0:T(8,128)(2,1)} %bitcast.196), calls=%async_computation.2 | async-start | bytes 4456448 | tf_op jit(solution)/shard_map/all_to_all | solution.py:456
  241.9 32.7 %all-to-all-start.5 = ((bf16[8,136,1024]{2,1,0:T(8,128)(2,1)}), bf16[8,136,1024]{2,1,0:T(8,128)(2,1)}, u32[]{:S(2)}, u32[]{:S(2)}) async-start(bf16[8,136,1024]{2,1,0:T(8,128)(2,1)} %bitcast.195), calls=%async_computation.5 | async-start | bytes 4456448 | tf_op jit(solution)/shard_map/all_to_all | solution.py:456
  274.5 35.6 %all-to-all-start.4 = ((bf16[8,136,1152]{2,1,0:T(8,128)(2,1)}), bf16[8,136,1152]{2,1,0:T(8,128)(2,1)}, u32[]{:S(2)}, u32[]{:S(2)}) async-start(bf16[8,136,1152]{2,1,0:T(8,128)(2,1)} %bitcast.192), calls=%async_computation.4 | async-start | bytes 5013504 | tf_op jit(solution)/shard_map/all_to_all | solution.py:456
  303.1 23.6 %collective-permute-start.23 = (bf16[128,1024]{1,0:T(8,128)(2,1)}, bf16[128,1024]{1,0:T(8,128)(2,1)}, u32[]{:S(2)}, u32[]{:S(2)}) collective-permute-start(bf16[128,1024]{1,0:T(8,128)(2,1)} %get-tuple-element.173), channel_id=1, source_target_pairs={{0,16},{8,24},{16,0},{24,8},{1,17},{9,25},{17,1},{25,9},{2,18},{10... | collective-permute-start | bytes 786440 | tf_op jit(solution)/shard_map/ppermute | solution.py:461
  310.1 44.5 %all-to-all-start.6 = ((bf16[8,136,1536]{2,1,0:T(8,128)(2,1)}), bf16[8,136,1536]{2,1,0:T(8,128)(2,1)}, u32[]{:S(2)}, u32[]{:S(2)}) async-start(bf16[8,136,1536]{2,1,0:T(8,128)(2,1)} %bitcast.191), calls=%async_computation.6 | async-start | bytes 6684672 | tf_op jit(solution)/shard_map/all_to_all | solution.py:456
  318.1 79.4 %all-gather.5.cloned.1.call-start = ((), (), s32[]{:S(2)}) async-start(), calls=%async_computation.11 | async-start | bytes 4718592 | tf_op jit(solution)/shard_map/all_gather | solution.py:880
  322.3 25.5 %collective-permute-start.20 = (bf16[128,1152]{1,0:T(8,128)(2,1)S(1)}, bf16[128,1152]{1,0:T(8,128)(2,1)S(1)}, u32[]{:S(2)}, u32[]{:S(2)}) collective-permute-start(bf16[128,1152]{1,0:T(8,128)(2,1)S(1)} %get-tuple-element.160), channel_id=1, source_target_pairs={{0,16},{8,24},{16,0},{24,8},{1,17},{9,25},{17,1},{25,9},{2,18},{10... | collective-permute-start | bytes 884744 | tf_op jit(solution)/shard_map/ppermute | solution.py:461
  365.1 28.3 %collective-permute-start.26 = (bf16[128,1536]{1,0:T(8,128)(2,1)S(1)}, bf16[128,1536]{1,0:T(8,128)(2,1)S(1)}, u32[]{:S(2)}, u32[]{:S(2)}) collective-permute-start(bf16[128,1536]{1,0:T(8,128)(2,1)S(1)} %get-tuple-element.157), channel_id=1, source_target_pairs={{0,16},{8,24},{16,0},{24,8},{1,17},{9,25},{17,1},{25,9},{2,18},{10... | collective-permute-start | bytes 1179656 | tf_op jit(solution)/shard_map/ppermute | solution.py:461
  367.2 26.2 %collective-permute-start.25 = (bf16[128,1536]{1,0:T(8,128)(2,1)S(1)}, bf16[128,1536]{1,0:T(8,128)(2,1)S(1)}, u32[]{:S(2)}, u32[]{:S(2)}) collective-permute-start(bf16[128,1536]{1,0:T(8,128)(2,1)S(1)} %get-tuple-element.155), channel_id=1, source_target_pairs={{0,24},{8,0},{16,8},{24,16},{1,25},{9,1},{17,9},{25,17},{2,26},{10... | collective-permute-start | bytes 1179656 | tf_op jit(solution)/shard_map/ppermute | solution.py:461
  402.6 27.4 %collective-permute-start.28 = (bf16[128,2048]{1,0:T(8,128)(2,1)S(1)}, bf16[128,2048]{1,0:T(8,128)(2,1)S(1)}, u32[]{:S(2)}, u32[]{:S(2)}) collective-permute-start(bf16[128,2048]{1,0:T(8,128)(2,1)S(1)} %get-tuple-element.151), channel_id=1, source_target_pairs={{0,8},{8,16},{16,24},{24,0},{1,9},{9,17},{17,25},{25,1},{2,10},{10... | collective-permute-start | bytes 1572872 | tf_op jit(solution)/shard_map/ppermute | solution.py:461
  408.7 44.5 %collective-permute-start.30 = (bf16[128,2048]{1,0:T(8,128)(2,1)S(1)}, bf16[128,2048]{1,0:T(8,128)(2,1)S(1)}, u32[]{:S(2)}, u32[]{:S(2)}) collective-permute-start(bf16[128,2048]{1,0:T(8,128)(2,1)S(1)} %get-tuple-element.149), channel_id=1, source_target_pairs={{0,16},{8,24},{16,0},{24,8},{1,17},{9,25},{17,1},{25,9},{2,18},{10... | collective-permute-start | bytes 1572872 | tf_op jit(solution)/shard_map/ppermute | solution.py:461
  473.3 69.3 %collective-permute-start.31 = (bf16[4,128,2048]{2,1,0:T(8,128)(2,1)}, bf16[4,128,2048]{2,1,0:T(8,128)(2,1)}, u32[]{:S(2)}, u32[]{:S(2)}) collective-permute-start(bf16[4,128,2048]{2,1,0:T(8,128)(2,1)} %convolution_convert_fusion.5), channel_id=1, source_target_pairs={{0,1},{1,0},{2,3},{3,2},{4,5},{5,4},{6,7},{7,6},{8,9},{9,8},{10,11... | collective-permute-start | bytes 6291464 | tf_op jit(solution)/shard_map/ppermute | solution.py:461
  488.9 124.0 %all-reduce.5.cloned.1.call-start = ((), (), s32[]{:S(2)}) async-start(), calls=%async_computation.12 | async-start | bytes 5242880 | tf_op jit(solution)/shard_map/psum | solution.py:930
  493.7 38.2 %collective-permute-start.45 = (bf16[128,2048]{1,0:T(8,128)(2,1)}, bf16[128,2048]{1,0:T(8,128)(2,1)}, u32[]{:S(2)}, u32[]{:S(2)}) collective-permute-start(bf16[128,2048]{1,0:T(8,128)(2,1)} %collective-permute-done.44), channel_id=1, source_target_pairs={{8,0},{9,1},{10,2},{11,3},{12,4},{13,5},{14,6},{15,7}} | collective-permute-start | bytes 1572872 | tf_op jit(solution)/shard_map/ppermute | solution.py:500
  506.3 41.3 %all-to-all-start.7 = ((bf16[8,136,512]{2,1,0:T(8,128)(2,1)}), bf16[8,136,512]{2,1,0:T(8,128)(2,1)}, u32[]{:S(2)}, u32[]{:S(2)}) async-start(bf16[8,136,512]{2,1,0:T(8,128)(2,1)} %bitcast.203), calls=%async_computation.7 | async-start | bytes 2228224 | tf_op jit(solution)/shard_map/all_to_all | solution.py:456
  (87 other events, 1414.1 us)
Sparse Core Ops, SparseCore 0:
  10.7 39.2 all-gather.2
  354.7 42.7 all-gather.4
  492.6 120.1 all-reduce.4

commit v6 on v5

--- a/solution.py
+++ b/solution.py
@@ -12,7 +12,7 @@
 highest = lax.Precision.HIGHEST
 chunk_count = 2
 grads_first = 7
-weighted_first = 12
+weighted_first = 13
 expert_steps = 2
 expert_vmem = 56 * 1024 * 1024
 kernel_vmem = 40 * 1024 * 1024

time: 638 us -> 639 us (level)
  transfers between devices with their start and end apart: 59 -> 59, of which waited for: 31 -> 29; matrix products, arithmetic and copies ran while one was open for 21% -> 21% of each run, Pallas kernels for 6% -> 6%
where the time goes in v6:
time: 639 us; the launch traced here: 630 us
  waiting for transfers between devices  256 us (40%)
  starting transfers between devices  142 us (22%)
  matrix products  75.7 us (12%)
  Pallas kernels  71.9 us (11%)
  other arithmetic  54.1 us (8%)
  local copies, waits for them, and re-layouts  15.2 us (2%)
  between operations  15.1 us (2%)
    ppermute x40, waiting for transfers between devices, rotate(): lax.ppermute(block, axis, [(i, (i + step) % size) for i in range(size)])  148 us
    ppermute x40, starting transfers between devices, rotate(): lax.ppermute(block, axis, [(i, (i + step) % size) for i in range(size)])  59.9 us
    all_to_all x8, starting transfers between devices, move_plane(): lax.all_to_all(parts, plane_axes, split_axis=0, concat_axis=0, tiled=True)  56.3 us
    all_to_all x8, waiting for transfers between devices, move_plane(): lax.all_to_all(parts, plane_axes, split_axis=0, concat_axis=0, tiled=True)  48.9 us
    dot_general x6, matrix products, transposed_times(): lax.dot_general(left, right, (((0,), (0,)), ((), ())), preferred_element_...  37.7 us
    pallas_call x1, Pallas kernels, expert_rows(): pl.pallas_call(functools.partial(expert_kernel, count=count, grads_widths...  34.3 us
    psum x1, waiting for transfers between devices, local(): query_kv = lax.psum(query_kv, 'expert')  29.7 us
    pallas_call x1, Pallas kernels, attend_rows_back(): pl.pallas_call(functools.partial(attend_back_kernel, head_dim=head_dim),...  19.9 us
  transfers between devices with their start and end apart: 59, of which 29 were waited for; matrix products, arithmetic and copies ran while one was open for 21% of the time, Pallas kernels for 6%

profile of v6, /device:TPU:1, one launch (start us, length us, event | category | flops | bytes accessed | tf_op | source)
XLA Modules:
  0.0 629.9 jit_solution(3805005605964138928)
XLA Ops:
  29.3 9.3 %collective-permute-done.4 = bf16[128,896]{1,0:T(8,128)(2,1)S(1)} collective-permute-done((bf16[128,896]{1,0:T(8,128)(2,1)S(1)}, bf16[128,896]{1,0:T(8,128)(2,1)S(1)}, u32[]{:S(2)}, u32[]{:S(2)}) %collective-permute-start.4) | collective-permute-done | bytes 229408 | tf_op jit(solution)/shard_map/ppermute | solution.py:461
  49.9 17.6 %attend_rows.1 = (bf16[512,2048]{1,0:T(8,128)(2,1)}, bf16[512,2048]{1,0:T(8,128)(2,1)}, bf16[1024,512]{1,0:T(8,128)(2,1)}, bf16[1024,128]{1,0:T(8,128)(2,1)}, bf...) custom-call(s32[4]{0:T(128)S(1)} %bitcast.183, ...), custom_call_target="tpu_custom_call" | custom-call | flops 6979321856 | bytes 12582912 | tf_op jit(solution)/shard_map/attend_rows/pallas_call | solution.py:184
  85.7 18.3 %collective-permute-done.11 = bf16[128,1152]{1,0:T(8,128)(2,1)S(1)} collective-permute-done((bf16[128,1152]{1,0:T(8,128)(2,1)S(1)}, bf16[128,1152]{1,0:T(8,128)(2,1)S(1)}, u32[]{:S(2)}, u32[]{:S(2)}) %collective-permute-start.11) | collective-permute-done | bytes 294944 | tf_op jit(solution)/shard_map/ppermute | solution.py:461
  123.3 16.8 %collective-permute-done.17 = bf16[128,1024]{1,0:T(8,128)(2,1)S(1)} collective-permute-done((bf16[128,1024]{1,0:T(8,128)(2,1)S(1)}, bf16[128,1024]{1,0:T(8,128)(2,1)S(1)}, u32[]{:S(2)}, u32[]{:S(2)}) %collective-permute-start.17) | collective-permute-done | bytes 262176 | tf_op jit(solution)/shard_map/ppermute | solution.py:461
  157.7 16.9 %collective-permute-done.14 = bf16[128,1024]{1,0:T(8,128)(2,1)S(1)} collective-permute-done((bf16[128,1024]{1,0:T(8,128)(2,1)S(1)}, bf16[128,1024]{1,0:T(8,128)(2,1)S(1)}, u32[]{:S(2)}, u32[]{:S(2)}) %collective-permute-start.14) | collective-permute-done | bytes 262176 | tf_op jit(solution)/shard_map/ppermute | solution.py:461
  184.9 22.7 %all-to-all-done.2 = bf16[8,136,1024]{2,1,0:T(8,128)(2,1)} async-done(((bf16[8,136,1024]{2,1,0:T(8,128)(2,1)}), bf16[8,136,1024]{2,1,0:T(8,128)(2,1)}, u32[]{:S(2)}, u32[]{:S(2)}) %all-to-all-start.2) | async-done | bytes 2228256 | tf_op jit(solution)/shard_map/all_to_all | solution.py:456
  207.6 34.3 %expert_rows.1 = (bf16[1088,1152]{1,0:T(8,128)(2,1)}, bf16[1088,1024]{1,0:T(8,128)(2,1)}, bf16[1088,1664]{1,0:T(8,128)(2,1)}, bf16[1088,384]{1,0:T(8,128)(2,1)},...) custom-call(s32[2]{0:T(128)} %pad_add_fusion.1.ids_ref, ...), custom_call_target="tpu_custom_call" | custom-call | flops 20535312384 | bytes 9437184 | tf_op jit(solution)/shard_map/expert_rows/pallas_call | solution.py:670
  241.9 8.1 %all-to-all-start.5 = ((bf16[8,136,1024]{2,1,0:T(8,128)(2,1)}), bf16[8,136,1024]{2,1,0:T(8,128)(2,1)}, u32[]{:S(2)}, u32[]{:S(2)}) async-start(bf16[8,136,1024]{2,1,0:T(8,128)(2,1)} %bitcast.195), calls=%async_computation.5 | async-start | bytes 4456448 | tf_op jit(solution)/shard_map/all_to_all | solution.py:456
  250.4 9.8 %fusion.60 = f32[2048,768]{1,0:T(8,128)} fusion(bf16[1088,2048]{1,0:T(8,128)(2,1)} %get-tuple-element.92, bf16[1088,768]{1,0:T(8,128)(2,1)} %get-tuple-element.93), kind=kOutput, calls=%fused_computation.174 | convolution fusion | flops 3422552064 | bytes 12419072 | tf_op jit(solution)/shard_map/dot_general | solution.py:447
  260.3 14.3 %all-to-all-done.5 = bf16[8,136,1024]{2,1,0:T(8,128)(2,1)} async-done(((bf16[8,136,1024]{2,1,0:T(8,128)(2,1)}), bf16[8,136,1024]{2,1,0:T(8,128)(2,1)}, u32[]{:S(2)}, u32[]{:S(2)}) %all-to-all-start.5) | async-done | bytes 2228256 | tf_op jit(solution)/shard_map/all_to_all | solution.py:456
  274.5 8.0 %all-to-all-start.4 = ((bf16[8,136,1152]{2,1,0:T(8,128)(2,1)}), bf16[8,136,1152]{2,1,0:T(8,128)(2,1)}, u32[]{:S(2)}, u32[]{:S(2)}) async-start(bf16[8,136,1152]{2,1,0:T(8,128)(2,1)} %bitcast.192), calls=%async_computation.4 | async-start | bytes 5013504 | tf_op jit(solution)/shard_map/all_to_all | solution.py:456
  282.6 10.0 %fusion.61 = f32[2048,768]{1,0:T(8,128)} fusion(bf16[1088,2048]{1,0:T(8,128)(2,1)} %get-tuple-element.92, bf16[1088,768]{1,0:T(8,128)(2,1)} %get-tuple-element.97), kind=kOutput, calls=%fused_computation.175 | convolution fusion | flops 3422552064 | bytes 12419072 | tf_op jit(solution)/shard_map/dot_general | solution.py:447
  310.1 8.0 %all-to-all-start.6 = ((bf16[8,136,1664]{2,1,0:T(8,128)(2,1)}), bf16[8,136,1664]{2,1,0:T(8,128)(2,1)}, u32[]{:S(2)}, u32[]{:S(2)}) async-start(bf16[8,136,1664]{2,1,0:T(8,128)(2,1)} %bitcast.191), calls=%async_computation.6 | async-start | bytes 7241728 | tf_op jit(solution)/shard_map/all_to_all | solution.py:456
  332.4 15.4 %collective-permute-done.20 = bf16[128,1152]{1,0:T(8,128)(2,1)S(1)} collective-permute-done((bf16[128,1152]{1,0:T(8,128)(2,1)S(1)}, bf16[128,1152]{1,0:T(8,128)(2,1)S(1)}, u32[]{:S(2)}, u32[]{:S(2)}) %collective-permute-start.20) | collective-permute-done | bytes 294944 | tf_op jit(solution)/shard_map/ppermute | solution.py:461
  367.7 7.0 %collective-permute-done.27 = bf16[128,1664]{1,0:T(8,128)(2,1)S(1)} collective-permute-done((bf16[128,1664]{1,0:T(8,128)(2,1)S(1)}, bf16[128,1664]{1,0:T(8,128)(2,1)S(1)}, u32[]{:S(2)}, u32[]{:S(2)}) %collective-permute-start.27) | collective-permute-done | bytes 426016 | tf_op jit(solution)/shard_map/ppermute | solution.py:461
  374.7 21.2 %collective-permute-done.26 = bf16[128,1664]{1,0:T(8,128)(2,1)S(1)} collective-permute-done((bf16[128,1664]{1,0:T(8,128)(2,1)S(1)}, bf16[128,1664]{1,0:T(8,128)(2,1)S(1)}, u32[]{:S(2)}, u32[]{:S(2)}) %collective-permute-start.26) | collective-permute-done | bytes 426016 | tf_op jit(solution)/shard_map/ppermute | solution.py:461
  402.6 9.0 %collective-permute-start.28 = (bf16[128,2048]{1,0:T(8,128)(2,1)S(1)}, bf16[128,2048]{1,0:T(8,128)(2,1)S(1)}, u32[]{:S(2)}, u32[]{:S(2)}) collective-permute-start(bf16[128,2048]{1,0:T(8,128)(2,1)S(1)} %get-tuple-element.151), channel_id=1, source_target_pairs={{0,8},{8,16},{16,24},{24,0},{1,9},{9,17},{17,25},{25,1},{2,10},{10... | collective-permute-start | bytes 1572872 | tf_op jit(solution)/shard_map/ppermute | solution.py:461
  413.3 19.9 %attend_rows_back.1 = (bf16[1024,512]{1,0:T(8,128)(2,1)}, bf16[1024,256]{1,0:T(8,128)(2,1)}, f32[1,128]{1,0:T(1,128)}, f32[1,128]{1,0:T(1,128)}) custom-call(s32[4]{0:T(128)S(1)} %bitcast.184, bf16[1024,2048]{1,0:T(8,128)(2,1)} %all-gather.5.cloned.1.call-done.grad_ref, bf16[512,2048]{1,0:T(8,128)(2,1)} %out_w_ref.3, ...), custom_call_target="tpu_custom_call" | custom-call | flops 5368709120 | bytes 6291456 | tf_op jit(solution)/shard_map/attend_rows_back/pallas_call | solution.py:387
  442.8 10.8 %collective-permute-done.30 = bf16[128,2048]{1,0:T(8,128)(2,1)S(1)} collective-permute-done((bf16[128,2048]{1,0:T(8,128)(2,1)S(1)}, bf16[128,2048]{1,0:T(8,128)(2,1)S(1)}, u32[]{:S(2)}, u32[]{:S(2)}) %collective-permute-start.30) | collective-permute-done | bytes 524320 | tf_op jit(solution)/shard_map/ppermute | solution.py:461
  463.7 7.6 %all-to-all-start.8 = ((f32[32,18,128]{2,1,0:T(8,128)}), f32[32,18,128]{2,1,0:T(8,128)}, u32[]{:S(2)}, u32[]{:S(2)}) async-start(f32[32,18,128]{2,1,0:T(8,128)} %reshape.398), calls=%async_computation.8 | async-start | bytes 786432 | tf_op jit(solution)/shard_map/all_to_all | solution.py:482
  498.4 11.3 %all-to-all-done.9 = f32[32,18,128]{2,1,0:T(8,128)S(1)} async-done(((f32[32,18,128]{2,1,0:T(8,128)}), f32[32,18,128]{2,1,0:T(8,128)S(1)}, u32[]{:S(2)}, u32[]{:S(2)}) %all-to-all-start.9) | async-done | bytes 294944 | tf_op jit(solution)/shard_map/all_to_all | solution.py:482
  523.3 12.0 %collective-permute-done.45 = bf16[128,2048]{1,0:T(8,128)(2,1)} collective-permute-done((bf16[128,2048]{1,0:T(8,128)(2,1)}, bf16[128,2048]{1,0:T(8,128)(2,1)}, u32[]{:S(2)}, u32[]{:S(2)}) %collective-permute-start.45) | collective-permute-done | bytes 524320 | tf_op jit(solution)/shard_map/ppermute | solution.py:500
  553.2 8.0 %collective-permute-start.36 = (bf16[128,384]{1,0:T(8,128)(2,1)S(1)}, bf16[128,384]{1,0:T(8,128)(2,1)S(1)}, u32[]{:S(2)}, u32[]{:S(2)}) collective-permute-start(bf16[128,384]{1,0:T(8,128)(2,1)S(1)} %get-tuple-element.186), channel_id=1, source_target_pairs={{0,16},{8,24},{16,0},{24,8},{1,17},{9,25},{17,1},{25,9},{2,18},{10... | collective-permute-start | bytes 294920 | tf_op jit(solution)/shard_map/ppermute | solution.py:461
  584.2 29.7 %all-reduce.5.cloned.1.call-done = bf16[2560,512]{1,0:T(8,128)(2,1)} async-done(((bf16[2560,512]{1,0:T(8,128)(2,1)}), bf16[2560,512]{1,0:T(8,128)(2,1)}) %all-reduce.5.cloned.1.call-update) | async-done | bytes 2621456 | tf_op jit(solution)/shard_map/psum | solution.py:930
  (330 shorter events, 268.7 us)
Async XLA Ops:
  7.2 42.7 %all-gather.3.cloned.1.call-start = ((), (), s32[]{:S(2)}) async-start(), calls=%async_computation.10 | async-start | bytes 4718592 | tf_op jit(solution)/shard_map/all_gather | solution.py:782
  41.4 31.3 %all-to-all-start = ((bf16[8,136,1024]{2,1,0:T(8,128)(2,1)}), bf16[8,136,1024]{2,1,0:T(8,128)(2,1)}, u32[]{:S(2)}, u32[]{:S(2)}) async-start(bf16[8,136,1024]{2,1,0:T(8,128)(2,1)} %bitcast.197), calls=%async_computation | async-start | bytes 4456448 | tf_op jit(solution)/shard_map/all_to_all | solution.py:456
  76.9 27.2 %collective-permute-start.11 = (bf16[128,1152]{1,0:T(8,128)(2,1)S(1)}, bf16[128,1152]{1,0:T(8,128)(2,1)S(1)}, u32[]{:S(2)}, u32[]{:S(2)}) collective-permute-start(bf16[128,1152]{1,0:T(8,128)(2,1)S(1)} %get-tuple-element.181), channel_id=1, source_target_pairs={{0,16},{8,24},{16,0},{24,8},{1,17},{9,25},{17,1},{25,9},{2,18},{10... | collective-permute-start | bytes 884744 | tf_op jit(solution)/shard_map/ppermute | solution.py:461
  77.8 26.3 %collective-permute-start.10 = (bf16[128,1152]{1,0:T(8,128)(2,1)S(1)}, bf16[128,1152]{1,0:T(8,128)(2,1)S(1)}, u32[]{:S(2)}, u32[]{:S(2)}) collective-permute-start(bf16[128,1152]{1,0:T(8,128)(2,1)S(1)} %get-tuple-element.181), channel_id=1, source_target_pairs={{0,8},{8,16},{16,24},{24,0},{1,9},{9,17},{17,25},{25,1},{2,10},{10... | collective-permute-start | bytes 884744 | tf_op jit(solution)/shard_map/ppermute | solution.py:461
  83.7 23.6 %collective-permute-start.9 = (bf16[128,2048]{1,0:T(8,128)(2,1)S(1)}, bf16[128,2048]{1,0:T(8,128)(2,1)S(1)}, u32[]{:S(2)}, u32[]{:S(2)}) collective-permute-start(bf16[128,2048]{1,0:T(8,128)(2,1)S(1)} %get-tuple-element.153), channel_id=1, source_target_pairs={{0,6},{2,0},{4,2},{6,4},{1,7},{3,1},{5,3},{7,5},{8,14},{10,8},{12,... | collective-permute-start | bytes 1572872 | tf_op jit(solution)/shard_map/ppermute | solution.py:461
  108.4 34.5 %all-to-all-start.1 = ((bf16[8,136,1152]{2,1,0:T(8,128)(2,1)}), bf16[8,136,1152]{2,1,0:T(8,128)(2,1)}, u32[]{:S(2)}, u32[]{:S(2)}) async-start(bf16[8,136,1152]{2,1,0:T(8,128)(2,1)} %bitcast.193), calls=%async_computation.1 | async-start | bytes 5013504 | tf_op jit(solution)/shard_map/all_to_all | solution.py:456
  116.5 23.6 %collective-permute-start.17 = (bf16[128,1024]{1,0:T(8,128)(2,1)S(1)}, bf16[128,1024]{1,0:T(8,128)(2,1)S(1)}, u32[]{:S(2)}, u32[]{:S(2)}) collective-permute-start(bf16[128,1024]{1,0:T(8,128)(2,1)S(1)} %get-tuple-element.178), channel_id=1, source_target_pairs={{0,16},{8,24},{16,0},{24,8},{1,17},{9,25},{17,1},{25,9},{2,18},{10... | collective-permute-start | bytes 786440 | tf_op jit(solution)/shard_map/ppermute | solution.py:461
  142.9 34.5 %all-to-all-start.3 = ((bf16[8,136,1024]{2,1,0:T(8,128)(2,1)}), bf16[8,136,1024]{2,1,0:T(8,128)(2,1)}, u32[]{:S(2)}, u32[]{:S(2)}) async-start(bf16[8,136,1024]{2,1,0:T(8,128)(2,1)} %bitcast.194), calls=%async_computation.3 | async-start | bytes 4456448 | tf_op jit(solution)/shard_map/all_to_all | solution.py:456
  151.0 23.7 %collective-permute-start.14 = (bf16[128,1024]{1,0:T(8,128)(2,1)S(1)}, bf16[128,1024]{1,0:T(8,128)(2,1)S(1)}, u32[]{:S(2)}, u32[]{:S(2)}) collective-permute-start(bf16[128,1024]{1,0:T(8,128)(2,1)S(1)} %get-tuple-element.179), channel_id=1, source_target_pairs={{0,16},{8,24},{16,0},{24,8},{1,17},{9,25},{17,1},{25,9},{2,18},{10... | collective-permute-start | bytes 786440 | tf_op jit(solution)/shard_map/ppermute | solution.py:461
  177.5 30.1 %all-to-all-start.2 = ((bf16[8,136,1024]{2,1,0:T(8,128)(2,1)}), bf16[8,136,1024]{2,1,0:T(8,128)(2,1)}, u32[]{:S(2)}, u32[]{:S(2)}) async-start(bf16[8,136,1024]{2,1,0:T(8,128)(2,1)} %bitcast.196), calls=%async_computation.2 | async-start | bytes 4456448 | tf_op jit(solution)/shard_map/all_to_all | solution.py:456
  241.9 32.7 %all-to-all-start.5 = ((bf16[8,136,1024]{2,1,0:T(8,128)(2,1)}), bf16[8,136,1024]{2,1,0:T(8,128)(2,1)}, u32[]{:S(2)}, u32[]{:S(2)}) async-start(bf16[8,136,1024]{2,1,0:T(8,128)(2,1)} %bitcast.195), calls=%async_computation.5 | async-start | bytes 4456448 | tf_op jit(solution)/shard_map/all_to_all | solution.py:456
  274.5 35.6 %all-to-all-start.4 = ((bf16[8,136,1152]{2,1,0:T(8,128)(2,1)}), bf16[8,136,1152]{2,1,0:T(8,128)(2,1)}, u32[]{:S(2)}, u32[]{:S(2)}) async-start(bf16[8,136,1152]{2,1,0:T(8,128)(2,1)} %bitcast.192), calls=%async_computation.4 | async-start | bytes 5013504 | tf_op jit(solution)/shard_map/all_to_all | solution.py:456
  303.2 23.7 %collective-permute-start.23 = (bf16[128,1024]{1,0:T(8,128)(2,1)}, bf16[128,1024]{1,0:T(8,128)(2,1)}, u32[]{:S(2)}, u32[]{:S(2)}) collective-permute-start(bf16[128,1024]{1,0:T(8,128)(2,1)} %get-tuple-element.173), channel_id=1, source_target_pairs={{0,16},{8,24},{16,0},{24,8},{1,17},{9,25},{17,1},{25,9},{2,18},{10... | collective-permute-start | bytes 786440 | tf_op jit(solution)/shard_map/ppermute | solution.py:461
  310.1 47.5 %all-to-all-start.6 = ((bf16[8,136,1664]{2,1,0:T(8,128)(2,1)}), bf16[8,136,1664]{2,1,0:T(8,128)(2,1)}, u32[]{:S(2)}, u32[]{:S(2)}) async-start(bf16[8,136,1664]{2,1,0:T(8,128)(2,1)} %bitcast.191), calls=%async_computation.6 | async-start | bytes 7241728 | tf_op jit(solution)/shard_map/all_to_all | solution.py:456
  318.1 79.4 %all-gather.5.cloned.1.call-start = ((), (), s32[]{:S(2)}) async-start(), calls=%async_computation.11 | async-start | bytes 4718592 | tf_op jit(solution)/shard_map/all_gather | solution.py:880
  322.4 25.4 %collective-permute-start.20 = (bf16[128,1152]{1,0:T(8,128)(2,1)S(1)}, bf16[128,1152]{1,0:T(8,128)(2,1)S(1)}, u32[]{:S(2)}, u32[]{:S(2)}) collective-permute-start(bf16[128,1152]{1,0:T(8,128)(2,1)S(1)} %get-tuple-element.160), channel_id=1, source_target_pairs={{0,16},{8,24},{16,0},{24,8},{1,17},{9,25},{17,1},{25,9},{2,18},{10... | collective-permute-start | bytes 884744 | tf_op jit(solution)/shard_map/ppermute | solution.py:461
  365.5 30.4 %collective-permute-start.26 = (bf16[128,1664]{1,0:T(8,128)(2,1)S(1)}, bf16[128,1664]{1,0:T(8,128)(2,1)S(1)}, u32[]{:S(2)}, u32[]{:S(2)}) collective-permute-start(bf16[128,1664]{1,0:T(8,128)(2,1)S(1)} %get-tuple-element.157), channel_id=1, source_target_pairs={{0,16},{8,24},{16,0},{24,8},{1,17},{9,25},{17,1},{25,9},{2,18},{10... | collective-permute-start | bytes 1277960 | tf_op jit(solution)/shard_map/ppermute | solution.py:461
  367.6 28.3 %collective-permute-start.25 = (bf16[128,1664]{1,0:T(8,128)(2,1)S(1)}, bf16[128,1664]{1,0:T(8,128)(2,1)S(1)}, u32[]{:S(2)}, u32[]{:S(2)}) collective-permute-start(bf16[128,1664]{1,0:T(8,128)(2,1)S(1)} %get-tuple-element.155), channel_id=1, source_target_pairs={{0,24},{8,0},{16,8},{24,16},{1,25},{9,1},{17,9},{25,17},{2,26},{10... | collective-permute-start | bytes 1277960 | tf_op jit(solution)/shard_map/ppermute | solution.py:461
  402.6 30.6 %collective-permute-start.28 = (bf16[128,2048]{1,0:T(8,128)(2,1)S(1)}, bf16[128,2048]{1,0:T(8,128)(2,1)S(1)}, u32[]{:S(2)}, u32[]{:S(2)}) collective-permute-start(bf16[128,2048]{1,0:T(8,128)(2,1)S(1)} %get-tuple-element.151), channel_id=1, source_target_pairs={{0,8},{8,16},{16,24},{24,0},{1,9},{9,17},{17,25},{25,1},{2,10},{10... | collective-permute-start | bytes 1572872 | tf_op jit(solution)/shard_map/ppermute | solution.py:461
  412.0 41.5 %collective-permute-start.30 = (bf16[128,2048]{1,0:T(8,128)(2,1)S(1)}, bf16[128,2048]{1,0:T(8,128)(2,1)S(1)}, u32[]{:S(2)}, u32[]{:S(2)}) collective-permute-start(bf16[128,2048]{1,0:T(8,128)(2,1)S(1)} %get-tuple-element.149), channel_id=1, source_target_pairs={{0,16},{8,24},{16,0},{24,8},{1,17},{9,25},{17,1},{25,9},{2,18},{10... | collective-permute-start | bytes 1572872 | tf_op jit(solution)/shard_map/ppermute | solution.py:461
  476.8 69.2 %collective-permute-start.31 = (bf16[4,128,2048]{2,1,0:T(8,128)(2,1)}, bf16[4,128,2048]{2,1,0:T(8,128)(2,1)}, u32[]{:S(2)}, u32[]{:S(2)}) collective-permute-start(bf16[4,128,2048]{2,1,0:T(8,128)(2,1)} %convolution_convert_fusion.5), channel_id=1, source_target_pairs={{0,1},{1,0},{2,3},{3,2},{4,5},{5,4},{6,7},{7,6},{8,9},{9,8},{10,11... | collective-permute-start | bytes 6291464 | tf_op jit(solution)/shard_map/ppermute | solution.py:461
  492.3 121.6 %all-reduce.5.cloned.1.call-start = ((), (), s32[]{:S(2)}) async-start(), calls=%async_computation.12 | async-start | bytes 5242880 | tf_op jit(solution)/shard_map/psum | solution.py:930
  497.1 38.1 %collective-permute-start.45 = (bf16[128,2048]{1,0:T(8,128)(2,1)}, bf16[128,2048]{1,0:T(8,128)(2,1)}, u32[]{:S(2)}, u32[]{:S(2)}) collective-permute-start(bf16[128,2048]{1,0:T(8,128)(2,1)} %collective-permute-done.44), channel_id=1, source_target_pairs={{8,0},{9,1},{10,2},{11,3},{12,4},{13,5},{14,6},{15,7}} | collective-permute-start | bytes 1572872 | tf_op jit(solution)/shard_map/ppermute | solution.py:500
  509.8 41.1 %all-to-all-start.7 = ((bf16[8,136,384]{2,1,0:T(8,128)(2,1)}), bf16[8,136,384]{2,1,0:T(8,128)(2,1)}, u32[]{:S(2)}, u32[]{:S(2)}) async-start(bf16[8,136,384]{2,1,0:T(8,128)(2,1)} %bitcast.209), calls=%async_computation.7 | async-start | bytes 1671168 | tf_op jit(solution)/shard_map/all_to_all | solution.py:456
  (87 other events, 1416.9 us)
Sparse Core Ops, SparseCore 0:
  10.7 39.2 all-gather.2
  357.8 39.7 all-gather.4
  496.1 117.7 all-reduce.4
